TPU v7x, 256 devices: a whole 4x4x8 slice. The times are simulated.
256 devices in a mesh: dp: 8 (over z), seq: 32 (over x, y, core).
Axes of the slice: x: 4, y: 4, z: 8, core: 2. Of those that a mesh axis runs over, the one named last changes fastest.
Arguments:
- query: bfloat16 [32768, 1024], P(('dp', 'seq')), may hold values from -6 to 6
- key: bfloat16 [32768, 1024], P(('dp', 'seq')), may hold values from -6 to 6
- value: bfloat16 [32768, 1024], P(('dp', 'seq')), may hold values from -6 to 6
- gate_u: bfloat16 [32768, 1024], P(('dp', 'seq')), may hold values from -6 to 6
- out_weight: bfloat16 [1024, 1024], replicated, may hold values from -0.1875 to 0.1875
- cotangent: bfloat16 [32768, 1024], P(('dp', 'seq')), may hold values from -6 to 6
- hist_lengths: int32 [8, 4], P('dp'), may hold values from 1 to 2048, 4096 in all within a row
Outputs:
- d_query: bfloat16 [32768, 1024], P(('dp', 'seq'))
- d_key: bfloat16 [32768, 1024], P(('dp', 'seq'))
- d_value: bfloat16 [32768, 1024], P(('dp', 'seq'))
- d_gate: bfloat16 [32768, 1024], P(('dp', 'seq'))
- d_weight: float32 [1024, 1024], P(('dp', 'seq'))
Inputs may be any that keep to these rules, and one draw needn't show every extreme that they name: `hist_lengths`: row r lists the lengths of the histories packed in order into the 4096 tokens of group r; each row sums to 4096 and its longest history has exactly 2048 tokens.
All inputs are finite; a program needn't handle non-finite values.
Results may differ from a plain program's by a relative error of at most 0.018.
Values may be sent and summed in bfloat16 or wider, within the bound.
No kernel may reach another device: no remote copies, remote signals or barrier semaphores. Data moves between devices by JAX's collectives and lax.ppermute only.
A program may use at most 128 MiB of HBM per device.

v0:
```python
import math

import jax
import jax.numpy as jnp
from jax import lax
from jax.experimental import pallas as pl
from jax.experimental.pallas import tpu as pltpu
from jax.sharding import Mesh, PartitionSpec as P

HEADS = 16
HEAD_DIM = 64
WIDTH = HEADS * HEAD_DIM
N_BLOCKS = 16
BLOCK = 128
HALF = N_BLOCKS * BLOCK
SUB = 256
F_TILE = 2048
B_TILE = 1024
STATS = 5
CHIP = ("x", "y")
SWAP = ((0, 1), (1, 0))
BF16 = jnp.bfloat16
F32 = jnp.float32


def dot(a, b):
    return lax.dot_general(a, b, (((1,), (0,)), ((), ())), preferred_element_type=F32)


def dot_nt(a, b):
    return lax.dot_general(a, b, (((1,), (1,)), ((), ())), preferred_element_type=F32)


def sigmoid(s):
    return pltpu.reciprocal(1.0 + jnp.exp(-s), approx=True)


def lanes():
    return lax.broadcasted_iota(jnp.int32, (1, BLOCK), 1)


def place_of(place_ref):
    first, second, third = (place_ref[i] for i in range(3))
    core = place_ref[4]
    is_first, is_second = first == HALF, second == HALF
    begin = jnp.where(is_first, 0, jnp.where(is_second, first, first + second + jnp.where(third == HALF, 0, third)))
    end1 = jnp.where(is_first, second, first)
    end2 = end1 + jnp.where(is_first | is_second, third, second)
    turn = jnp.where(core == 0, begin & (HALF - 1), 0)
    return core, begin, turn, jnp.where(core == 0, HALF, end1), jnp.where(core == 0, HALF, end2)


def low_is_mine(j, core, begin):
    return ((2 * j + core) * BLOCK + lanes() >= begin) == (core == 0)


def live_of(q_at, k_at, end1, end2, diagonal):
    q_place = q_at + lax.broadcasted_iota(jnp.int32, (1, SUB), 1)
    k_place = k_at + lax.broadcasted_iota(jnp.int32, (SUB, 1), 0)
    start = jnp.where(q_place < end1, 0, jnp.where(q_place < end2, end1, end2))
    live = k_place >= start
    return live & (k_place <= q_place) if diagonal else live


def below(n_tiles, tile):
    n_sub = tile // SUB
    for i in range(n_tiles):
        for j in range(i + 1):
            subs = [(q, k) for q in range(n_sub) for k in range(n_sub) if j < i or k <= q]
            yield i * tile, j * tile, subs


def forward_kernel(
    place_ref, got_ref, other_ref, x_ref, attn_ref, mine_ref, theirs_ref, stat_ref, k_ref, slot_ref, stats_ref
):
    core, begin, turn, end1, end2 = place_of(place_ref)
    whole, rest = turn // BLOCK, turn % BLOCK
    lane = lanes()
    for b in range(N_BLOCKS):
        j = b // 2
        mine = jnp.where(low_is_mine(j, core, begin), got_ref[j], got_ref[8 + j])
        here = jnp.where(core == b % 2, mine, other_ref[j])
        slot_ref[b] = pltpu.roll(here.astype(F32), lax.rem(BLOCK - rest, BLOCK), 1)
    for b in range(N_BLOCKS):
        first, second = slot_ref[lax.rem(b + whole, N_BLOCKS)], slot_ref[lax.rem(b + whole + 1, N_BLOCKS)]
        here = jnp.where(lane < BLOCK - rest, first, second)
        x_ref[0:64, b * BLOCK : (b + 1) * BLOCK] = (here[0:64] * 0.125).astype(BF16)
        x_ref[64:256, b * BLOCK : (b + 1) * BLOCK] = here[64:256].astype(BF16)
        k_ref[b * BLOCK : (b + 1) * BLOCK, :] = here[64:128].astype(BF16).T

    for q_at, k_at, subs in below(HALF // F_TILE, F_TILE):
        weights = {}
        for q, k in subs:
            q_sub, k_sub = q_at + q * SUB, k_at + k * SUB
            s = dot(k_ref[k_sub : k_sub + SUB, :], x_ref[0:64, q_sub : q_sub + SUB])
            live = live_of(q_sub, k_sub, end1, end2, q_sub == k_sub)
            weights[q, k] = jnp.where(live, s * sigmoid(s), 0.0).astype(BF16)
        for q in range(F_TILE // SUB):
            q_sub = q_at + q * SUB
            acc = jnp.zeros((HEAD_DIM, SUB), F32)
            for k in range(F_TILE // SUB):
                if (q, k) in weights:
                    k_sub = k_at + k * SUB
                    acc += dot(x_ref[128:192, k_sub : k_sub + SUB], weights[q, k])
            attn_ref[:, q_sub : q_sub + SUB] = acc.astype(BF16)

    turned = []
    for b in range(N_BLOCKS):
        cols = slice(b * BLOCK, (b + 1) * BLOCK)
        attn = attn_ref[:, cols].astype(F32)
        g = x_ref[192:256, cols].astype(F32)
        mean = jnp.mean(attn, axis=0, keepdims=True)
        centre = attn - mean
        both = jnp.sum(centre * g, axis=0, keepdims=True)
        mean_hi = mean.astype(BF16).astype(F32)
        square = jnp.sum(centre * centre, axis=0, keepdims=True)
        total = jnp.sum(g, axis=0, keepdims=True)
        for i, row in enumerate((mean_hi, mean - mean_hi, both, square, total)):
            stats_ref[i * N_BLOCKS + b : i * N_BLOCKS + b + 1, :] = row
        turned.append(attn)
    stat_ref[...] = stats_ref[...].astype(BF16)
    turn_out(turned, turn, core, slot_ref, mine_ref, theirs_ref)


def turn_out(blocks, turn, core, slot_ref, mine_ref, theirs_ref):
    whole, rest = turn // BLOCK, turn % BLOCK
    rows = blocks[0].shape[0]
    for b, block in enumerate(blocks):
        slot_ref[b, 0:rows, :] = pltpu.roll(block, rest, 1)
    from_this = lanes() >= rest
    for j in range(8):
        pair = []
        for b in (2 * j, 2 * j + 1):
            this = slot_ref[lax.rem(b - whole + N_BLOCKS, N_BLOCKS), 0:rows, :]
            last = slot_ref[lax.rem(b - whole + N_BLOCKS - 1, N_BLOCKS), 0:rows, :]
            pair.append(jnp.where(from_this, this, last).astype(BF16))
        mine_ref[j] = jnp.where(core == 0, pair[0], pair[1])
        theirs_ref[j] = jnp.where(core == 0, pair[1], pair[0])


def backward_kernel(
    place_ref, x_ref, attn_ref, got_ref, mine_ref, theirs_ref,
    qn_ref, kn_ref, vn_ref, dn_ref, dt_ref, dq_ref, dk_ref, dv_ref, slot_ref,
):
    core, _, turn, end1, end2 = place_of(place_ref)
    stat = got_ref[:, 64 : 64 + STATS * N_BLOCKS, :].astype(F32).reshape(HEADS, STATS, N_BLOCKS, BLOCK)
    mean_h = stat[:, 0] + stat[:, 1]
    mean = jnp.mean(mean_h, axis=0)
    off = mean_h - mean[None]
    square = jnp.sum(stat[:, 3] + HEAD_DIM * off * off, axis=0)
    rstd = lax.rsqrt(square * (1.0 / WIDTH) + 1e-05)
    g_sum = stat[:, 4]
    g_mean = jnp.sum(g_sum, axis=0) * (1.0 / WIDTH)
    both = jnp.sum(stat[:, 2] + off * g_sum, axis=0) * rstd * (1.0 / WIDTH)
    for b in range(N_BLOCKS):
        cols = slice(b * BLOCK, (b + 1) * BLOCK)
        here = x_ref[:, cols]
        r = rstd[b : b + 1]
        normed = (attn_ref[:, cols].astype(F32) - mean[b : b + 1]) * r
        d = (r * (here[192:256].astype(F32) - g_mean[b : b + 1] - normed * both[b : b + 1])).astype(BF16)
        dt_ref[:, cols] = d
        dn_ref[cols, :] = d.T
        qn_ref[cols, :] = here[0:64].T
        kn_ref[cols, :] = here[64:128].T
        vn_ref[cols, :] = here[128:192].T

    for q_at, k_at, subs in below(HALF // B_TILE, B_TILE):
        made = {}
        for q, k in subs:
            q_cols = slice(q_at + q * SUB, q_at + (q + 1) * SUB)
            k_cols = slice(k_at + k * SUB, k_at + (k + 1) * SUB)
            s = dot(kn_ref[k_cols, :], x_ref[0:64, q_cols])
            d_p = dot(vn_ref[k_cols, :], dt_ref[:, q_cols])
            live = live_of(q_cols.start, k_cols.start, end1, end2, q_cols.start == k_cols.start)
            sigma = jnp.where(live, sigmoid(s), 0.0)
            silu = s * sigma
            made[q, k] = silu.astype(BF16), (d_p * (sigma + silu * (1.0 - sigma))).astype(BF16)
        for k in range(B_TILE // SUB):
            k_cols = slice(k_at + k * SUB, k_at + (k + 1) * SUB)
            d_v, d_k = [], []
            for q in range(B_TILE // SUB):
                if (q, k) in made:
                    q_cols = slice(q_at + q * SUB, q_at + (q + 1) * SUB)
                    d_v.append(dot(made[q, k][0], dn_ref[q_cols, :]))
                    d_k.append(dot(made[q, k][1], qn_ref[q_cols, :]))
            if q_at == k_at:
                dv_ref[k_cols, :], dk_ref[k_cols, :] = sum(d_v), sum(d_k)
            else:
                dv_ref[k_cols, :] += sum(d_v)
                dk_ref[k_cols, :] += sum(d_k)
        for q in range(B_TILE // SUB):
            q_cols = slice(q_at + q * SUB, q_at + (q + 1) * SUB)
            d_q = []
            for k in range(B_TILE // SUB):
                if (q, k) in made:
                    d_q.append(dot(x_ref[64:128, k_at + k * SUB : k_at + (k + 1) * SUB], made[q, k][1]))
            if k_at == 0:
                dq_ref[:, q_cols] = sum(d_q)
            else:
                dq_ref[:, q_cols] += sum(d_q)

    turned = []
    for b in range(N_BLOCKS):
        cols = slice(b * BLOCK, (b + 1) * BLOCK)
        turned.append(jnp.concatenate([dq_ref[:, cols] * 0.125, dk_ref[cols, :].T, dv_ref[cols, :].T], axis=0))
    turn_out(turned, turn, core, slot_ref, mine_ref, theirs_ref)


def prepare_kernel(q_ref, k_ref, v_ref, u_ref, cot_ref, w_ref, send_ref, ut_ref, dg_ref):
    d_gated = dot_nt(w_ref[...], cot_ref[...])
    u_t = u_ref[...].T
    dg_ref[...] = d_gated
    ut_ref[...] = u_t
    g_t = (d_gated * u_t.astype(F32)).astype(BF16)
    for i, rows in enumerate((q_ref[...].T, k_ref[...].T, v_ref[...].T, g_t)):
        for h in range(4):
            send_ref[h, i * 64 : (i + 1) * 64, :] = rows[h * 64 : (h + 1) * 64]


def other_half_kernel(place_ref, got_ref, out_ref):
    core, begin = place_of(place_ref)[:2]
    for j in range(8):
        out_ref[j] = jnp.where(low_is_mine(j, core, begin), got_ref[8 + j], got_ref[j])


def to_owners_kernel(place_ref, mine_ref, theirs_ref, out_ref):
    core, begin = place_of(place_ref)[:2]
    for j in range(8):
        low_mine = low_is_mine(j, core, begin)
        mine, theirs = mine_ref[j], theirs_ref[j]
        out_ref[j] = jnp.where(low_mine, mine, theirs)
        out_ref[8 + j] = jnp.where(low_mine, theirs, mine)


def attn_to_owners_kernel(place_ref, mine_ref, theirs_ref, stat_ref, out_ref):
    to_owners_kernel(place_ref, mine_ref, theirs_ref, out_ref.at[:, 0:64, :])
    for j in range(HEADS):
        out_ref[j, 64:, :] = stat_ref[...]


def normalised(got_ref):
    attn = got_ref[:, 0:64, :].astype(F32).reshape(WIDTH, BLOCK)
    centre = attn - jnp.mean(attn, axis=0, keepdims=True)
    return centre * lax.rsqrt(jnp.mean(centre * centre, axis=0, keepdims=True) + 1e-05)


def gated_kernel(place_ref, got_ref, ut_ref, mine_ref, theirs_ref, zero_ref, one_ref):
    core = place_ref[4]
    gated = normalised(got_ref) * ut_ref[...].astype(F32)
    for z in range(0, 8, 2):
        for chip in range(HEADS):
            at = z * BLOCK + chip * 8
            one, two = gated[at : at + 8], gated[at + BLOCK : at + BLOCK + 8]
            rows = slice(chip * 32 + z * 4, chip * 32 + z * 4 + 8)
            zero_ref[rows, :] = jnp.concatenate([one[0:4], two[0:4]], axis=0)
            one_ref[rows, :] = jnp.concatenate([one[4:8], two[4:8]], axis=0)
    zero, one = zero_ref[...].astype(BF16), one_ref[...].astype(BF16)
    mine_ref[...] = jnp.where(core == 0, zero, one)
    theirs_ref[...] = jnp.where(core == 0, one, zero)


def d_gate_kernel(got_ref, dg_ref, after_ref, out_ref):
    d_gate = (dg_ref[...] * normalised(got_ref)).astype(BF16)
    for i in range(WIDTH // BLOCK):
        out_ref[:, i * BLOCK : (i + 1) * BLOCK] = d_gate[i * BLOCK : (i + 1) * BLOCK].T


def product_kernel(a_ref, b_ref, c_ref, d_ref, out_ref):
    for at in range(0, 512, 128):
        rows = slice(at, at + 128)
        out_ref[rows, :] = (dot(a_ref[rows, :], c_ref[...]) + dot(b_ref[rows, :], d_ref[...])).astype(BF16)


def finish_kernel(got_ref, dq_ref, dk_ref, dv_ref):
    for i, out_ref in enumerate((dq_ref, dk_ref, dv_ref)):
        for h in range(0, HEADS, 2):
            pair = got_ref[h : h + 2, i * 64 : (i + 1) * 64, :].reshape(BLOCK, BLOCK)
            out_ref[:, h * 64 : (h + 2) * 64] = pair.T


SMEM = pl.BlockSpec(memory_space=pltpu.SMEM)
VMEM = pl.BlockSpec(memory_space=pltpu.VMEM)


def call(kernel, name, out_shape, in_specs, args, scratch=(), flops=1 << 28, transcendentals=0):
    return pl.pallas_call(
        kernel,
        out_shape=out_shape,
        in_specs=in_specs,
        out_specs=jax.tree.map(lambda _: VMEM, out_shape),
        scratch_shapes=list(scratch),
        compiler_params=pltpu.CompilerParams(vmem_limit_bytes=56 * 1024 * 1024),
        cost_estimate=pl.CostEstimate(flops=flops, bytes_accessed=1 << 21, transcendentals=transcendentals),
        name=name,
    )(*args)


def shape(dims, dtype=BF16):
    return jax.ShapeDtypeStruct(dims, dtype)


def prepare(query, key, value, gate_u, cotangent, out_weight):
    cols = pl.BlockSpec((BLOCK, 256), lambda i: (0, i))
    return pl.pallas_call(
        prepare_kernel,
        grid=(4,),
        out_shape=(shape((HEADS, 256, BLOCK)), shape((WIDTH, BLOCK)), shape((WIDTH, BLOCK), F32)),
        in_specs=[cols] * 4
        + [pl.BlockSpec((BLOCK, WIDTH), lambda i: (0, 0)), pl.BlockSpec((256, WIDTH), lambda i: (i, 0))],
        out_specs=(
            pl.BlockSpec((4, 256, BLOCK), lambda i: (i, 0, 0)),
            pl.BlockSpec((256, BLOCK), lambda i: (i, 0)),
            pl.BlockSpec((256, BLOCK), lambda i: (i, 0)),
        ),
        name="prepare",
    )(query, key, value, gate_u, cotangent, out_weight)


def attend_forward(place, got, other):
    return call(
        forward_kernel,
        "attend_forward",
        (
            shape((256, HALF)),
            shape((HEAD_DIM, HALF)),
            shape((8, HEAD_DIM, BLOCK)),
            shape((8, HEAD_DIM, BLOCK)),
            shape((STATS * N_BLOCKS, BLOCK)),
        ),
        [SMEM, VMEM, VMEM],
        (place, got, other),
        [
            pltpu.VMEM((HALF, HEAD_DIM), BF16),
            pltpu.VMEM((N_BLOCKS, 256, BLOCK), F32),
            pltpu.VMEM((STATS * N_BLOCKS, BLOCK), F32),
        ],
        flops=1 << 30,
        transcendentals=1 << 22,
    )


def attend_backward(place, x, attn, got):
    return call(
        backward_kernel,
        "attend_backward",
        (shape((8, 192, BLOCK)), shape((8, 192, BLOCK))),
        [SMEM, VMEM, VMEM, VMEM],
        (place, x, attn, got),
        [pltpu.VMEM((HALF, HEAD_DIM), BF16)] * 4
        + [pltpu.VMEM((HEAD_DIM, HALF), BF16), pltpu.VMEM((HEAD_DIM, HALF), F32)]
        + [pltpu.VMEM((HALF, HEAD_DIM), F32)] * 2
        + [pltpu.VMEM((N_BLOCKS, 192, BLOCK), F32)],
        flops=1 << 33,
        transcendentals=1 << 24,
    )


def on_device(query, key, value, gate_u, out_weight, cotangent, hist_lengths):
    core = lax.axis_index("core")
    place = jnp.concatenate([hist_lengths[0], core[None]]).astype(jnp.int32)

    def swap(x):
        return lax.ppermute(x, "core", SWAP)

    def chips(x):
        return lax.all_to_all(x, CHIP, 0, 0, tiled=True)

    send, u_t, d_gated_t = prepare(query, key, value, gate_u, cotangent, out_weight)
    got = chips(send)
    theirs = call(other_half_kernel, "other_half", shape((8, 256, BLOCK)), [SMEM, VMEM], (place, got))
    x, attn, mine, theirs, stat = attend_forward(place, got, swap(theirs))

    rows = HEAD_DIM + STATS * N_BLOCKS
    send = call(
        attn_to_owners_kernel,
        "attn_to_owners",
        shape((HEADS, rows, BLOCK)),
        [SMEM] + [VMEM] * 3,
        (place, mine, swap(theirs), stat),
    )
    got_attn = chips(send)

    mine, theirs = call(
        gated_kernel,
        "gated",
        (shape((512, BLOCK)), shape((512, BLOCK))),
        [SMEM] + [VMEM] * 2,
        (place, got_attn, u_t),
        [pltpu.VMEM((512, BLOCK), F32)] * 2,
    )
    part = call(
        product_kernel,
        "product",
        shape((512, WIDTH)),
        [VMEM] * 4,
        (mine, swap(theirs), cotangent, swap(cotangent)),
    )
    parts = chips(part.reshape(HEADS, 32, WIDTH))

    mine, theirs = attend_backward(place, x, attn, got_attn)
    send = call(
        to_owners_kernel,
        "grads_to_owners",
        shape((HEADS, 192, BLOCK)),
        [SMEM] + [VMEM] * 2,
        (place, mine, swap(theirs)),
    )
    got = chips(send)

    part = jnp.sum(parts.astype(F32), axis=0).reshape(8, 4, WIDTH)
    z = lax.axis_index("dp")
    for step in (4, 2, 1):
        high = (z // step) % 2
        halves = part.reshape(2, step, 4, WIDTH)
        away = lax.dynamic_index_in_dim(halves, 1 - high, 0, keepdims=False)
        kept = lax.dynamic_index_in_dim(halves, high, 0, keepdims=False)
        part = kept + lax.ppermute(away, "dp", [(i, i ^ step) for i in range(8)])
    d_weight = part.reshape(4, WIDTH) * (1.0 / math.sqrt(32768))

    d_gate = call(
        d_gate_kernel,
        "d_gate",
        shape((BLOCK, WIDTH)),
        [VMEM, VMEM, pl.BlockSpec(memory_space=pl.ANY)],
        (got_attn, d_gated_t, send),
    )
    d_query, d_key, d_value = call(finish_kernel, "finish", (shape((BLOCK, WIDTH)),) * 3, [VMEM], (got,))
    return d_query, d_key, d_value, d_gate, d_weight


def solution(mesh):
    axes = ("dp", "x", "y", "core")
    inner = Mesh(mesh.devices.reshape(8, 4, 4, 2), axes)
    rows = P(axes, None)
    return jax.shard_map(
        on_device,
        mesh=inner,
        in_specs=(rows, rows, rows, rows, P(), rows, P("dp", None)),
        out_specs=(rows, rows, rows, rows, rows),
        check_vma=False,
    )
```

profile of v0, /device:TPU:2, one launch (start us, length us, event | category | flops | bytes accessed | tf_op | source)
XLA Modules:
  0.0 122.3 jit_solution(17175051001859258379)
XLA Ops:
  0.6 0.0 copy-start.9
  0.6 4.7 %prepare.1 = (bf16[16,256,128]{2,1,0:T(8,128)(2,1)}, bf16[1024,128]{1,0:T(8,128)(2,1)}, f32[1024,128]{1,0:T(8,128)}) custom-call(bf16[128,1024]{1,0:T(8,128)(2,1)} %q_ref.1, bf16[128,1024]{1,0:T(8,128)(2,1)} %k_ref.1, bf16[128,1024]{1,0:T(8,128)(2,1)} %v_ref.1, bf16[128,1024]{1,0:T(8,128)(2,1)} %u_ref.1, bf16[128,1024]{1,0:T(8,128)(2,1)} %c_ref.1, ...), custom_call_target="tpu_custom_call" | custom-call | tf_op jit(solution)/shard_map/prepare/pallas_call | solution.py:304
  5.3 7.5 %all-to-all-start = ((bf16[16,256,128]{2,1,0:T(8,128)(2,1)}), bf16[16,256,128]{2,1,0:T(8,128)(2,1)S(1)}, u32[]{:S(2)}, u32[]{:S(2)}) async-start(bf16[16,256,128]{2,1,0:T(8,128)(2,1)} %get-tuple-element.20), calls=%async_computation | async-start | bytes 2097152 | tf_op jit(solution)/shard_map/all_to_all | solution.py:366
  12.8 0.0 copy-done.9
  12.8 0.7 pad_add_fusion.place_ref
  13.5 14.4 %all-to-all-done.got_ref = bf16[16,256,128]{2,1,0:T(8,128)(2,1)S(1)} async-done(((bf16[16,256,128]{2,1,0:T(8,128)(2,1)}), bf16[16,256,128]{2,1,0:T(8,128)(2,1)S(1)}, u32[]{:S(2)}, u32[]{:S(2)}) %all-to-all-start) | async-done | bytes 1048608 | tf_op jit(solution)/shard_map/all_to_all | solution.py:366
  27.9 0.0 copy-start
  27.9 1.0 copy-done
  28.8 2.2 %other_half.1 = bf16[8,256,128]{2,1,0:T(8,128)(2,1)} custom-call(s32[5]{0:T(128)} %pad_add_fusion.place_ref, bf16[16,256,128]{2,1,0:T(8,128)(2,1)} %copy-done), custom_call_target="tpu_custom_call" | custom-call | flops 268435456 | bytes 2097152 | tf_op jit(solution)/shard_map/other_half/pallas_call | solution.py:286
  31.0 0.0 collective-permute-start
  31.0 2.1 %collective-permute-done.other_ref = bf16[8,256,128]{2,1,0:T(8,128)(2,1)S(1)} collective-permute-done((bf16[8,256,128]{2,1,0:T(8,128)(2,1)}, bf16[8,256,128]{2,1,0:T(8,128)(2,1)S(1)}, u32[]{:S(2)}, u32[]{:S(2)}) %collective-permute-start) | collective-permute-done | bytes 524320 | tf_op jit(solution)/shard_map/ppermute | solution.py:363
  33.1 0.0 copy-start.7
  33.1 0.8 copy-done.7
  33.9 6.5 %attend_forward.1 = (bf16[256,2048]{1,0:T(8,128)(2,1)}, bf16[64,2048]{1,0:T(8,128)(2,1)}, bf16[8,64,128]{2,1,0:T(8,128)(2,1)}, bf16[8,64,128]{2,1,0:T(8,128)(2,1)}, bf16[80,128]{1,0:T(8,128)(2,1)}) custom-call(s32[5]{0:T(128)} %pad_add_fusion.place_ref, bf16[16,256,128]{2,1,0:T(8,128)(2,1)} %copy-done, bf16[8,256,128]{2,1,0:T(8,128)(2,1)} %copy-done.7), custom_call_target="tpu_custom_call" | custom-call | flops 1073741824 | bytes 2097152 | tf_op jit(solution)/shard_map/attend_forward/pallas_call | solution.py:286
  40.4 0.0 copy-start.2
  40.4 0.1 collective-permute-start.1
  40.6 1.4 %collective-permute-done.1.theirs_ref = bf16[8,64,128]{2,1,0:T(8,128)(2,1)S(1)} collective-permute-done((bf16[8,64,128]{2,1,0:T(8,128)(2,1)}, bf16[8,64,128]{2,1,0:T(8,128)(2,1)S(1)}, u32[]{:S(2)}, u32[]{:S(2)}) %collective-permute-start.1) | collective-permute-done | bytes 131104 | tf_op jit(solution)/shard_map/ppermute | solution.py:363
  42.0 0.0 copy-start.8
  42.0 0.7 copy-done.8
  42.6 1.9 %attn_to_owners.1 = bf16[16,144,128]{2,1,0:T(8,128)(2,1)} custom-call(s32[5]{0:T(128)} %pad_add_fusion.place_ref, bf16[8,64,128]{2,1,0:T(8,128)(2,1)} %get-tuple-element.23.mine_ref, bf16[8,64,128]{2,1,0:T(8,128)(2,1)} %copy-done.8, bf16[80,128]{1,0:T(8,128)(2,1)} %get-tuple-element.25.stat_ref), custom_call_target="tpu_custom_call" | custom-call | flops 268435456 | bytes 2097152 | tf_op jit(solution)/shard_map/attn_to_owners/pallas_call | solution.py:286
  44.5 6.1 %all-to-all-start.1 = ((bf16[16,144,128]{2,1,0:T(8,128)(2,1)}), bf16[16,144,128]{2,1,0:T(8,128)(2,1)S(1)}, u32[]{:S(2)}, u32[]{:S(2)}) async-start(bf16[16,144,128]{2,1,0:T(8,128)(2,1)} %attn_to_owners.1), calls=%async_computation.1 | async-start | bytes 1179648 | tf_op jit(solution)/shard_map/all_to_all | solution.py:366
  50.7 0.0 copy-done.2
  50.7 0.1 collective-permute-start.4
  50.8 10.4 %all-to-all-done.1.got_ref = bf16[16,144,128]{2,1,0:T(8,128)(2,1)S(1)} async-done(((bf16[16,144,128]{2,1,0:T(8,128)(2,1)}), bf16[16,144,128]{2,1,0:T(8,128)(2,1)S(1)}, u32[]{:S(2)}, u32[]{:S(2)}) %all-to-all-start.1) | async-done | bytes 589856 | tf_op jit(solution)/shard_map/all_to_all | solution.py:366
  61.2 0.0 copy-start.1
  61.2 0.8 copy-done.1
  62.0 2.2 %gated.1 = (bf16[512,128]{1,0:T(8,128)(2,1)}, bf16[512,128]{1,0:T(8,128)(2,1)}) custom-call(s32[5]{0:T(128)} %pad_add_fusion.place_ref, bf16[16,144,128]{2,1,0:T(8,128)(2,1)} %copy-done.1, bf16[1024,128]{1,0:T(8,128)(2,1)} %get-tuple-element.32.ut_ref), custom_call_target="tpu_custom_call" | custom-call | flops 268435456 | bytes 2097152 | tf_op jit(solution)/shard_map/gated/pallas_call | solution.py:286
  64.3 0.0 collective-permute-start.3
  64.3 0.0 collective-permute-done.4.d_ref
  64.3 0.0 copy-start.5
  64.3 1.5 %collective-permute-done.3.b_ref = bf16[512,128]{1,0:T(8,128)(2,1)S(1)} collective-permute-done((bf16[512,128]{1,0:T(8,128)(2,1)}, bf16[512,128]{1,0:T(8,128)(2,1)S(1)}, u32[]{:S(2)}, u32[]{:S(2)}) %collective-permute-start.3) | collective-permute-done | bytes 131104 | tf_op jit(solution)/shard_map/ppermute | solution.py:363
  65.8 0.0 copy-start.6
  65.8 0.0 copy-done.5
  65.8 0.7 copy-done.6
  66.5 2.8 %product.1 = bf16[512,1024]{1,0:T(8,128)(2,1)} custom-call(bf16[512,128]{1,0:T(8,128)(2,1)} %get-tuple-element.33.a_ref, bf16[512,128]{1,0:T(8,128)(2,1)} %copy-done.6, bf16[128,1024]{1,0:T(8,128)(2,1)} %c_ref.1, bf16[128,1024]{1,0:T(8,128)(2,1)} %copy-done.5), custom_call_target="tpu_custom_call" | custom-call | flops 268435456 | bytes 2097152 | tf_op jit(solution)/shard_map/product/pallas_call | solution.py:286
  69.3 5.9 %all-to-all-start.3 = ((bf16[16,32,1024]{2,1,0:T(8,128)(2,1)}), bf16[16,32,1024]{2,1,0:T(8,128)(2,1)S(1)}, u32[]{:S(2)}, u32[]{:S(2)}) async-start(bf16[16,32,1024]{2,1,0:T(8,128)(2,1)} %bitcast.14), calls=%async_computation.3 | async-start | bytes 2097152 | tf_op jit(solution)/shard_map/all_to_all | solution.py:366
  75.2 10.6 %attend_backward.1 = (bf16[8,192,128]{2,1,0:T(8,128)(2,1)}, bf16[8,192,128]{2,1,0:T(8,128)(2,1)}) custom-call(s32[5]{0:T(128)} %pad_add_fusion.place_ref, bf16[256,2048]{1,0:T(8,128)(2,1)} %get-tuple-element.21.x_ref, bf16[64,2048]{1,0:T(8,128)(2,1)} %get-tuple-element.22.attn_ref, bf16[16,144,128]{2,1,0:T(8,128)(2,1)} %copy-done.1), custom_call_target="tpu_custom_call" | custom-call | flops 8589934592 | bytes 2097152 | tf_op jit(solution)/shard_map/attend_backward/pallas_call | solution.py:286
  85.8 0.0 collective-permute-start.2
  85.8 5.2 %all-to-all-done.3 = bf16[16,32,1024]{2,1,0:T(8,128)(2,1)S(1)} async-done(((bf16[16,32,1024]{2,1,0:T(8,128)(2,1)}), bf16[16,32,1024]{2,1,0:T(8,128)(2,1)S(1)}, u32[]{:S(2)}, u32[]{:S(2)}) %all-to-all-start.3) | async-done | bytes 1048608 | tf_op jit(solution)/shard_map/all_to_all | solution.py:366
  91.0 0.2 convert_reduce_fusion
  91.3 7.3 %collective-permute-start.5 = (f32[4,4,1024]{2,1,0:T(4,128)S(1)}, f32[4,4,1024]{2,1,0:T(4,128)S(1)}, u32[]{:S(2)}, u32[]{:S(2)}) collective-permute-start(f32[4,4,1024]{2,1,0:T(4,128)S(1)} %dynamic-slice_bitcast_fusion), channel_id=1, source_target_pairs={{0,128},{32,160},{64,192},{96,224},{128,0},{160,32},{192,64},{224,... | collective-permute-start | bytes 196616 | tf_op jit(solution)/shard_map/ppermute | solution.py:417
  98.5 0.0 collective-permute-done.2.theirs_ref
  98.5 0.0 copy-start.4
  98.5 0.8 copy-done.4
  99.3 2.2 %grads_to_owners.1.after_ref = bf16[16,192,128]{2,1,0:T(8,128)(2,1)} custom-call(s32[5]{0:T(128)} %pad_add_fusion.place_ref, bf16[8,192,128]{2,1,0:T(8,128)(2,1)} %get-tuple-element.26.mine_ref, bf16[8,192,128]{2,1,0:T(8,128)(2,1)} %copy-done.4), custom_call_target="tpu_custom_call" | custom-call | flops 268435456 | bytes 2097152 | tf_op jit(solution)/shard_map/grads_to_owners/pallas_call | solution.py:286
  101.5 6.2 %all-to-all-start.2 = ((bf16[16,192,128]{2,1,0:T(8,128)(2,1)}), bf16[16,192,128]{2,1,0:T(8,128)(2,1)S(1)}, u32[]{:S(2)}, u32[]{:S(2)}) async-start(bf16[16,192,128]{2,1,0:T(8,128)(2,1)} %grads_to_owners.1.after_ref), calls=%async_computation.2 | async-start | bytes 1572864 | tf_op jit(solution)/shard_map/all_to_all | solution.py:366
  107.6 0.0 collective-permute-done.5
  107.7 1.6 %collective-permute-start.6 = (f32[2,4,1024]{2,1,0:T(4,128)S(1)}, f32[2,4,1024]{2,1,0:T(4,128)S(1)}, u32[]{:S(2)}, u32[]{:S(2)}) collective-permute-start(f32[2,4,1024]{2,1,0:T(4,128)S(1)} %dynamic-slice_bitcast_fusion.1), channel_id=1, source_target_pairs={{0,64},{32,96},{64,0},{96,32},{128,192},{160,224},{192,128},{224,1... | collective-permute-start | bytes 98312 | tf_op jit(solution)/shard_map/ppermute | solution.py:417
  109.3 2.3 %d_gate.1 = bf16[128,1024]{1,0:T(8,128)(2,1)} custom-call(bf16[16,144,128]{2,1,0:T(8,128)(2,1)} %copy-done.1, f32[1024,128]{1,0:T(8,128)} %get-tuple-element.31.dg_ref, bf16[16,192,128]{2,1,0:T(8,128)(2,1)} %grads_to_owners.1.after_ref), custom_call_target="tpu_custom_call" | custom-call | flops 268435456 | bytes 2097152 | tf_op jit(solution)/shard_map/d_gate/pallas_call | solution.py:286
  111.6 1.0 collective-permute-done.6
  112.6 1.1 collective-permute-start.7
  113.7 4.9 %all-to-all-done.2.got_ref = bf16[16,192,128]{2,1,0:T(8,128)(2,1)S(1)} async-done(((bf16[16,192,128]{2,1,0:T(8,128)(2,1)}), bf16[16,192,128]{2,1,0:T(8,128)(2,1)S(1)}, u32[]{:S(2)}, u32[]{:S(2)}) %all-to-all-start.2) | async-done | bytes 786464 | tf_op jit(solution)/shard_map/all_to_all | solution.py:366
  118.7 0.0 copy-start.3
  118.7 0.9 copy-done.3
  119.5 2.1 %finish.1 = (bf16[128,1024]{1,0:T(8,128)(2,1)}, bf16[128,1024]{1,0:T(8,128)(2,1)}, bf16[128,1024]{1,0:T(8,128)(2,1)}) custom-call(bf16[16,192,128]{2,1,0:T(8,128)(2,1)} %copy-done.3), custom_call_target="tpu_custom_call" | custom-call | flops 268435456 | bytes 2097152 | tf_op jit(solution)/shard_map/finish/pallas_call | solution.py:286
  121.7 0.0 collective-permute-done.7
  121.7 0.6 multiply_bitcast_fusion
  (6 shorter events, 0.1 us)
Async XLA Ops:
  0.6 12.2 %copy-start.9 = (s32[1,4]{1,0:T(1,128)S(1)}, s32[1,4]{1,0:T(1,128)}, u32[]{:S(2)}) copy-start(s32[1,4]{1,0:T(1,128)} %param.13) | copy-start | bytes 52
  5.3 22.5 %all-to-all-start = ((bf16[16,256,128]{2,1,0:T(8,128)(2,1)}), bf16[16,256,128]{2,1,0:T(8,128)(2,1)S(1)}, u32[]{:S(2)}, u32[]{:S(2)}) async-start(bf16[16,256,128]{2,1,0:T(8,128)(2,1)} %get-tuple-element.20), calls=%async_computation | async-start | bytes 2097152 | tf_op jit(solution)/shard_map/all_to_all | solution.py:366
  27.9 1.0 copy-start
  31.0 2.1 %collective-permute-start = (bf16[8,256,128]{2,1,0:T(8,128)(2,1)}, bf16[8,256,128]{2,1,0:T(8,128)(2,1)S(1)}, u32[]{:S(2)}, u32[]{:S(2)}) collective-permute-start(bf16[8,256,128]{2,1,0:T(8,128)(2,1)} %other_half.1), channel_id=1, source_target_pairs={{0,1},{1,0},{2,3},{3,2},{4,5},{5,4},{6,7},{7,6},{8,9},{9,8},{10,11... | collective-permute-start | bytes 1572872 | tf_op jit(solution)/shard_map/ppermute | solution.py:363
  33.1 0.8 copy-start.7
  40.4 10.2 %copy-start.2 = (bf16[128,1024]{1,0:T(8,128)(2,1)S(1)}, bf16[128,1024]{1,0:T(8,128)(2,1)}, u32[]{:S(2)}) copy-start(bf16[128,1024]{1,0:T(8,128)(2,1)} %c_ref.1) | copy-start | bytes 786436
  40.4 1.6 %collective-permute-start.1 = (bf16[8,64,128]{2,1,0:T(8,128)(2,1)}, bf16[8,64,128]{2,1,0:T(8,128)(2,1)S(1)}, u32[]{:S(2)}, u32[]{:S(2)}) collective-permute-start(bf16[8,64,128]{2,1,0:T(8,128)(2,1)} %get-tuple-element.24), channel_id=1, source_target_pairs={{0,1},{1,0},{2,3},{3,2},{4,5},{5,4},{6,7},{7,6},{8,9},{9,8},{10,11... | collective-permute-start | bytes 393224 | tf_op jit(solution)/shard_map/ppermute | solution.py:363
  42.0 0.7 copy-start.8
  44.5 16.6 %all-to-all-start.1 = ((bf16[16,144,128]{2,1,0:T(8,128)(2,1)}), bf16[16,144,128]{2,1,0:T(8,128)(2,1)S(1)}, u32[]{:S(2)}, u32[]{:S(2)}) async-start(bf16[16,144,128]{2,1,0:T(8,128)(2,1)} %attn_to_owners.1), calls=%async_computation.1 | async-start | bytes 1179648 | tf_op jit(solution)/shard_map/all_to_all | solution.py:366
  50.7 13.6 %collective-permute-start.4 = (bf16[128,1024]{1,0:T(8,128)(2,1)S(1)}, bf16[128,1024]{1,0:T(8,128)(2,1)S(1)}, u32[]{:S(2)}, u32[]{:S(2)}) collective-permute-start(bf16[128,1024]{1,0:T(8,128)(2,1)S(1)} %copy-done.2), channel_id=1, source_target_pairs={{0,1},{1,0},{2,3},{3,2},{4,5},{5,4},{6,7},{7,6},{8,9},{9,8},{10,11... | collective-permute-start | bytes 786440 | tf_op jit(solution)/shard_map/ppermute | solution.py:363
  61.2 0.8 copy-start.1
  64.3 1.6 %collective-permute-start.3 = (bf16[512,128]{1,0:T(8,128)(2,1)}, bf16[512,128]{1,0:T(8,128)(2,1)S(1)}, u32[]{:S(2)}, u32[]{:S(2)}) collective-permute-start(bf16[512,128]{1,0:T(8,128)(2,1)} %get-tuple-element.34), channel_id=1, source_target_pairs={{0,1},{1,0},{2,3},{3,2},{4,5},{5,4},{6,7},{7,6},{8,9},{9,8},{10,11... | collective-permute-start | bytes 393224 | tf_op jit(solution)/shard_map/ppermute | solution.py:363
  64.3 1.6 %copy-start.5 = (bf16[128,1024]{1,0:T(8,128)(2,1)}, bf16[128,1024]{1,0:T(8,128)(2,1)S(1)}, u32[]{:S(2)}) copy-start(bf16[128,1024]{1,0:T(8,128)(2,1)S(1)} %collective-permute-done.4.d_ref) | copy-start | bytes 786436
  65.8 0.7 copy-start.6
  69.3 21.7 %all-to-all-start.3 = ((bf16[16,32,1024]{2,1,0:T(8,128)(2,1)}), bf16[16,32,1024]{2,1,0:T(8,128)(2,1)S(1)}, u32[]{:S(2)}, u32[]{:S(2)}) async-start(bf16[16,32,1024]{2,1,0:T(8,128)(2,1)} %bitcast.14), calls=%async_computation.3 | async-start | bytes 2097152 | tf_op jit(solution)/shard_map/all_to_all | solution.py:366
  85.8 12.8 %collective-permute-start.2 = (bf16[8,192,128]{2,1,0:T(8,128)(2,1)}, bf16[8,192,128]{2,1,0:T(8,128)(2,1)S(1)}, u32[]{:S(2)}, u32[]{:S(2)}) collective-permute-start(bf16[8,192,128]{2,1,0:T(8,128)(2,1)} %get-tuple-element.27), channel_id=1, source_target_pairs={{0,1},{1,0},{2,3},{3,2},{4,5},{5,4},{6,7},{7,6},{8,9},{9,8},{10,11... | collective-permute-start | bytes 1179656 | tf_op jit(solution)/shard_map/ppermute | solution.py:363
  91.3 16.4 %collective-permute-start.5 = (f32[4,4,1024]{2,1,0:T(4,128)S(1)}, f32[4,4,1024]{2,1,0:T(4,128)S(1)}, u32[]{:S(2)}, u32[]{:S(2)}) collective-permute-start(f32[4,4,1024]{2,1,0:T(4,128)S(1)} %dynamic-slice_bitcast_fusion), channel_id=1, source_target_pairs={{0,128},{32,160},{64,192},{96,224},{128,0},{160,32},{192,64},{224,... | collective-permute-start | bytes 196616 | tf_op jit(solution)/shard_map/ppermute | solution.py:417
  98.5 0.8 copy-start.4
  101.5 17.2 %all-to-all-start.2 = ((bf16[16,192,128]{2,1,0:T(8,128)(2,1)}), bf16[16,192,128]{2,1,0:T(8,128)(2,1)S(1)}, u32[]{:S(2)}, u32[]{:S(2)}) async-start(bf16[16,192,128]{2,1,0:T(8,128)(2,1)} %grads_to_owners.1.after_ref), calls=%async_computation.2 | async-start | bytes 1572864 | tf_op jit(solution)/shard_map/all_to_all | solution.py:366
  107.7 4.9 %collective-permute-start.6 = (f32[2,4,1024]{2,1,0:T(4,128)S(1)}, f32[2,4,1024]{2,1,0:T(4,128)S(1)}, u32[]{:S(2)}, u32[]{:S(2)}) collective-permute-start(f32[2,4,1024]{2,1,0:T(4,128)S(1)} %dynamic-slice_bitcast_fusion.1), channel_id=1, source_target_pairs={{0,64},{32,96},{64,0},{96,32},{128,192},{160,224},{192,128},{224,1... | collective-permute-start | bytes 98312 | tf_op jit(solution)/shard_map/ppermute | solution.py:417
  112.6 9.1 %collective-permute-start.7 = (f32[1,4,1024]{2,1,0:T(4,128)S(1)}, f32[1,4,1024]{2,1,0:T(4,128)S(1)}, u32[]{:S(2)}, u32[]{:S(2)}) collective-permute-start(f32[1,4,1024]{2,1,0:T(4,128)S(1)} %constant_dynamic-slice_fusion), channel_id=1, source_target_pairs={{0,32},{32,0},{64,96},{96,64},{128,160},{160,128},{192,224},{224,1... | collective-permute-start | bytes 49160 | tf_op jit(solution)/shard_map/ppermute | solution.py:417
  118.7 0.9 copy-start.3
where the time goes:
time: 124 us; the launch traced here: 122 us
  waiting for transfers between devices  41 us (33%)
  Pallas kernels  37.5 us (30%)
  starting transfers between devices  35.8 us (29%)
  local copies, waits for them, and re-layouts  5.65 us (5%)
  other arithmetic  1.5 us (1%)
    all_to_all x4, waiting for transfers between devices, chips(): return lax.all_to_all(x, CHIP, 0, 0, tiled=True)  35 us
    pallas_call x9, Pallas kernels, call(): pl.pallas_call(kernel, out_shape=out_shape, in_specs=in_specs, out_specs=...  32.8 us
    all_to_all x4, starting transfers between devices, chips(): return lax.all_to_all(x, CHIP, 0, 0, tiled=True)  25.7 us
    ppermute x3, starting transfers between devices, on_device(): part = kept + lax.ppermute(away, 'dp', [(i, i ^ step) for i in range(8)])  9.94 us
    unnamed x20, local copies, waits for them, and re-layouts  5.58 us
    ppermute x5, waiting for transfers between devices, swap(): return lax.ppermute(x, 'core', SWAP)  5.08 us
    pallas_call x1, Pallas kernels, prepare(): pl.pallas_call(prepare_kernel, grid=(4,), out_shape=(shape((HEADS, 256, B...  4.69 us
  transfers between devices with their start and end apart: 12, of which 8 were waited for; matrix products, arithmetic and copies ran while one was open for 1% of the time, Pallas kernels for 16%

commit v1 on v0

--- a/solution.py
+++ b/solution.py
@@ -29,6 +29,12 @@
 
 def dot_nt(a, b):
     return lax.dot_general(a, b, (((1,), (1,)), ((), ())), preferred_element_type=F32)
+
+
+def turned(x):
+    n = x.shape[1]
+    row, col = (lax.broadcasted_iota(jnp.int32, (n, n), i) for i in range(2))
+    return dot_nt(jnp.where(row == col, 1.0, 0.0).astype(BF16), x).astype(BF16)
 
 
 def sigmoid(s):
@@ -208,11 +214,11 @@
 
 def prepare_kernel(q_ref, k_ref, v_ref, u_ref, cot_ref, w_ref, send_ref, ut_ref, dg_ref):
     d_gated = dot_nt(w_ref[...], cot_ref[...])
-    u_t = u_ref[...].T
+    u_t = turned(u_ref[...])
     dg_ref[...] = d_gated
     ut_ref[...] = u_t
     g_t = (d_gated * u_t.astype(F32)).astype(BF16)
-    for i, rows in enumerate((q_ref[...].T, k_ref[...].T, v_ref[...].T, g_t)):
+    for i, rows in enumerate((turned(q_ref[...]), turned(k_ref[...]), turned(v_ref[...]), g_t)):
         for h in range(4):
             send_ref[h, i * 64 : (i + 1) * 64, :] = rows[h * 64 : (h + 1) * 64]
 
@@ -262,7 +268,7 @@
 def d_gate_kernel(got_ref, dg_ref, after_ref, out_ref):
     d_gate = (dg_ref[...] * normalised(got_ref)).astype(BF16)
     for i in range(WIDTH // BLOCK):
-        out_ref[:, i * BLOCK : (i + 1) * BLOCK] = d_gate[i * BLOCK : (i + 1) * BLOCK].T
+        out_ref[:, i * BLOCK : (i + 1) * BLOCK] = turned(d_gate[i * BLOCK : (i + 1) * BLOCK])
 
 
 def product_kernel(a_ref, b_ref, c_ref, d_ref, out_ref):
@@ -273,23 +279,23 @@
 
 def finish_kernel(got_ref, dq_ref, dk_ref, dv_ref):
     for i, out_ref in enumerate((dq_ref, dk_ref, dv_ref)):
-        for h in range(0, HEADS, 2):
-            pair = got_ref[h : h + 2, i * 64 : (i + 1) * 64, :].reshape(BLOCK, BLOCK)
-            out_ref[:, h * 64 : (h + 2) * 64] = pair.T
+        for h in range(0, HEADS, 4):
+            heads = got_ref[h : h + 4, i * 64 : (i + 1) * 64, :].reshape(256, BLOCK)
+            out_ref[:, h * 64 : (h + 4) * 64] = turned(heads)
 
 
 SMEM = pl.BlockSpec(memory_space=pltpu.SMEM)
 VMEM = pl.BlockSpec(memory_space=pltpu.VMEM)
 
 
-def call(kernel, name, out_shape, in_specs, args, scratch=(), flops=1 << 28, transcendentals=0):
+def call(kernel, name, out_shape, in_specs, args, scratch=(), mib=8, flops=1 << 26, transcendentals=0):
     return pl.pallas_call(
         kernel,
         out_shape=out_shape,
         in_specs=in_specs,
         out_specs=jax.tree.map(lambda _: VMEM, out_shape),
         scratch_shapes=list(scratch),
-        compiler_params=pltpu.CompilerParams(vmem_limit_bytes=56 * 1024 * 1024),
+        compiler_params=pltpu.CompilerParams(vmem_limit_bytes=mib * 1024 * 1024),
         cost_estimate=pl.CostEstimate(flops=flops, bytes_accessed=1 << 21, transcendentals=transcendentals),
         name=name,
     )(*args)
@@ -334,6 +340,7 @@
             pltpu.VMEM((N_BLOCKS, 256, BLOCK), F32),
             pltpu.VMEM((STATS * N_BLOCKS, BLOCK), F32),
         ],
+        mib=20,
         flops=1 << 30,
         transcendentals=1 << 22,
     )
@@ -350,6 +357,7 @@
         + [pltpu.VMEM((HEAD_DIM, HALF), BF16), pltpu.VMEM((HEAD_DIM, HALF), F32)]
         + [pltpu.VMEM((HALF, HEAD_DIM), F32)] * 2
         + [pltpu.VMEM((N_BLOCKS, 192, BLOCK), F32)],
+        mib=24,
         flops=1 << 33,
         transcendentals=1 << 24,
     )
@@ -406,7 +414,16 @@
         (place, mine, swap(theirs)),
     )
     got = chips(send)
-
+    d_gate = call(
+        d_gate_kernel,
+        "d_gate",
+        shape((BLOCK, WIDTH)),
+        [VMEM, VMEM, pl.BlockSpec(memory_space=pl.ANY)],
+        (got_attn, d_gated_t, send),
+        flops=1 << 20,
+    )
+
+    parts, d_gate = lax.optimization_barrier((parts, d_gate))
     part = jnp.sum(parts.astype(F32), axis=0).reshape(8, 4, WIDTH)
     z = lax.axis_index("dp")
     for step in (4, 2, 1):
@@ -417,13 +434,6 @@
         part = kept + lax.ppermute(away, "dp", [(i, i ^ step) for i in range(8)])
     d_weight = part.reshape(4, WIDTH) * (1.0 / math.sqrt(32768))
 
-    d_gate = call(
-        d_gate_kernel,
-        "d_gate",
-        shape((BLOCK, WIDTH)),
-        [VMEM, VMEM, pl.BlockSpec(memory_space=pl.ANY)],
-        (got_attn, d_gated_t, send),
-    )
     d_query, d_key, d_value = call(finish_kernel, "finish", (shape((BLOCK, WIDTH)),) * 3, [VMEM], (got,))
     return d_query, d_key, d_value, d_gate, d_weight
 

time: 124 us -> 111 us (0.90)
  Pallas kernels: 37.5 us -> 27.5 us
  local copies, waits for them, and re-layouts: 5.65 us -> 0.11 us
    pallas_call x9, Pallas kernels: 32.8 us -> 22.5 us  [call(): pl.pallas_call(kernel, out_shape=out_shape, in_specs=in_specs, out_specs=...]
    unnamed x20 -> x12, local copies, waits for them, and re-layouts: 5.58 us -> 0.03 us
    ppermute x3, waiting for transfers between devices: 1 us -> 3.37 us  [on_device(): part = kept + lax.ppermute(away, 'dp', [(i, i ^ step) for i in range(8)])]
    all_to_all x4, waiting for transfers between devices: 35 us -> 32.7 us  [chips(): return lax.all_to_all(x, CHIP, 0, 0, tiled=True)]
  transfers between devices with their start and end apart: 12 -> 12, of which waited for: 8 -> 9; matrix products, arithmetic and copies ran while one was open for 1% -> 0% of each run, Pallas kernels for 16% -> 13%
where the time goes in v1:
time: 111 us; the launch traced here: 110 us
  waiting for transfers between devices  42.2 us (38%)
  starting transfers between devices  36.9 us (33%)
  Pallas kernels  27.5 us (25%)
  other arithmetic  2.14 us (2%)
    all_to_all x4, waiting for transfers between devices, chips(): return lax.all_to_all(x, CHIP, 0, 0, tiled=True)  32.7 us
    all_to_all x4, starting transfers between devices, chips(): return lax.all_to_all(x, CHIP, 0, 0, tiled=True)  26.4 us
    pallas_call x9, Pallas kernels, call(): pl.pallas_call(kernel, out_shape=out_shape, in_specs=in_specs, out_specs=...  22.5 us
    ppermute x3, starting transfers between devices, on_device(): part = kept + lax.ppermute(away, 'dp', [(i, i ^ step) for i in range(8)])  9.92 us
    ppermute x5, waiting for transfers between devices, swap(): return lax.ppermute(x, 'core', SWAP)  6.11 us
    pallas_call x1, Pallas kernels, prepare(): pl.pallas_call(prepare_kernel, grid=(4,), out_shape=(shape((HEADS, 256, B...  4.94 us
    ppermute x3, waiting for transfers between devices, on_device(): part = kept + lax.ppermute(away, 'dp', [(i, i ^ step) for i in range(8)])  3.37 us
  transfers between devices with their start and end apart: 12, of which 9 were waited for; matrix products, arithmetic and copies ran while one was open for 0% of the time, Pallas kernels for 13%

profile of v1, /device:TPU:2, one launch (start us, length us, event | category | flops | bytes accessed | tf_op | source)
XLA Modules:
  0.0 109.7 jit_solution(478862549916512220)
XLA Ops:
  0.6 0.0 copy-start.5
  0.6 4.9 %prepare.1 = (bf16[16,256,128]{2,1,0:T(8,128)(2,1)}, bf16[1024,128]{1,0:T(8,128)(2,1)}, f32[1024,128]{1,0:T(8,128)}) custom-call(bf16[128,1024]{1,0:T(8,128)(2,1)} %q_ref.1, bf16[128,1024]{1,0:T(8,128)(2,1)} %k_ref.1, bf16[128,1024]{1,0:T(8,128)(2,1)} %v_ref.1, bf16[128,1024]{1,0:T(8,128)(2,1)} %u_ref.1, bf16[128,1024]{1,0:T(8,128)(2,1)} %c_ref.1, ...), custom_call_target="tpu_custom_call" | custom-call | tf_op jit(solution)/shard_map/prepare/pallas_call | solution.py:310
  5.6 7.5 %all-to-all-start = ((bf16[16,256,128]{2,1,0:T(8,128)(2,1)}), bf16[16,256,128]{2,1,0:T(8,128)(2,1)S(1)}, u32[]{:S(2)}, u32[]{:S(2)}) async-start(bf16[16,256,128]{2,1,0:T(8,128)(2,1)} %get-tuple-element.22), calls=%async_computation | async-start | bytes 2097152 | tf_op jit(solution)/shard_map/all_to_all | solution.py:374
  13.1 0.0 copy-done.5
  13.1 0.1 pad_add_fusion.place_ref
  13.1 15.0 %all-to-all-done.got_ref = bf16[16,256,128]{2,1,0:T(8,128)(2,1)S(1)} async-done(((bf16[16,256,128]{2,1,0:T(8,128)(2,1)}), bf16[16,256,128]{2,1,0:T(8,128)(2,1)S(1)}, u32[]{:S(2)}, u32[]{:S(2)}) %all-to-all-start) | async-done | bytes 1048608 | tf_op jit(solution)/shard_map/all_to_all | solution.py:374
  28.1 0.7 other_half.1
  28.8 0.0 copy-start
  28.8 0.1 collective-permute-start
  28.9 1.9 %collective-permute-done.other_ref = bf16[8,256,128]{2,1,0:T(8,128)(2,1)S(1)} collective-permute-done((bf16[8,256,128]{2,1,0:T(8,128)(2,1)S(1)}, bf16[8,256,128]{2,1,0:T(8,128)(2,1)S(1)}, u32[]{:S(2)}, u32[]{:S(2)}) %collective-permute-start) | collective-permute-done | bytes 524320 | tf_op jit(solution)/shard_map/ppermute | solution.py:371
  30.8 5.0 %attend_forward.1 = (bf16[256,2048]{1,0:T(8,128)(2,1)S(1)}, bf16[64,2048]{1,0:T(8,128)(2,1)S(1)}, bf16[8,64,128]{2,1,0:T(8,128)(2,1)S(1)}, bf16[8,64,128]{2,1,0:T(8,128)(2,1)S(1)}, bf16[80,128]{1,0:T(8,128)(2,1)S(1)}) custom-call(s32[5]{0:T(128)S(1)} %pad_add_fusion.place_ref, bf16[16,256,128]{2,1,0:T(8,128)(2,1)S(1)} %all-to-all-done.got_ref, ...), custom_call_target="tpu_custom_call" | custom-call | flops 1073741824 | bytes 2097152 | tf_op jit(solution)/shard_map/attend_forward/pallas_call | solution.py:292
  35.8 0.0 copy-start.3
  35.8 0.0 copy-start.2
  35.8 0.2 collective-permute-start.1
  36.0 1.2 %collective-permute-done.1.theirs_ref = bf16[8,64,128]{2,1,0:T(8,128)(2,1)S(1)} collective-permute-done((bf16[8,64,128]{2,1,0:T(8,128)(2,1)S(1)}, bf16[8,64,128]{2,1,0:T(8,128)(2,1)S(1)}, u32[]{:S(2)}, u32[]{:S(2)}) %collective-permute-start.1) | collective-permute-done | bytes 131104 | tf_op jit(solution)/shard_map/ppermute | solution.py:371
  37.2 1.5 %attn_to_owners.1 = bf16[16,144,128]{2,1,0:T(8,128)(2,1)} custom-call(s32[5]{0:T(128)S(1)} %pad_add_fusion.place_ref, bf16[8,64,128]{2,1,0:T(8,128)(2,1)S(1)} %get-tuple-element.25.mine_ref, bf16[8,64,128]{2,1,0:T(8,128)(2,1)S(1)} %collective-permute-done.1.theirs_ref, bf16[80,128]{1,0:T(8,128)(2,1)S(1)} %get-tuple-element.27.stat_ref), custom_call_target="tpu_custom_call" | custom-call | flops 67108864 | bytes 2097152 | tf_op jit(solution)/shard_map/attn_to_owners/pallas_call | solution.py:292
  38.7 6.1 %all-to-all-start.1 = ((bf16[16,144,128]{2,1,0:T(8,128)(2,1)}), bf16[16,144,128]{2,1,0:T(8,128)(2,1)S(1)}, u32[]{:S(2)}, u32[]{:S(2)}) async-start(bf16[16,144,128]{2,1,0:T(8,128)(2,1)} %attn_to_owners.1), calls=%async_computation.1 | async-start | bytes 1179648 | tf_op jit(solution)/shard_map/all_to_all | solution.py:374
  44.8 0.0 copy-done
  44.8 0.1 collective-permute-start.4
  44.9 10.4 %all-to-all-done.1.got_ref = bf16[16,144,128]{2,1,0:T(8,128)(2,1)S(1)} async-done(((bf16[16,144,128]{2,1,0:T(8,128)(2,1)}), bf16[16,144,128]{2,1,0:T(8,128)(2,1)S(1)}, u32[]{:S(2)}, u32[]{:S(2)}) %all-to-all-start.1) | async-done | bytes 589856 | tf_op jit(solution)/shard_map/all_to_all | solution.py:374
  55.3 0.0 copy-done.2
  55.3 1.0 gated.1
  56.3 0.1 collective-permute-start.3
  56.4 0.0 collective-permute-done.4.d_ref
  56.4 1.3 %collective-permute-done.3.b_ref = bf16[512,128]{1,0:T(8,128)(2,1)S(1)} collective-permute-done((bf16[512,128]{1,0:T(8,128)(2,1)S(1)}, bf16[512,128]{1,0:T(8,128)(2,1)S(1)}, u32[]{:S(2)}, u32[]{:S(2)}) %collective-permute-start.3) | collective-permute-done | bytes 131104 | tf_op jit(solution)/shard_map/ppermute | solution.py:371
  57.7 1.7 %product.1 = bf16[512,1024]{1,0:T(8,128)(2,1)} custom-call(bf16[512,128]{1,0:T(8,128)(2,1)S(1)} %get-tuple-element.34.a_ref, bf16[512,128]{1,0:T(8,128)(2,1)S(1)} %collective-permute-done.3.b_ref, bf16[128,1024]{1,0:T(8,128)(2,1)S(1)} %copy-done, bf16[128,1024]{1,0:T(8,128)(2,1)S(1)} %collective-permute-done.4.d_ref), custom_call_target="tpu_custom_call" | custom-call | flops 67108864 | bytes 2097152 | tf_op jit(solution)/shard_map/product/pallas_call | solution.py:292
  59.4 0.0 copy-done.3
  59.4 0.0 copy-start.4
  59.4 6.7 %all-to-all-start.3 = ((bf16[16,32,1024]{2,1,0:T(8,128)(2,1)}), bf16[16,32,1024]{2,1,0:T(8,128)(2,1)}, u32[]{:S(2)}, u32[]{:S(2)}) async-start(bf16[16,32,1024]{2,1,0:T(8,128)(2,1)} %bitcast.2), calls=%async_computation.3 | async-start | bytes 2097152 | tf_op jit(solution)/shard_map/all_to_all | solution.py:374
  66.1 0.0 copy-done.4
  66.1 0.0 copy-start.1
  66.1 8.8 %attend_backward.1 = (bf16[8,192,128]{2,1,0:T(8,128)(2,1)S(1)}, bf16[8,192,128]{2,1,0:T(8,128)(2,1)S(1)}) custom-call(s32[5]{0:T(128)S(1)} %pad_add_fusion.place_ref, bf16[256,2048]{1,0:T(8,128)(2,1)S(1)} %get-tuple-element.23.x_ref, bf16[64,2048]{1,0:T(8,128)(2,1)S(1)} %copy-done.4, bf16[16,144,128]{2,1,0:T(8,128)(2,1)S(1)} %all-to-all-done.1.got_ref), custom_call_target="tpu_custom_call" | custom-call | flops 8589934592 | bytes 2097152 | tf_op jit(solution)/shard_map/attend_backward/pallas_call | solution.py:292
  74.9 0.1 collective-permute-start.2
  75.1 1.7 %collective-permute-done.2.theirs_ref = bf16[8,192,128]{2,1,0:T(8,128)(2,1)S(1)} collective-permute-done((bf16[8,192,128]{2,1,0:T(8,128)(2,1)S(1)}, bf16[8,192,128]{2,1,0:T(8,128)(2,1)S(1)}, u32[]{:S(2)}, u32[]{:S(2)}) %collective-permute-start.2) | collective-permute-done | bytes 393248 | tf_op jit(solution)/shard_map/ppermute | solution.py:371
  76.7 1.6 %grads_to_owners.1.after_ref = bf16[16,192,128]{2,1,0:T(8,128)(2,1)} custom-call(s32[5]{0:T(128)S(1)} %pad_add_fusion.place_ref, bf16[8,192,128]{2,1,0:T(8,128)(2,1)S(1)} %get-tuple-element.28.mine_ref, bf16[8,192,128]{2,1,0:T(8,128)(2,1)S(1)} %collective-permute-done.2.theirs_ref), custom_call_target="tpu_custom_call" | custom-call | flops 67108864 | bytes 2097152 | tf_op jit(solution)/shard_map/grads_to_owners/pallas_call | solution.py:292
  78.3 0.0 copy-done.1
  78.3 1.3 %d_gate.1 = bf16[128,1024]{1,0:T(8,128)(2,1)} custom-call(bf16[16,144,128]{2,1,0:T(8,128)(2,1)S(1)} %all-to-all-done.1.got_ref, f32[1024,128]{1,0:T(8,128)S(1)} %copy-done.1, bf16[16,192,128]{2,1,0:T(8,128)(2,1)} %grads_to_owners.1.after_ref), custom_call_target="tpu_custom_call" | custom-call | flops 1048576 | bytes 2097152 | tf_op jit(solution)/shard_map/d_gate/pallas_call | solution.py:292
  79.6 2.4 %all-to-all-done.3 = bf16[16,32,1024]{2,1,0:T(8,128)(2,1)} async-done(((bf16[16,32,1024]{2,1,0:T(8,128)(2,1)}), bf16[16,32,1024]{2,1,0:T(8,128)(2,1)}, u32[]{:S(2)}, u32[]{:S(2)}) %all-to-all-start.3) | async-done | bytes 1048608 | tf_op jit(solution)/shard_map/all_to_all | solution.py:374
  82.0 1.4 %convert_reduce_fusion = f32[32,1024]{1,0:T(8,128)S(1)} fusion(bf16[16,32,1024]{2,1,0:T(8,128)(2,1)} %all-to-all-done.3), kind=kLoop, calls=%fused_computation | loop fusion | flops 1015808 | bytes 1179648 | tf_op jit(solution)/shard_map/reduce_sum | solution.py:427
  83.5 7.3 %collective-permute-start.5 = (f32[4,4,1024]{2,1,0:T(4,128)S(1)}, f32[4,4,1024]{2,1,0:T(4,128)S(1)}, u32[]{:S(2)}, u32[]{:S(2)}) collective-permute-start(f32[4,4,1024]{2,1,0:T(4,128)S(1)} %dynamic-slice_bitcast_fusion), channel_id=1, source_target_pairs={{0,128},{32,160},{64,192},{96,224},{128,0},{160,32},{192,64},{224,... | collective-permute-start | bytes 196616 | tf_op jit(solution)/shard_map/ppermute | solution.py:434
  90.7 6.2 %all-to-all-start.2 = ((bf16[16,192,128]{2,1,0:T(8,128)(2,1)}), bf16[16,192,128]{2,1,0:T(8,128)(2,1)S(1)}, u32[]{:S(2)}, u32[]{:S(2)}) async-start(bf16[16,192,128]{2,1,0:T(8,128)(2,1)} %grads_to_owners.1.after_ref), calls=%async_computation.2 | async-start | bytes 1572864 | tf_op jit(solution)/shard_map/all_to_all | solution.py:374
  96.9 0.0 collective-permute-done.5
  97.0 1.6 %collective-permute-start.6 = (f32[2,4,1024]{2,1,0:T(4,128)S(1)}, f32[2,4,1024]{2,1,0:T(4,128)S(1)}, u32[]{:S(2)}, u32[]{:S(2)}) collective-permute-start(f32[2,4,1024]{2,1,0:T(4,128)S(1)} %dynamic-slice_bitcast_fusion.1), channel_id=1, source_target_pairs={{0,64},{32,96},{64,0},{96,32},{128,192},{160,224},{192,128},{224,1... | collective-permute-start | bytes 98312 | tf_op jit(solution)/shard_map/ppermute | solution.py:434
  98.5 3.4 %collective-permute-done.6 = f32[2,4,1024]{2,1,0:T(4,128)S(1)} collective-permute-done((f32[2,4,1024]{2,1,0:T(4,128)S(1)}, f32[2,4,1024]{2,1,0:T(4,128)S(1)}, u32[]{:S(2)}, u32[]{:S(2)}) %collective-permute-start.6) | collective-permute-done | bytes 32800 | tf_op jit(solution)/shard_map/ppermute | solution.py:434
  101.9 1.1 collective-permute-start.7
  103.0 4.9 %all-to-all-done.2.got_ref = bf16[16,192,128]{2,1,0:T(8,128)(2,1)S(1)} async-done(((bf16[16,192,128]{2,1,0:T(8,128)(2,1)}), bf16[16,192,128]{2,1,0:T(8,128)(2,1)S(1)}, u32[]{:S(2)}, u32[]{:S(2)}) %all-to-all-start.2) | async-done | bytes 786464 | tf_op jit(solution)/shard_map/all_to_all | solution.py:374
  107.9 1.1 %finish.1 = (bf16[128,1024]{1,0:T(8,128)(2,1)}, bf16[128,1024]{1,0:T(8,128)(2,1)}, bf16[128,1024]{1,0:T(8,128)(2,1)}) custom-call(bf16[16,192,128]{2,1,0:T(8,128)(2,1)S(1)} %all-to-all-done.2.got_ref), custom_call_target="tpu_custom_call" | custom-call | flops 67108864 | bytes 2097152 | tf_op jit(solution)/shard_map/finish/pallas_call | solution.py:292
  109.1 0.0 collective-permute-done.7
  109.1 0.6 multiply_bitcast_fusion
  (6 shorter events, 0.1 us)
Async XLA Ops:
  0.6 12.4 %copy-start.5 = (s32[1,4]{1,0:T(1,128)S(1)}, s32[1,4]{1,0:T(1,128)}, u32[]{:S(2)}) copy-start(s32[1,4]{1,0:T(1,128)} %param.13) | copy-start | bytes 52
  5.6 22.5 %all-to-all-start = ((bf16[16,256,128]{2,1,0:T(8,128)(2,1)}), bf16[16,256,128]{2,1,0:T(8,128)(2,1)S(1)}, u32[]{:S(2)}, u32[]{:S(2)}) async-start(bf16[16,256,128]{2,1,0:T(8,128)(2,1)} %get-tuple-element.22), calls=%async_computation | async-start | bytes 2097152 | tf_op jit(solution)/shard_map/all_to_all | solution.py:374
  28.8 16.0 %copy-start = (bf16[128,1024]{1,0:T(8,128)(2,1)S(1)}, bf16[128,1024]{1,0:T(8,128)(2,1)}, u32[]{:S(2)}) copy-start(bf16[128,1024]{1,0:T(8,128)(2,1)} %c_ref.1) | copy-start | bytes 786436
  28.8 2.0 %collective-permute-start = (bf16[8,256,128]{2,1,0:T(8,128)(2,1)S(1)}, bf16[8,256,128]{2,1,0:T(8,128)(2,1)S(1)}, u32[]{:S(2)}, u32[]{:S(2)}) collective-permute-start(bf16[8,256,128]{2,1,0:T(8,128)(2,1)S(1)} %other_half.1), channel_id=1, source_target_pairs={{0,1},{1,0},{2,3},{3,2},{4,5},{5,4},{6,7},{7,6},{8,9},{9,8},{10,11... | collective-permute-start | bytes 1572872 | tf_op jit(solution)/shard_map/ppermute | solution.py:371
  35.8 23.6 %copy-start.3 = (bf16[64,2048]{1,0:T(8,128)(2,1)}, bf16[64,2048]{1,0:T(8,128)(2,1)S(1)}, u32[]{:S(2)}) copy-start(bf16[64,2048]{1,0:T(8,128)(2,1)S(1)} %get-tuple-element.24.attn_ref) | copy-start | bytes 786436
  35.8 19.6 %copy-start.2 = (bf16[1024,128]{1,0:T(8,128)(2,1)S(1)}, bf16[1024,128]{1,0:T(8,128)(2,1)}, u32[]{:S(2)}) copy-start(bf16[1024,128]{1,0:T(8,128)(2,1)} %get-tuple-element.33.ut_ref) | copy-start | bytes 786436
  35.8 1.4 %collective-permute-start.1 = (bf16[8,64,128]{2,1,0:T(8,128)(2,1)S(1)}, bf16[8,64,128]{2,1,0:T(8,128)(2,1)S(1)}, u32[]{:S(2)}, u32[]{:S(2)}) collective-permute-start(bf16[8,64,128]{2,1,0:T(8,128)(2,1)S(1)} %get-tuple-element.26), channel_id=1, source_target_pairs={{0,1},{1,0},{2,3},{3,2},{4,5},{5,4},{6,7},{7,6},{8,9},{9,8},{10,11... | collective-permute-start | bytes 393224 | tf_op jit(solution)/shard_map/ppermute | solution.py:371
  38.7 16.6 %all-to-all-start.1 = ((bf16[16,144,128]{2,1,0:T(8,128)(2,1)}), bf16[16,144,128]{2,1,0:T(8,128)(2,1)S(1)}, u32[]{:S(2)}, u32[]{:S(2)}) async-start(bf16[16,144,128]{2,1,0:T(8,128)(2,1)} %attn_to_owners.1), calls=%async_computation.1 | async-start | bytes 1179648 | tf_op jit(solution)/shard_map/all_to_all | solution.py:374
  44.8 11.6 %collective-permute-start.4 = (bf16[128,1024]{1,0:T(8,128)(2,1)S(1)}, bf16[128,1024]{1,0:T(8,128)(2,1)S(1)}, u32[]{:S(2)}, u32[]{:S(2)}) collective-permute-start(bf16[128,1024]{1,0:T(8,128)(2,1)S(1)} %copy-done), channel_id=1, source_target_pairs={{0,1},{1,0},{2,3},{3,2},{4,5},{5,4},{6,7},{7,6},{8,9},{9,8},{10,11... | collective-permute-start | bytes 786440 | tf_op jit(solution)/shard_map/ppermute | solution.py:371
  56.3 1.4 %collective-permute-start.3 = (bf16[512,128]{1,0:T(8,128)(2,1)S(1)}, bf16[512,128]{1,0:T(8,128)(2,1)S(1)}, u32[]{:S(2)}, u32[]{:S(2)}) collective-permute-start(bf16[512,128]{1,0:T(8,128)(2,1)S(1)} %get-tuple-element.35), channel_id=1, source_target_pairs={{0,1},{1,0},{2,3},{3,2},{4,5},{5,4},{6,7},{7,6},{8,9},{9,8},{10,11... | collective-permute-start | bytes 393224 | tf_op jit(solution)/shard_map/ppermute | solution.py:371
  59.4 6.7 %copy-start.4 = (bf16[64,2048]{1,0:T(8,128)(2,1)S(1)}, bf16[64,2048]{1,0:T(8,128)(2,1)}, u32[]{:S(2)}) copy-start(bf16[64,2048]{1,0:T(8,128)(2,1)} %copy-done.3) | copy-start | bytes 786436
  59.4 22.6 %all-to-all-start.3 = ((bf16[16,32,1024]{2,1,0:T(8,128)(2,1)}), bf16[16,32,1024]{2,1,0:T(8,128)(2,1)}, u32[]{:S(2)}, u32[]{:S(2)}) async-start(bf16[16,32,1024]{2,1,0:T(8,128)(2,1)} %bitcast.2), calls=%async_computation.3 | async-start | bytes 2097152 | tf_op jit(solution)/shard_map/all_to_all | solution.py:374
  66.1 12.2 %copy-start.1 = (f32[1024,128]{1,0:T(8,128)S(1)}, f32[1024,128]{1,0:T(8,128)}, u32[]{:S(2)}) copy-start(f32[1024,128]{1,0:T(8,128)} %get-tuple-element.36.dg_ref) | copy-start | bytes 1572868
  74.9 1.8 %collective-permute-start.2 = (bf16[8,192,128]{2,1,0:T(8,128)(2,1)S(1)}, bf16[8,192,128]{2,1,0:T(8,128)(2,1)S(1)}, u32[]{:S(2)}, u32[]{:S(2)}) collective-permute-start(bf16[8,192,128]{2,1,0:T(8,128)(2,1)S(1)} %get-tuple-element.29), channel_id=1, source_target_pairs={{0,1},{1,0},{2,3},{3,2},{4,5},{5,4},{6,7},{7,6},{8,9},{9,8},{10,11... | collective-permute-start | bytes 1179656 | tf_op jit(solution)/shard_map/ppermute | solution.py:371
  83.5 13.4 %collective-permute-start.5 = (f32[4,4,1024]{2,1,0:T(4,128)S(1)}, f32[4,4,1024]{2,1,0:T(4,128)S(1)}, u32[]{:S(2)}, u32[]{:S(2)}) collective-permute-start(f32[4,4,1024]{2,1,0:T(4,128)S(1)} %dynamic-slice_bitcast_fusion), channel_id=1, source_target_pairs={{0,128},{32,160},{64,192},{96,224},{128,0},{160,32},{192,64},{224,... | collective-permute-start | bytes 196616 | tf_op jit(solution)/shard_map/ppermute | solution.py:434
  90.7 17.2 %all-to-all-start.2 = ((bf16[16,192,128]{2,1,0:T(8,128)(2,1)}), bf16[16,192,128]{2,1,0:T(8,128)(2,1)S(1)}, u32[]{:S(2)}, u32[]{:S(2)}) async-start(bf16[16,192,128]{2,1,0:T(8,128)(2,1)} %grads_to_owners.1.after_ref), calls=%async_computation.2 | async-start | bytes 1572864 | tf_op jit(solution)/shard_map/all_to_all | solution.py:374
  97.0 4.9 %collective-permute-start.6 = (f32[2,4,1024]{2,1,0:T(4,128)S(1)}, f32[2,4,1024]{2,1,0:T(4,128)S(1)}, u32[]{:S(2)}, u32[]{:S(2)}) collective-permute-start(f32[2,4,1024]{2,1,0:T(4,128)S(1)} %dynamic-slice_bitcast_fusion.1), channel_id=1, source_target_pairs={{0,64},{32,96},{64,0},{96,32},{128,192},{160,224},{192,128},{224,1... | collective-permute-start | bytes 98312 | tf_op jit(solution)/shard_map/ppermute | solution.py:434
  101.9 7.1 %collective-permute-start.7 = (f32[1,4,1024]{2,1,0:T(4,128)S(1)}, f32[1,4,1024]{2,1,0:T(4,128)S(1)}, u32[]{:S(2)}, u32[]{:S(2)}) collective-permute-start(f32[1,4,1024]{2,1,0:T(4,128)S(1)} %constant_dynamic-slice_fusion), channel_id=1, source_target_pairs={{0,32},{32,0},{64,96},{96,64},{128,160},{160,128},{192,224},{224,1... | collective-permute-start | bytes 49160 | tf_op jit(solution)/shard_map/ppermute | solution.py:434

commit v2 on v1

--- a/solution.py
+++ b/solution.py
@@ -29,12 +29,6 @@
 
 def dot_nt(a, b):
     return lax.dot_general(a, b, (((1,), (1,)), ((), ())), preferred_element_type=F32)
-
-
-def turned(x):
-    n = x.shape[1]
-    row, col = (lax.broadcasted_iota(jnp.int32, (n, n), i) for i in range(2))
-    return dot_nt(jnp.where(row == col, 1.0, 0.0).astype(BF16), x).astype(BF16)
 
 
 def sigmoid(s):
@@ -144,9 +138,28 @@
         theirs_ref[j] = jnp.where(core == 0, pair[1], pair[0])
 
 
+PAIRS = [(q, k) for q in range(HALF // SUB) for k in range(q + 1)]
+AT = {pair: i for i, pair in enumerate(PAIRS)}
+
+
+def derive_kernel(place_ref, x_ref, silu_ref, slope_ref, qn_ref, kn_ref, vn_ref):
+    end1, end2 = place_of(place_ref)[3:]
+    for b in range(N_BLOCKS):
+        cols = slice(b * BLOCK, (b + 1) * BLOCK)
+        for i, out_ref in enumerate((qn_ref, kn_ref, vn_ref)):
+            out_ref[cols, :] = x_ref[i * 64 : (i + 1) * 64, cols].T
+    for q, k in PAIRS:
+        q_cols, k_cols = slice(q * SUB, (q + 1) * SUB), slice(k * SUB, (k + 1) * SUB)
+        s = dot(kn_ref[k_cols, :], x_ref[0:64, q_cols])
+        sigma = jnp.where(live_of(q * SUB, k * SUB, end1, end2, q == k), sigmoid(s), 0.0)
+        silu = s * sigma
+        silu_ref[AT[q, k]] = silu.astype(BF16)
+        slope_ref[AT[q, k]] = (sigma + silu * (1.0 - sigma)).astype(BF16)
+
+
 def backward_kernel(
-    place_ref, x_ref, attn_ref, got_ref, mine_ref, theirs_ref,
-    qn_ref, kn_ref, vn_ref, dn_ref, dt_ref, dq_ref, dk_ref, dv_ref, slot_ref,
+    place_ref, x_ref, attn_ref, got_ref, silu_ref, slope_ref, qn_ref, kn_ref, vn_ref, mine_ref, theirs_ref,
+    dn_ref, dt_ref, dq_ref, dk_ref, dv_ref, slot_ref,
 ):
     core, _, turn, end1, end2 = place_of(place_ref)
     stat = got_ref[:, 64 : 64 + STATS * N_BLOCKS, :].astype(F32).reshape(HEADS, STATS, N_BLOCKS, BLOCK)
@@ -160,46 +173,40 @@
     both = jnp.sum(stat[:, 2] + off * g_sum, axis=0) * rstd * (1.0 / WIDTH)
     for b in range(N_BLOCKS):
         cols = slice(b * BLOCK, (b + 1) * BLOCK)
-        here = x_ref[:, cols]
         r = rstd[b : b + 1]
         normed = (attn_ref[:, cols].astype(F32) - mean[b : b + 1]) * r
-        d = (r * (here[192:256].astype(F32) - g_mean[b : b + 1] - normed * both[b : b + 1])).astype(BF16)
+        d = (r * (x_ref[192:256, cols].astype(F32) - g_mean[b : b + 1] - normed * both[b : b + 1])).astype(BF16)
         dt_ref[:, cols] = d
         dn_ref[cols, :] = d.T
-        qn_ref[cols, :] = here[0:64].T
-        kn_ref[cols, :] = here[64:128].T
-        vn_ref[cols, :] = here[128:192].T
 
     for q_at, k_at, subs in below(HALF // B_TILE, B_TILE):
+        n = B_TILE // SUB
+        q_first, k_first = q_at // SUB, k_at // SUB
         made = {}
         for q, k in subs:
             q_cols = slice(q_at + q * SUB, q_at + (q + 1) * SUB)
             k_cols = slice(k_at + k * SUB, k_at + (k + 1) * SUB)
-            s = dot(kn_ref[k_cols, :], x_ref[0:64, q_cols])
             d_p = dot(vn_ref[k_cols, :], dt_ref[:, q_cols])
-            live = live_of(q_cols.start, k_cols.start, end1, end2, q_cols.start == k_cols.start)
-            sigma = jnp.where(live, sigmoid(s), 0.0)
-            silu = s * sigma
-            made[q, k] = silu.astype(BF16), (d_p * (sigma + silu * (1.0 - sigma))).astype(BF16)
-        for k in range(B_TILE // SUB):
+            made[q, k] = (d_p * slope_ref[AT[q_first + q, k_first + k]].astype(F32)).astype(BF16)
+        for k in range(n):
             k_cols = slice(k_at + k * SUB, k_at + (k + 1) * SUB)
             d_v, d_k = [], []
-            for q in range(B_TILE // SUB):
+            for q in range(n):
                 if (q, k) in made:
                     q_cols = slice(q_at + q * SUB, q_at + (q + 1) * SUB)
-                    d_v.append(dot(made[q, k][0], dn_ref[q_cols, :]))
-                    d_k.append(dot(made[q, k][1], qn_ref[q_cols, :]))
+                    d_v.append(dot(silu_ref[AT[q_first + q, k_first + k]], dn_ref[q_cols, :]))
+                    d_k.append(dot(made[q, k], qn_ref[q_cols, :]))
             if q_at == k_at:
                 dv_ref[k_cols, :], dk_ref[k_cols, :] = sum(d_v), sum(d_k)
             else:
                 dv_ref[k_cols, :] += sum(d_v)
                 dk_ref[k_cols, :] += sum(d_k)
-        for q in range(B_TILE // SUB):
+        for q in range(n):
             q_cols = slice(q_at + q * SUB, q_at + (q + 1) * SUB)
             d_q = []
-            for k in range(B_TILE // SUB):
+            for k in range(n):
                 if (q, k) in made:
-                    d_q.append(dot(x_ref[64:128, k_at + k * SUB : k_at + (k + 1) * SUB], made[q, k][1]))
+                    d_q.append(dot(x_ref[64:128, k_at + k * SUB : k_at + (k + 1) * SUB], made[q, k]))
             if k_at == 0:
                 dq_ref[:, q_cols] = sum(d_q)
             else:
@@ -213,14 +220,16 @@
 
 
 def prepare_kernel(q_ref, k_ref, v_ref, u_ref, cot_ref, w_ref, send_ref, ut_ref, dg_ref):
-    d_gated = dot_nt(w_ref[...], cot_ref[...])
-    u_t = turned(u_ref[...])
-    dg_ref[...] = d_gated
-    ut_ref[...] = u_t
-    g_t = (d_gated * u_t.astype(F32)).astype(BF16)
-    for i, rows in enumerate((turned(q_ref[...]), turned(k_ref[...]), turned(v_ref[...]), g_t)):
-        for h in range(4):
-            send_ref[h, i * 64 : (i + 1) * 64, :] = rows[h * 64 : (h + 1) * 64]
+    for at in range(0, WIDTH, 256):
+        cols = slice(at, at + 256)
+        d_gated = dot_nt(w_ref[cols, :], cot_ref[...])
+        u_t = u_ref[:, cols].T
+        dg_ref[cols, :] = d_gated
+        ut_ref[cols, :] = u_t
+        g_t = (d_gated * u_t.astype(F32)).astype(BF16)
+        for i, rows in enumerate((q_ref[:, cols].T, k_ref[:, cols].T, v_ref[:, cols].T, g_t)):
+            for h in range(4):
+                send_ref[at // 64 + h, i * 64 : (i + 1) * 64, :] = rows[h * 64 : (h + 1) * 64]
 
 
 def other_half_kernel(place_ref, got_ref, out_ref):
@@ -268,7 +277,7 @@
 def d_gate_kernel(got_ref, dg_ref, after_ref, out_ref):
     d_gate = (dg_ref[...] * normalised(got_ref)).astype(BF16)
     for i in range(WIDTH // BLOCK):
-        out_ref[:, i * BLOCK : (i + 1) * BLOCK] = turned(d_gate[i * BLOCK : (i + 1) * BLOCK])
+        out_ref[:, i * BLOCK : (i + 1) * BLOCK] = d_gate[i * BLOCK : (i + 1) * BLOCK].T
 
 
 def product_kernel(a_ref, b_ref, c_ref, d_ref, out_ref):
@@ -281,7 +290,7 @@
     for i, out_ref in enumerate((dq_ref, dk_ref, dv_ref)):
         for h in range(0, HEADS, 4):
             heads = got_ref[h : h + 4, i * 64 : (i + 1) * 64, :].reshape(256, BLOCK)
-            out_ref[:, h * 64 : (h + 4) * 64] = turned(heads)
+            out_ref[:, h * 64 : (h + 4) * 64] = heads.T
 
 
 SMEM = pl.BlockSpec(memory_space=pltpu.SMEM)
@@ -305,21 +314,9 @@
     return jax.ShapeDtypeStruct(dims, dtype)
 
 
-def prepare(query, key, value, gate_u, cotangent, out_weight):
-    cols = pl.BlockSpec((BLOCK, 256), lambda i: (0, i))
-    return pl.pallas_call(
-        prepare_kernel,
-        grid=(4,),
-        out_shape=(shape((HEADS, 256, BLOCK)), shape((WIDTH, BLOCK)), shape((WIDTH, BLOCK), F32)),
-        in_specs=[cols] * 4
-        + [pl.BlockSpec((BLOCK, WIDTH), lambda i: (0, 0)), pl.BlockSpec((256, WIDTH), lambda i: (i, 0))],
-        out_specs=(
-            pl.BlockSpec((4, 256, BLOCK), lambda i: (i, 0, 0)),
-            pl.BlockSpec((256, BLOCK), lambda i: (i, 0)),
-            pl.BlockSpec((256, BLOCK), lambda i: (i, 0)),
-        ),
-        name="prepare",
-    )(query, key, value, gate_u, cotangent, out_weight)
+def prepare(*args):
+    shapes = shape((HEADS, 256, BLOCK)), shape((WIDTH, BLOCK)), shape((WIDTH, BLOCK), F32)
+    return call(prepare_kernel, "prepare", shapes, [VMEM] * 6, args, mib=12)
 
 
 def attend_forward(place, got, other):
@@ -346,20 +343,37 @@
     )
 
 
-def attend_backward(place, x, attn, got):
+def derive(place, x):
+    tiles = shape((len(PAIRS), SUB, SUB))
+    return call(
+        derive_kernel,
+        "derive",
+        (tiles, tiles) + (shape((HALF, HEAD_DIM)),) * 3,
+        [SMEM, VMEM],
+        (place, x),
+        mib=16,
+        flops=1 << 31,
+        transcendentals=1 << 22,
+    )
+
+
+def attend_backward(place, x, attn, got, derived):
     return call(
         backward_kernel,
         "attend_backward",
         (shape((8, 192, BLOCK)), shape((8, 192, BLOCK))),
-        [SMEM, VMEM, VMEM, VMEM],
-        (place, x, attn, got),
-        [pltpu.VMEM((HALF, HEAD_DIM), BF16)] * 4
-        + [pltpu.VMEM((HEAD_DIM, HALF), BF16), pltpu.VMEM((HEAD_DIM, HALF), F32)]
-        + [pltpu.VMEM((HALF, HEAD_DIM), F32)] * 2
-        + [pltpu.VMEM((N_BLOCKS, 192, BLOCK), F32)],
-        mib=24,
+        [SMEM] + [VMEM] * 8,
+        (place, x, attn, got) + derived,
+        [
+            pltpu.VMEM((HALF, HEAD_DIM), BF16),
+            pltpu.VMEM((HEAD_DIM, HALF), BF16),
+            pltpu.VMEM((HEAD_DIM, HALF), F32),
+            pltpu.VMEM((HALF, HEAD_DIM), F32),
+            pltpu.VMEM((HALF, HEAD_DIM), F32),
+            pltpu.VMEM((N_BLOCKS, 192, BLOCK), F32),
+        ],
+        mib=20,
         flops=1 << 33,
-        transcendentals=1 << 24,
     )
 
 
@@ -387,6 +401,7 @@
         (place, mine, swap(theirs), stat),
     )
     got_attn = chips(send)
+    derived = derive(place, x)
 
     mine, theirs = call(
         gated_kernel,
@@ -405,7 +420,7 @@
     )
     parts = chips(part.reshape(HEADS, 32, WIDTH))
 
-    mine, theirs = attend_backward(place, x, attn, got_attn)
+    mine, theirs = attend_backward(place, x, attn, got_attn, derived)
     send = call(
         to_owners_kernel,
         "grads_to_owners",
@@ -424,15 +439,19 @@
     )
 
     parts, d_gate = lax.optimization_barrier((parts, d_gate))
-    part = jnp.sum(parts.astype(F32), axis=0).reshape(8, 4, WIDTH)
+    part = jnp.sum(parts.astype(F32), axis=0).reshape(4, 2, 4, WIDTH)
     z = lax.axis_index("dp")
-    for step in (4, 2, 1):
-        high = (z // step) % 2
-        halves = part.reshape(2, step, 4, WIDTH)
-        away = lax.dynamic_index_in_dim(halves, 1 - high, 0, keepdims=False)
-        kept = lax.dynamic_index_in_dim(halves, high, 0, keepdims=False)
-        part = kept + lax.ppermute(away, "dp", [(i, i ^ step) for i in range(8)])
-    d_weight = part.reshape(4, WIDTH) * (1.0 / math.sqrt(32768))
+
+    def exchange(x, step):
+        return lax.ppermute(x, "dp", [(i, i ^ step) for i in range(8)])
+
+    away = lax.dynamic_index_in_dim(part, 1 - z % 2, 1, keepdims=False)
+    part = lax.dynamic_index_in_dim(part, z % 2, 1, keepdims=False) + exchange(away, 1)
+    d_weight = lax.dynamic_index_in_dim(part, z // 2, 0, keepdims=False)
+    for step in (1, 2, 3):
+        away = lax.dynamic_index_in_dim(part, (z // 2) ^ step, 0, keepdims=False)
+        d_weight = d_weight + exchange(away, 2 * step)
+    d_weight = d_weight * (1.0 / math.sqrt(32768))
 
     d_query, d_key, d_value = call(finish_kernel, "finish", (shape((BLOCK, WIDTH)),) * 3, [VMEM], (got,))
     return d_query, d_key, d_value, d_gate, d_weight

time: 111 us -> 125 us (1.13)
  local copies, waits for them, and re-layouts: 0.11 us -> 18.5 us
  waiting for transfers between devices: 42.2 us -> 37.2 us
  starting transfers between devices: 36.9 us -> 39.1 us
  Pallas kernels: 27.5 us -> 25.9 us
    unnamed x12 -> x36, local copies, waits for them, and re-layouts: 0.03 us -> 18.5 us
    all_to_all x4, waiting for transfers between devices: 32.7 us -> 25.4 us  [chips(): return lax.all_to_all(x, CHIP, 0, 0, tiled=True)]
    pallas_call x1 -> x0, Pallas kernels: 4.94 us -> none  [prepare(): pl.pallas_call(prepare_kernel, grid=(4,), out_shape=(shape((HEADS, 256, B...]
    ppermute x3 -> x4, waiting for transfers between devices: 3.37 us -> 7.21 us  [exchange(): return lax.ppermute(x, 'dp', [(i, i ^ step) for i in range(8)])]
    pallas_call x9 -> x11, Pallas kernels: 22.5 us -> 25.9 us  [call(): pl.pallas_call(kernel, out_shape=out_shape, in_specs=in_specs, out_specs=...]
    ppermute x5, waiting for transfers between devices: 6.11 us -> 4.63 us  [swap(): return lax.ppermute(x, 'core', SWAP)]
    ppermute x3 -> x4, starting transfers between devices: 9.92 us -> 10.7 us  [exchange(): return lax.ppermute(x, 'dp', [(i, i ^ step) for i in range(8)])]
  transfers between devices with their start and end apart: 12 -> 13, of which waited for: 9 -> 8; matrix products, arithmetic and copies ran while one was open for 0% -> 1% of each run, Pallas kernels for 13% -> 13%
where the time goes in v2:
time: 125 us; the launch traced here: 124 us
  starting transfers between devices  39.1 us (31%)
  waiting for transfers between devices  37.2 us (30%)
  Pallas kernels  25.9 us (21%)
  local copies, waits for them, and re-layouts  18.5 us (15%)
  other arithmetic  2.14 us (2%)
    all_to_all x4, starting transfers between devices, chips(): return lax.all_to_all(x, CHIP, 0, 0, tiled=True)  27.4 us
    pallas_call x11, Pallas kernels, call(): pl.pallas_call(kernel, out_shape=out_shape, in_specs=in_specs, out_specs=...  25.9 us
    all_to_all x4, waiting for transfers between devices, chips(): return lax.all_to_all(x, CHIP, 0, 0, tiled=True)  25.4 us
    unnamed x36, local copies, waits for them, and re-layouts  18.5 us
    ppermute x4, starting transfers between devices, exchange(): return lax.ppermute(x, 'dp', [(i, i ^ step) for i in range(8)])  10.7 us
    ppermute x4, waiting for transfers between devices, exchange(): return lax.ppermute(x, 'dp', [(i, i ^ step) for i in range(8)])  7.21 us
    ppermute x5, waiting for transfers between devices, swap(): return lax.ppermute(x, 'core', SWAP)  4.63 us
  transfers between devices with their start and end apart: 13, of which 8 were waited for; matrix products, arithmetic and copies ran while one was open for 1% of the time, Pallas kernels for 13%

profile of v2, /device:TPU:2, one launch (start us, length us, event | category | flops | bytes accessed | tf_op | source)
XLA Modules:
  0.0 123.7 jit_solution(4699642200504496684)
XLA Ops:
  0.6 0.0 copy-start
  0.6 1.6 %copy-done = bf16[1024,1024]{1,0:T(8,128)(2,1)S(1)} copy-done((bf16[1024,1024]{1,0:T(8,128)(2,1)S(1)}, bf16[1024,1024]{1,0:T(8,128)(2,1)}, u32[]{:S(2)}) %copy-start) | copy-done | bytes 2097176
  2.2 0.0 copy-start.1
  2.2 0.9 copy-done.1
  3.2 0.0 copy-start.3
  3.2 0.9 copy-done.3
  4.1 0.0 copy-start.4
  4.1 0.9 copy-done.4
  5.1 0.9 copy-done.5
  6.0 0.9 copy-done.6
  7.0 1.7 %prepare.1 = (bf16[16,256,128]{2,1,0:T(8,128)(2,1)}, bf16[1024,128]{1,0:T(8,128)(2,1)S(1)}, f32[1024,128]{1,0:T(8,128)S(1)}) custom-call(bf16[128,1024]{1,0:T(8,128)(2,1)S(1)} %copy-done.3, bf16[128,1024]{1,0:T(8,128)(2,1)S(1)} %copy-done.4, bf16[128,1024]{1,0:T(8,128)(2,1)S(1)} %copy-done.5, bf16[128,1024]{1,0:T(8,128)(2,1)S(1)} %copy-done.6, ...), custom_call_target="tpu_custom_call" | custom-call | flops 67108864 | bytes 2097152 | tf_op jit(solution)/shard_map/prepare/pallas_call | solution.py:301
  8.7 7.5 %all-to-all-start = ((bf16[16,256,128]{2,1,0:T(8,128)(2,1)}), bf16[16,256,128]{2,1,0:T(8,128)(2,1)S(1)}, u32[]{:S(2)}, u32[]{:S(2)}) async-start(bf16[16,256,128]{2,1,0:T(8,128)(2,1)} %get-tuple-element.27), calls=%async_computation | async-start | bytes 2097152 | tf_op jit(solution)/shard_map/all_to_all | solution.py:388
  16.1 0.0 copy-done.17
  16.2 0.1 pad_add_fusion.place_ref
  16.2 15.0 %all-to-all-done.got_ref = bf16[16,256,128]{2,1,0:T(8,128)(2,1)S(1)} async-done(((bf16[16,256,128]{2,1,0:T(8,128)(2,1)}), bf16[16,256,128]{2,1,0:T(8,128)(2,1)S(1)}, u32[]{:S(2)}, u32[]{:S(2)}) %all-to-all-start) | async-done | bytes 1048608 | tf_op jit(solution)/shard_map/all_to_all | solution.py:388
  31.2 0.7 other_half.1
  31.9 0.0 copy-start.2
  31.9 0.1 collective-permute-start
  32.0 1.9 %collective-permute-done.other_ref = bf16[8,256,128]{2,1,0:T(8,128)(2,1)S(1)} collective-permute-done((bf16[8,256,128]{2,1,0:T(8,128)(2,1)S(1)}, bf16[8,256,128]{2,1,0:T(8,128)(2,1)S(1)}, u32[]{:S(2)}, u32[]{:S(2)}) %collective-permute-start) | collective-permute-done | bytes 524320 | tf_op jit(solution)/shard_map/ppermute | solution.py:385
  33.9 4.9 %attend_forward.1 = (bf16[256,2048]{1,0:T(8,128)(2,1)S(1)}, bf16[64,2048]{1,0:T(8,128)(2,1)S(1)}, bf16[8,64,128]{2,1,0:T(8,128)(2,1)S(1)}, bf16[8,64,128]{2,1,0:T(8,128)(2,1)S(1)}, bf16[80,128]{1,0:T(8,128)(2,1)S(1)}) custom-call(s32[5]{0:T(128)S(1)} %pad_add_fusion.place_ref, bf16[16,256,128]{2,1,0:T(8,128)(2,1)S(1)} %all-to-all-done.got_ref, ...), custom_call_target="tpu_custom_call" | custom-call | flops 1073741824 | bytes 2097152 | tf_op jit(solution)/shard_map/attend_forward/pallas_call | solution.py:301
  38.8 0.2 collective-permute-start.1
  39.0 1.2 collective-permute-done.1.theirs_ref
  40.2 1.5 %attn_to_owners.1 = bf16[16,144,128]{2,1,0:T(8,128)(2,1)} custom-call(s32[5]{0:T(128)S(1)} %pad_add_fusion.place_ref, bf16[8,64,128]{2,1,0:T(8,128)(2,1)S(1)} %get-tuple-element.30.mine_ref, bf16[8,64,128]{2,1,0:T(8,128)(2,1)S(1)} %collective-permute-done.1.theirs_ref, bf16[80,128]{1,0:T(8,128)(2,1)S(1)} %get-tuple-element.32.stat_ref), custom_call_target="tpu_custom_call" | custom-call | flops 67108864 | bytes 2097152 | tf_op jit(solution)/shard_map/attn_to_owners/pallas_call | solution.py:301
  41.7 6.1 %all-to-all-start.1 = ((bf16[16,144,128]{2,1,0:T(8,128)(2,1)}), bf16[16,144,128]{2,1,0:T(8,128)(2,1)S(1)}, u32[]{:S(2)}, u32[]{:S(2)}) async-start(bf16[16,144,128]{2,1,0:T(8,128)(2,1)} %attn_to_owners.1), calls=%async_computation.1 | async-start | bytes 1179648 | tf_op jit(solution)/shard_map/all_to_all | solution.py:388
  47.8 0.0 copy-done.2
  47.8 0.1 collective-permute-start.4
  47.9 10.4 %all-to-all-done.1.got_ref = bf16[16,144,128]{2,1,0:T(8,128)(2,1)S(1)} async-done(((bf16[16,144,128]{2,1,0:T(8,128)(2,1)}), bf16[16,144,128]{2,1,0:T(8,128)(2,1)S(1)}, u32[]{:S(2)}, u32[]{:S(2)}) %all-to-all-start.1) | async-done | bytes 589856 | tf_op jit(solution)/shard_map/all_to_all | solution.py:388
  58.3 1.0 gated.1
  59.3 0.3 collective-permute-start.3
  59.5 4.9 %derive.1 = (bf16[36,256,256]{2,1,0:T(8,128)(2,1)S(1)}, bf16[36,256,256]{2,1,0:T(8,128)(2,1)S(1)}, bf16[2048,64]{1,0:T(8,128)(2,1)S(1)}, bf16[2048,64]{1,0:T(8,128)(2,1)S(1)}, bf16[2048,64]{1,0:T(8,128)(2,1)S(1)}) custom-call(s32[5]{0:T(128)S(1)} %pad_add_fusion.place_ref, bf16[256,2048]{1,0:T(8,128)(2,1)S(1)} %get-tuple-element.28.x_ref), custom_call_target="tpu_custom_call" | custom-call | flops 2147483648 | bytes 2097152 | tf_op jit(solution)/shard_map/derive/pallas_call | solution.py:301
  64.5 0.0 copy-start.7
  64.5 2.1 %copy-done.7 = bf16[36,256,256]{2,1,0:T(8,128)(2,1)} copy-done((bf16[36,256,256]{2,1,0:T(8,128)(2,1)}, bf16[36,256,256]{2,1,0:T(8,128)(2,1)S(1)}, u32[]{:S(2)}) %copy-start.7) | copy-done | bytes 4718616
  66.6 2.2 %copy-done.9 = bf16[36,256,256]{2,1,0:T(8,128)(2,1)} copy-done((bf16[36,256,256]{2,1,0:T(8,128)(2,1)}, bf16[36,256,256]{2,1,0:T(8,128)(2,1)S(1)}, u32[]{:S(2)}) %copy-start.9) | copy-done | bytes 4718616
  68.8 0.0 collective-permute-done.4.d_ref
  68.8 0.0 collective-permute-done.3.b_ref
  68.8 1.7 %product.1 = bf16[512,1024]{1,0:T(8,128)(2,1)} custom-call(bf16[512,128]{1,0:T(8,128)(2,1)S(1)} %get-tuple-element.44.a_ref, bf16[512,128]{1,0:T(8,128)(2,1)S(1)} %collective-permute-done.3.b_ref, bf16[128,1024]{1,0:T(8,128)(2,1)S(1)} %copy-done.2, bf16[128,1024]{1,0:T(8,128)(2,1)S(1)} %collective-permute-done.4.d_ref), custom_call_target="tpu_custom_call" | custom-call | flops 67108864 | bytes 2097152 | tf_op jit(solution)/shard_map/product/pallas_call | solution.py:301
  70.5 0.0 copy-done.11
  70.5 0.0 copy-done.13
  70.5 0.0 copy-done.15
  70.5 6.5 %all-to-all-start.3 = ((bf16[16,32,1024]{2,1,0:T(8,128)(2,1)}), bf16[16,32,1024]{2,1,0:T(8,128)(2,1)}, u32[]{:S(2)}, u32[]{:S(2)}) async-start(bf16[16,32,1024]{2,1,0:T(8,128)(2,1)} %bitcast.2), calls=%async_computation.3 | async-start | bytes 2097152 | tf_op jit(solution)/shard_map/all_to_all | solution.py:388
  77.0 2.3 %copy-done.8 = bf16[36,256,256]{2,1,0:T(8,128)(2,1)S(1)} copy-done((bf16[36,256,256]{2,1,0:T(8,128)(2,1)S(1)}, bf16[36,256,256]{2,1,0:T(8,128)(2,1)}, u32[]{:S(2)}) %copy-start.8) | copy-done | bytes 4718616
  79.4 2.3 %copy-done.10 = bf16[36,256,256]{2,1,0:T(8,128)(2,1)S(1)} copy-done((bf16[36,256,256]{2,1,0:T(8,128)(2,1)S(1)}, bf16[36,256,256]{2,1,0:T(8,128)(2,1)}, u32[]{:S(2)}) %copy-start.10) | copy-done | bytes 4718616
  81.7 1.0 copy-done.12
  82.7 1.0 copy-done.14
  83.8 1.0 copy-done.16
  84.8 6.0 %attend_backward.1 = (bf16[8,192,128]{2,1,0:T(8,128)(2,1)S(1)}, bf16[8,192,128]{2,1,0:T(8,128)(2,1)S(1)}) custom-call(s32[5]{0:T(128)S(1)} %pad_add_fusion.place_ref, bf16[256,2048]{1,0:T(8,128)(2,1)S(1)} %get-tuple-element.28.x_ref, bf16[64,2048]{1,0:T(8,128)(2,1)S(1)} %get-tuple-element.29.attn_ref, bf16[16,144,128]{2,1,0:T(8,128)(2,1)S(1)} %all-to-all-done.1.got_ref, ...), custom_call_target="tpu_custom_call" | custom-call | flops 8589934592 | bytes 2097152 | tf_op jit(solution)/shard_map/attend_backward/pallas_call | solution.py:301
  90.8 0.3 collective-permute-start.2
  91.1 1.5 %collective-permute-done.2.theirs_ref = bf16[8,192,128]{2,1,0:T(8,128)(2,1)S(1)} collective-permute-done((bf16[8,192,128]{2,1,0:T(8,128)(2,1)S(1)}, bf16[8,192,128]{2,1,0:T(8,128)(2,1)S(1)}, u32[]{:S(2)}, u32[]{:S(2)}) %collective-permute-start.2) | collective-permute-done | bytes 393248 | tf_op jit(solution)/shard_map/ppermute | solution.py:385
  92.6 1.6 %grads_to_owners.1.after_ref = bf16[16,192,128]{2,1,0:T(8,128)(2,1)} custom-call(s32[5]{0:T(128)S(1)} %pad_add_fusion.place_ref, bf16[8,192,128]{2,1,0:T(8,128)(2,1)S(1)} %get-tuple-element.38.mine_ref, bf16[8,192,128]{2,1,0:T(8,128)(2,1)S(1)} %collective-permute-done.2.theirs_ref), custom_call_target="tpu_custom_call" | custom-call | flops 67108864 | bytes 2097152 | tf_op jit(solution)/shard_map/grads_to_owners/pallas_call | solution.py:301
  94.2 0.0 all-to-all-done.3
  94.2 7.3 %all-to-all-start.2 = ((bf16[16,192,128]{2,1,0:T(8,128)(2,1)}), bf16[16,192,128]{2,1,0:T(8,128)(2,1)S(1)}, u32[]{:S(2)}, u32[]{:S(2)}) async-start(bf16[16,192,128]{2,1,0:T(8,128)(2,1)} %grads_to_owners.1.after_ref), calls=%async_computation.2 | async-start | bytes 1572864 | tf_op jit(solution)/shard_map/all_to_all | solution.py:388
  101.4 1.1 d_gate.1
  102.6 1.4 %convert_reduce_fusion = f32[32,1024]{1,0:T(8,128)S(1)} fusion(bf16[16,32,1024]{2,1,0:T(8,128)(2,1)} %all-to-all-done.3), kind=kLoop, calls=%fused_computation | loop fusion | flops 1015808 | bytes 1179648 | tf_op jit(solution)/shard_map/reduce_sum | solution.py:442
  104.1 2.0 %collective-permute-start.5 = (f32[4,4,1024]{2,1,0:T(4,128)S(1)}, f32[4,4,1024]{2,1,0:T(4,128)S(1)}, u32[]{:S(2)}, u32[]{:S(2)}) collective-permute-start(f32[4,4,1024]{2,1,0:T(4,128)S(1)} %dynamic-slice_bitcast_fusion), channel_id=1, source_target_pairs={{0,32},{32,0},{64,96},{96,64},{128,160},{160,128},{192,224},{224,1... | collective-permute-start | bytes 196616 | tf_op jit(solution)/shard_map/ppermute | solution.py:446
  106.1 2.4 %collective-permute-done.5 = f32[4,4,1024]{2,1,0:T(4,128)S(1)} collective-permute-done((f32[4,4,1024]{2,1,0:T(4,128)S(1)}, f32[4,4,1024]{2,1,0:T(4,128)S(1)}, u32[]{:S(2)}, u32[]{:S(2)}) %collective-permute-start.5) | collective-permute-done | bytes 65568 | tf_op jit(solution)/shard_map/ppermute | solution.py:446
  108.5 3.4 %collective-permute-start.6 = (f32[4,1024]{1,0:T(4,128)S(1)}, f32[4,1024]{1,0:T(4,128)S(1)}, u32[]{:S(2)}, u32[]{:S(2)}) collective-permute-start(f32[4,1024]{1,0:T(4,128)S(1)} %get-tuple-element.49), channel_id=1, source_target_pairs={{0,64},{32,96},{64,0},{96,32},{128,192},{160,224},{192,128},{224,1... | collective-permute-start | bytes 49160 | tf_op jit(solution)/shard_map/ppermute | solution.py:446
  111.8 5.4 %collective-permute-start.7 = (f32[4,1024]{1,0:T(4,128)S(1)}, f32[4,1024]{1,0:T(4,128)S(1)}, u32[]{:S(2)}, u32[]{:S(2)}) collective-permute-start(f32[4,1024]{1,0:T(4,128)S(1)} %get-tuple-element.51), channel_id=1, source_target_pairs={{0,128},{32,160},{64,192},{96,224},{128,0},{160,32},{192,64},{224,... | collective-permute-start | bytes 49160 | tf_op jit(solution)/shard_map/ppermute | solution.py:446
  117.2 0.0 collective-permute-start.8
  117.2 0.0 all-to-all-done.2.got_ref
  117.2 1.0 finish.1
  118.2 0.0 collective-permute-done.6
  118.2 1.2 %collective-permute-done.7 = f32[4,1024]{1,0:T(4,128)S(1)} collective-permute-done((f32[4,1024]{1,0:T(4,128)S(1)}, f32[4,1024]{1,0:T(4,128)S(1)}, u32[]{:S(2)}, u32[]{:S(2)}) %collective-permute-start.7) | collective-permute-done | bytes 16416 | tf_op jit(solution)/shard_map/ppermute | solution.py:446
  119.5 3.6 %collective-permute-done.8 = f32[4,1024]{1,0:T(4,128)S(1)} collective-permute-done((f32[4,1024]{1,0:T(4,128)S(1)}, f32[4,1024]{1,0:T(4,128)S(1)}, u32[]{:S(2)}, u32[]{:S(2)}) %collective-permute-start.8) | collective-permute-done | bytes 16416 | tf_op jit(solution)/shard_map/ppermute | solution.py:446
  123.1 0.6 fusion.2
  (16 shorter events, 0.1 us)
Async XLA Ops:
  0.6 1.6 %copy-start = (bf16[1024,1024]{1,0:T(8,128)(2,1)S(1)}, bf16[1024,1024]{1,0:T(8,128)(2,1)}, u32[]{:S(2)}) copy-start(bf16[1024,1024]{1,0:T(8,128)(2,1)} %w_ref.1) | copy-start | bytes 6291460
  2.2 0.9 copy-start.1
  3.2 0.9 copy-start.3
  4.1 0.9 copy-start.4
  5.1 0.9 copy-start.5
  6.0 0.9 copy-start.6
  7.0 9.2 %copy-start.17 = (s32[1,4]{1,0:T(1,128)S(1)}, s32[1,4]{1,0:T(1,128)}, u32[]{:S(2)}) copy-start(s32[1,4]{1,0:T(1,128)} %param.13) | copy-start | bytes 52
  8.7 22.5 %all-to-all-start = ((bf16[16,256,128]{2,1,0:T(8,128)(2,1)}), bf16[16,256,128]{2,1,0:T(8,128)(2,1)S(1)}, u32[]{:S(2)}, u32[]{:S(2)}) async-start(bf16[16,256,128]{2,1,0:T(8,128)(2,1)} %get-tuple-element.27), calls=%async_computation | async-start | bytes 2097152 | tf_op jit(solution)/shard_map/all_to_all | solution.py:388
  31.9 15.9 %copy-start.2 = (bf16[128,1024]{1,0:T(8,128)(2,1)S(1)}, bf16[128,1024]{1,0:T(8,128)(2,1)}, u32[]{:S(2)}) copy-start(bf16[128,1024]{1,0:T(8,128)(2,1)} %c_ref.1) | copy-start | bytes 786436
  31.9 2.0 %collective-permute-start = (bf16[8,256,128]{2,1,0:T(8,128)(2,1)S(1)}, bf16[8,256,128]{2,1,0:T(8,128)(2,1)S(1)}, u32[]{:S(2)}, u32[]{:S(2)}) collective-permute-start(bf16[8,256,128]{2,1,0:T(8,128)(2,1)S(1)} %other_half.1), channel_id=1, source_target_pairs={{0,1},{1,0},{2,3},{3,2},{4,5},{5,4},{6,7},{7,6},{8,9},{9,8},{10,11... | collective-permute-start | bytes 1572872 | tf_op jit(solution)/shard_map/ppermute | solution.py:385
  38.8 1.4 %collective-permute-start.1 = (bf16[8,64,128]{2,1,0:T(8,128)(2,1)S(1)}, bf16[8,64,128]{2,1,0:T(8,128)(2,1)S(1)}, u32[]{:S(2)}, u32[]{:S(2)}) collective-permute-start(bf16[8,64,128]{2,1,0:T(8,128)(2,1)S(1)} %get-tuple-element.31), channel_id=1, source_target_pairs={{0,1},{1,0},{2,3},{3,2},{4,5},{5,4},{6,7},{7,6},{8,9},{9,8},{10,11... | collective-permute-start | bytes 393224 | tf_op jit(solution)/shard_map/ppermute | solution.py:385
  41.7 16.6 %all-to-all-start.1 = ((bf16[16,144,128]{2,1,0:T(8,128)(2,1)}), bf16[16,144,128]{2,1,0:T(8,128)(2,1)S(1)}, u32[]{:S(2)}, u32[]{:S(2)}) async-start(bf16[16,144,128]{2,1,0:T(8,128)(2,1)} %attn_to_owners.1), calls=%async_computation.1 | async-start | bytes 1179648 | tf_op jit(solution)/shard_map/all_to_all | solution.py:388
  47.8 21.0 %collective-permute-start.4 = (bf16[128,1024]{1,0:T(8,128)(2,1)S(1)}, bf16[128,1024]{1,0:T(8,128)(2,1)S(1)}, u32[]{:S(2)}, u32[]{:S(2)}) collective-permute-start(bf16[128,1024]{1,0:T(8,128)(2,1)S(1)} %copy-done.2), channel_id=1, source_target_pairs={{0,1},{1,0},{2,3},{3,2},{4,5},{5,4},{6,7},{7,6},{8,9},{9,8},{10,11... | collective-permute-start | bytes 786440 | tf_op jit(solution)/shard_map/ppermute | solution.py:385
  59.3 9.6 %collective-permute-start.3 = (bf16[512,128]{1,0:T(8,128)(2,1)S(1)}, bf16[512,128]{1,0:T(8,128)(2,1)S(1)}, u32[]{:S(2)}, u32[]{:S(2)}) collective-permute-start(bf16[512,128]{1,0:T(8,128)(2,1)S(1)} %get-tuple-element.45), channel_id=1, source_target_pairs={{0,1},{1,0},{2,3},{3,2},{4,5},{5,4},{6,7},{7,6},{8,9},{9,8},{10,11... | collective-permute-start | bytes 393224 | tf_op jit(solution)/shard_map/ppermute | solution.py:385
  64.5 2.1 %copy-start.7 = (bf16[36,256,256]{2,1,0:T(8,128)(2,1)}, bf16[36,256,256]{2,1,0:T(8,128)(2,1)S(1)}, u32[]{:S(2)}) copy-start(bf16[36,256,256]{2,1,0:T(8,128)(2,1)S(1)} %get-tuple-element.33.silu_ref) | copy-start | bytes 14155780
  66.6 2.2 %copy-start.9 = (bf16[36,256,256]{2,1,0:T(8,128)(2,1)}, bf16[36,256,256]{2,1,0:T(8,128)(2,1)S(1)}, u32[]{:S(2)}) copy-start(bf16[36,256,256]{2,1,0:T(8,128)(2,1)S(1)} %get-tuple-element.34.slope_ref) | copy-start | bytes 14155780
  68.8 1.7 %copy-start.11 = (bf16[2048,64]{1,0:T(8,128)(2,1)}, bf16[2048,64]{1,0:T(8,128)(2,1)S(1)}, u32[]{:S(2)}) copy-start(bf16[2048,64]{1,0:T(8,128)(2,1)S(1)} %get-tuple-element.35.qn_ref) | copy-start | bytes 786436
  68.8 1.7 %copy-start.13 = (bf16[2048,64]{1,0:T(8,128)(2,1)}, bf16[2048,64]{1,0:T(8,128)(2,1)S(1)}, u32[]{:S(2)}) copy-start(bf16[2048,64]{1,0:T(8,128)(2,1)S(1)} %get-tuple-element.36.kn_ref) | copy-start | bytes 786436
  68.8 1.7 %copy-start.15 = (bf16[2048,64]{1,0:T(8,128)(2,1)}, bf16[2048,64]{1,0:T(8,128)(2,1)S(1)}, u32[]{:S(2)}) copy-start(bf16[2048,64]{1,0:T(8,128)(2,1)S(1)} %get-tuple-element.37.vn_ref) | copy-start | bytes 786436
  70.5 23.7 %all-to-all-start.3 = ((bf16[16,32,1024]{2,1,0:T(8,128)(2,1)}), bf16[16,32,1024]{2,1,0:T(8,128)(2,1)}, u32[]{:S(2)}, u32[]{:S(2)}) async-start(bf16[16,32,1024]{2,1,0:T(8,128)(2,1)} %bitcast.2), calls=%async_computation.3 | async-start | bytes 2097152 | tf_op jit(solution)/shard_map/all_to_all | solution.py:388
  77.0 2.3 %copy-start.8 = (bf16[36,256,256]{2,1,0:T(8,128)(2,1)S(1)}, bf16[36,256,256]{2,1,0:T(8,128)(2,1)}, u32[]{:S(2)}) copy-start(bf16[36,256,256]{2,1,0:T(8,128)(2,1)} %copy-done.7) | copy-start | bytes 14155780
  79.4 2.3 %copy-start.10 = (bf16[36,256,256]{2,1,0:T(8,128)(2,1)S(1)}, bf16[36,256,256]{2,1,0:T(8,128)(2,1)}, u32[]{:S(2)}) copy-start(bf16[36,256,256]{2,1,0:T(8,128)(2,1)} %copy-done.9) | copy-start | bytes 14155780
  81.7 1.0 copy-start.12
  82.7 1.0 copy-start.14
  83.8 1.0 copy-start.16
  90.8 1.8 %collective-permute-start.2 = (bf16[8,192,128]{2,1,0:T(8,128)(2,1)S(1)}, bf16[8,192,128]{2,1,0:T(8,128)(2,1)S(1)}, u32[]{:S(2)}, u32[]{:S(2)}) collective-permute-start(bf16[8,192,128]{2,1,0:T(8,128)(2,1)S(1)} %get-tuple-element.39), channel_id=1, source_target_pairs={{0,1},{1,0},{2,3},{3,2},{4,5},{5,4},{6,7},{7,6},{8,9},{9,8},{10,11... | collective-permute-start | bytes 1179656 | tf_op jit(solution)/shard_map/ppermute | solution.py:385
  94.2 23.0 %all-to-all-start.2 = ((bf16[16,192,128]{2,1,0:T(8,128)(2,1)}), bf16[16,192,128]{2,1,0:T(8,128)(2,1)S(1)}, u32[]{:S(2)}, u32[]{:S(2)}) async-start(bf16[16,192,128]{2,1,0:T(8,128)(2,1)} %grads_to_owners.1.after_ref), calls=%async_computation.2 | async-start | bytes 1572864 | tf_op jit(solution)/shard_map/all_to_all | solution.py:388
  104.1 4.4 %collective-permute-start.5 = (f32[4,4,1024]{2,1,0:T(4,128)S(1)}, f32[4,4,1024]{2,1,0:T(4,128)S(1)}, u32[]{:S(2)}, u32[]{:S(2)}) collective-permute-start(f32[4,4,1024]{2,1,0:T(4,128)S(1)} %dynamic-slice_bitcast_fusion), channel_id=1, source_target_pairs={{0,32},{32,0},{64,96},{96,64},{128,160},{160,128},{192,224},{224,1... | collective-permute-start | bytes 196616 | tf_op jit(solution)/shard_map/ppermute | solution.py:446
  108.5 9.8 %collective-permute-start.6 = (f32[4,1024]{1,0:T(4,128)S(1)}, f32[4,1024]{1,0:T(4,128)S(1)}, u32[]{:S(2)}, u32[]{:S(2)}) collective-permute-start(f32[4,1024]{1,0:T(4,128)S(1)} %get-tuple-element.49), channel_id=1, source_target_pairs={{0,64},{32,96},{64,0},{96,32},{128,192},{160,224},{192,128},{224,1... | collective-permute-start | bytes 49160 | tf_op jit(solution)/shard_map/ppermute | solution.py:446
  111.8 7.6 %collective-permute-start.7 = (f32[4,1024]{1,0:T(4,128)S(1)}, f32[4,1024]{1,0:T(4,128)S(1)}, u32[]{:S(2)}, u32[]{:S(2)}) collective-permute-start(f32[4,1024]{1,0:T(4,128)S(1)} %get-tuple-element.51), channel_id=1, source_target_pairs={{0,128},{32,160},{64,192},{96,224},{128,0},{160,32},{192,64},{224,... | collective-permute-start | bytes 49160 | tf_op jit(solution)/shard_map/ppermute | solution.py:446
  117.2 5.8 %collective-permute-start.8 = (f32[4,1024]{1,0:T(4,128)S(1)}, f32[4,1024]{1,0:T(4,128)S(1)}, u32[]{:S(2)}, u32[]{:S(2)}) collective-permute-start(f32[4,1024]{1,0:T(4,128)S(1)} %get-tuple-element.50), channel_id=1, source_target_pairs={{0,192},{32,224},{64,128},{96,160},{128,64},{160,96},{192,0},{224,... | collective-permute-start | bytes 49160 | tf_op jit(solution)/shard_map/ppermute | solution.py:446

commit v3 on v2

--- a/solution.py
+++ b/solution.py
@@ -138,29 +138,67 @@
         theirs_ref[j] = jnp.where(core == 0, pair[1], pair[0])
 
 
-PAIRS = [(q, k) for q in range(HALF // SUB) for k in range(q + 1)]
+GROUPS = [[(q_at // SUB + q, k_at // SUB + k) for q, k in subs] for q_at, k_at, subs in below(HALF // B_TILE, B_TILE)]
+PAIRS = [pair for group in GROUPS for pair in group]
 AT = {pair: i for i, pair in enumerate(PAIRS)}
 
 
-def derive_kernel(place_ref, x_ref, silu_ref, slope_ref, qn_ref, kn_ref, vn_ref):
+def group_copies(from_ref, to_ref, sems):
+    copies, at = [], 0
+    for i, group in enumerate(GROUPS):
+        part = pl.ds(at, len(group))
+        copies.append(pltpu.make_async_copy(from_ref.at[part], to_ref.at[part], sems.at[i]))
+        at += len(group)
+    return copies
+
+
+def derive_kernel(
+    place_ref, x_ref, silu_out, slope_out, q_out, v_out,
+    silu_ref, slope_ref, qn_ref, kn_ref, vn_ref, silu_sems, slope_sems, sems,
+):
     end1, end2 = place_of(place_ref)[3:]
     for b in range(N_BLOCKS):
         cols = slice(b * BLOCK, (b + 1) * BLOCK)
         for i, out_ref in enumerate((qn_ref, kn_ref, vn_ref)):
             out_ref[cols, :] = x_ref[i * 64 : (i + 1) * 64, cols].T
-    for q, k in PAIRS:
-        q_cols, k_cols = slice(q * SUB, (q + 1) * SUB), slice(k * SUB, (k + 1) * SUB)
-        s = dot(kn_ref[k_cols, :], x_ref[0:64, q_cols])
-        sigma = jnp.where(live_of(q * SUB, k * SUB, end1, end2, q == k), sigmoid(s), 0.0)
-        silu = s * sigma
-        silu_ref[AT[q, k]] = silu.astype(BF16)
-        slope_ref[AT[q, k]] = (sigma + silu * (1.0 - sigma)).astype(BF16)
+    copies = [
+        pltpu.make_async_copy(qn_ref, q_out, sems.at[0]),
+        pltpu.make_async_copy(vn_ref, v_out, sems.at[1]),
+    ]
+    for copy in copies:
+        copy.start()
+    silu_copies = group_copies(silu_ref, silu_out, silu_sems)
+    slope_copies = group_copies(slope_ref, slope_out, slope_sems)
+    for i, group in enumerate(GROUPS):
+        for q, k in group:
+            q_cols, k_cols = slice(q * SUB, (q + 1) * SUB), slice(k * SUB, (k + 1) * SUB)
+            s = dot(kn_ref[k_cols, :], x_ref[0:64, q_cols])
+            sigma = jnp.where(live_of(q * SUB, k * SUB, end1, end2, q == k), sigmoid(s), 0.0)
+            silu = s * sigma
+            silu_ref[AT[q, k]] = silu.astype(BF16)
+            slope_ref[AT[q, k]] = (sigma + silu * (1.0 - sigma)).astype(BF16)
+        silu_copies[i].start()
+        slope_copies[i].start()
+    for copy in copies + silu_copies + slope_copies:
+        copy.wait()
 
 
 def backward_kernel(
-    place_ref, x_ref, attn_ref, got_ref, silu_ref, slope_ref, qn_ref, kn_ref, vn_ref, mine_ref, theirs_ref,
-    dn_ref, dt_ref, dq_ref, dk_ref, dv_ref, slot_ref,
+    place_ref, x_ref, attn_ref, got_ref, silu_in, slope_in, q_in, v_in, mine_ref, theirs_ref,
+    silu_ref, slope_ref, qn_ref, vn_ref, dn_ref, dt_ref, dq_ref, dk_ref, dv_ref, slot_ref,
+    silu_sems, slope_sems, sems,
 ):
+    v_copy = pltpu.make_async_copy(v_in, vn_ref, sems.at[1])
+    q_copy = pltpu.make_async_copy(q_in, qn_ref, sems.at[0])
+    silu_copies = group_copies(silu_in, silu_ref, silu_sems)
+    slope_copies = group_copies(slope_in, slope_ref, slope_sems)
+    v_copy.start()
+    slope_copies[0].start()
+    silu_copies[0].start()
+    q_copy.start()
+    for i in range(1, len(GROUPS)):
+        slope_copies[i].start()
+        silu_copies[i].start()
     core, _, turn, end1, end2 = place_of(place_ref)
     stat = got_ref[:, 64 : 64 + STATS * N_BLOCKS, :].astype(F32).reshape(HEADS, STATS, N_BLOCKS, BLOCK)
     mean_h = stat[:, 0] + stat[:, 1]
@@ -179,7 +217,9 @@
         dt_ref[:, cols] = d
         dn_ref[cols, :] = d.T
 
-    for q_at, k_at, subs in below(HALF // B_TILE, B_TILE):
+    v_copy.wait()
+    for i, (q_at, k_at, subs) in enumerate(below(HALF // B_TILE, B_TILE)):
+        slope_copies[i].wait()
         n = B_TILE // SUB
         q_first, k_first = q_at // SUB, k_at // SUB
         made = {}
@@ -188,6 +228,9 @@
             k_cols = slice(k_at + k * SUB, k_at + (k + 1) * SUB)
             d_p = dot(vn_ref[k_cols, :], dt_ref[:, q_cols])
             made[q, k] = (d_p * slope_ref[AT[q_first + q, k_first + k]].astype(F32)).astype(BF16)
+        silu_copies[i].wait()
+        if i == 0:
+            q_copy.wait()
         for k in range(n):
             k_cols = slice(k_at + k * SUB, k_at + (k + 1) * SUB)
             d_v, d_k = [], []
@@ -219,17 +262,48 @@
     turn_out(turned, turn, core, slot_ref, mine_ref, theirs_ref)
 
 
-def prepare_kernel(q_ref, k_ref, v_ref, u_ref, cot_ref, w_ref, send_ref, ut_ref, dg_ref):
-    for at in range(0, WIDTH, 256):
-        cols = slice(at, at + 256)
+def prepare_kernel(
+    q_in, k_in, v_in, u_in, cot_in, w_in, send_out, ut_out, dg_out,
+    q_ref, k_ref, v_ref, u_ref, cot_ref, w_ref, send_ref, ut_ref, dg_ref, in_sems, w_sems, out_sems,
+):
+    pairs = (q_in, q_ref), (k_in, k_ref), (v_in, v_ref), (cot_in, cot_ref), (u_in, u_ref)
+    copies = [pltpu.make_async_copy(a, b, in_sems.at[i]) for i, (a, b) in enumerate(pairs)]
+    parts = [pl.ds(at, 256) for at in range(0, WIDTH, 256)]
+    heads = [pl.ds(at, 4) for at in range(0, HEADS, 4)]
+    w_copies = [pltpu.make_async_copy(w_in.at[part], w_ref.at[part], w_sems.at[i]) for i, part in enumerate(parts)]
+    outs = [
+        [
+            pltpu.make_async_copy(send_ref.at[heads[i]], send_out.at[heads[i]], out_sems.at[0, i]),
+            pltpu.make_async_copy(ut_ref.at[parts[i]], ut_out.at[parts[i]], out_sems.at[1, i]),
+            pltpu.make_async_copy(dg_ref.at[parts[i]], dg_out.at[parts[i]], out_sems.at[2, i]),
+        ]
+        for i in range(4)
+    ]
+    for copy in copies + w_copies:
+        copy.start()
+    for i, ref in enumerate((q_ref, k_ref, v_ref)):
+        copies[i].wait()
+        for at in range(0, WIDTH, 256):
+            rows = ref[:, at : at + 256].T
+            for h in range(4):
+                send_ref[at // 64 + h, i * 64 : (i + 1) * 64, :] = rows[h * 64 : (h + 1) * 64]
+    copies[3].wait()
+    copies[4].wait()
+    for i in range(4):
+        cols = slice(i * 256, (i + 1) * 256)
+        u_t = u_ref[:, cols].T
+        w_copies[i].wait()
         d_gated = dot_nt(w_ref[cols, :], cot_ref[...])
-        u_t = u_ref[:, cols].T
         dg_ref[cols, :] = d_gated
         ut_ref[cols, :] = u_t
         g_t = (d_gated * u_t.astype(F32)).astype(BF16)
-        for i, rows in enumerate((q_ref[:, cols].T, k_ref[:, cols].T, v_ref[:, cols].T, g_t)):
-            for h in range(4):
-                send_ref[at // 64 + h, i * 64 : (i + 1) * 64, :] = rows[h * 64 : (h + 1) * 64]
+        for h in range(4):
+            send_ref[4 * i + h, 192:256, :] = g_t[h * 64 : (h + 1) * 64]
+        for copy in outs[i]:
+            copy.start()
+    for out in outs:
+        for copy in out:
+            copy.wait()
 
 
 def other_half_kernel(place_ref, got_ref, out_ref):
@@ -262,11 +336,12 @@
 def gated_kernel(place_ref, got_ref, ut_ref, mine_ref, theirs_ref, zero_ref, one_ref):
     core = place_ref[4]
     gated = normalised(got_ref) * ut_ref[...].astype(F32)
-    for z in range(0, 8, 2):
+    for z in (0, 1, 4, 5):
         for chip in range(HEADS):
             at = z * BLOCK + chip * 8
-            one, two = gated[at : at + 8], gated[at + BLOCK : at + BLOCK + 8]
-            rows = slice(chip * 32 + z * 4, chip * 32 + z * 4 + 8)
+            one, two = gated[at : at + 8], gated[at + 2 * BLOCK : at + 2 * BLOCK + 8]
+            row = (z % 2) * 256 + chip * 16 + (z // 2) * 4
+            rows = slice(row, row + 8)
             zero_ref[rows, :] = jnp.concatenate([one[0:4], two[0:4]], axis=0)
             one_ref[rows, :] = jnp.concatenate([one[4:8], two[4:8]], axis=0)
     zero, one = zero_ref[...].astype(BF16), one_ref[...].astype(BF16)
@@ -295,14 +370,16 @@
 
 SMEM = pl.BlockSpec(memory_space=pltpu.SMEM)
 VMEM = pl.BlockSpec(memory_space=pltpu.VMEM)
-
-
-def call(kernel, name, out_shape, in_specs, args, scratch=(), mib=8, flops=1 << 26, transcendentals=0):
+ANY = pl.BlockSpec(memory_space=pl.ANY)
+DMA = pltpu.SemaphoreType.DMA
+
+
+def call(kernel, name, out_shape, in_specs, args, scratch=(), out=VMEM, mib=8, flops=1 << 26, transcendentals=0):
     return pl.pallas_call(
         kernel,
         out_shape=out_shape,
         in_specs=in_specs,
-        out_specs=jax.tree.map(lambda _: VMEM, out_shape),
+        out_specs=jax.tree.map(lambda _: out, out_shape),
         scratch_shapes=list(scratch),
         compiler_params=pltpu.CompilerParams(vmem_limit_bytes=mib * 1024 * 1024),
         cost_estimate=pl.CostEstimate(flops=flops, bytes_accessed=1 << 21, transcendentals=transcendentals),
@@ -316,7 +393,19 @@
 
 def prepare(*args):
     shapes = shape((HEADS, 256, BLOCK)), shape((WIDTH, BLOCK)), shape((WIDTH, BLOCK), F32)
-    return call(prepare_kernel, "prepare", shapes, [VMEM] * 6, args, mib=12)
+    return call(
+        prepare_kernel,
+        "prepare",
+        shapes,
+        [ANY] * 6,
+        args,
+        [pltpu.VMEM((BLOCK, WIDTH), BF16)] * 5
+        + [pltpu.VMEM((WIDTH, WIDTH), BF16)]
+        + [pltpu.VMEM(s.shape, s.dtype) for s in shapes]
+        + [DMA((5,)), DMA((4,)), DMA((3, 4))],
+        out=ANY,
+        mib=12,
+    )
 
 
 def attend_forward(place, got, other):
@@ -344,35 +433,42 @@
 
 
 def derive(place, x):
-    tiles = shape((len(PAIRS), SUB, SUB))
+    tiles, rows = (len(PAIRS), SUB, SUB), (HALF, HEAD_DIM)
     return call(
         derive_kernel,
         "derive",
-        (tiles, tiles) + (shape((HALF, HEAD_DIM)),) * 3,
+        (shape(tiles), shape(tiles), shape(rows), shape(rows)),
         [SMEM, VMEM],
         (place, x),
-        mib=16,
+        [pltpu.VMEM(tiles, BF16)] * 2
+        + [pltpu.VMEM(rows, BF16)] * 3
+        + [DMA((len(GROUPS),)), DMA((len(GROUPS),)), DMA((2,))],
+        out=ANY,
+        mib=24,
         flops=1 << 31,
         transcendentals=1 << 22,
     )
 
 
 def attend_backward(place, x, attn, got, derived):
+    tiles, rows = (len(PAIRS), SUB, SUB), (HALF, HEAD_DIM)
     return call(
         backward_kernel,
         "attend_backward",
         (shape((8, 192, BLOCK)), shape((8, 192, BLOCK))),
-        [SMEM] + [VMEM] * 8,
+        [SMEM] + [VMEM] * 3 + [ANY] * 4,
         (place, x, attn, got) + derived,
-        [
-            pltpu.VMEM((HALF, HEAD_DIM), BF16),
+        [pltpu.VMEM(tiles, BF16)] * 2
+        + [pltpu.VMEM(rows, BF16)] * 3
+        + [
             pltpu.VMEM((HEAD_DIM, HALF), BF16),
             pltpu.VMEM((HEAD_DIM, HALF), F32),
-            pltpu.VMEM((HALF, HEAD_DIM), F32),
-            pltpu.VMEM((HALF, HEAD_DIM), F32),
+            pltpu.VMEM(rows, F32),
+            pltpu.VMEM(rows, F32),
             pltpu.VMEM((N_BLOCKS, 192, BLOCK), F32),
-        ],
-        mib=20,
+        ]
+        + [DMA((len(GROUPS),)), DMA((len(GROUPS),)), DMA((2,))],
+        mib=32,
         flops=1 << 33,
     )
 
@@ -401,7 +497,7 @@
         (place, mine, swap(theirs), stat),
     )
     got_attn = chips(send)
-    derived = derive(place, x)
+    got_attn, derived = lax.optimization_barrier((got_attn, derive(place, x)))
 
     mine, theirs = call(
         gated_kernel,
@@ -418,7 +514,7 @@
         [VMEM] * 4,
         (mine, swap(theirs), cotangent, swap(cotangent)),
     )
-    parts = chips(part.reshape(HEADS, 32, WIDTH))
+    parts = lax.all_to_all(part.reshape(32, 16, WIDTH), ("zl",) + CHIP, 0, 0, tiled=True)
 
     mine, theirs = attend_backward(place, x, attn, got_attn, derived)
     send = call(
@@ -433,38 +529,34 @@
         d_gate_kernel,
         "d_gate",
         shape((BLOCK, WIDTH)),
-        [VMEM, VMEM, pl.BlockSpec(memory_space=pl.ANY)],
+        [VMEM, VMEM, ANY],
         (got_attn, d_gated_t, send),
         flops=1 << 20,
     )
 
     parts, d_gate = lax.optimization_barrier((parts, d_gate))
-    part = jnp.sum(parts.astype(F32), axis=0).reshape(4, 2, 4, WIDTH)
-    z = lax.axis_index("dp")
-
-    def exchange(x, step):
-        return lax.ppermute(x, "dp", [(i, i ^ step) for i in range(8)])
-
-    away = lax.dynamic_index_in_dim(part, 1 - z % 2, 1, keepdims=False)
-    part = lax.dynamic_index_in_dim(part, z % 2, 1, keepdims=False) + exchange(away, 1)
-    d_weight = lax.dynamic_index_in_dim(part, z // 2, 0, keepdims=False)
-    for step in (1, 2, 3):
-        away = lax.dynamic_index_in_dim(part, (z // 2) ^ step, 0, keepdims=False)
-        d_weight = d_weight + exchange(away, 2 * step)
-    d_weight = d_weight * (1.0 / math.sqrt(32768))
+    part = jnp.sum(parts.astype(F32), axis=0).reshape(4, 4, WIDTH)
+    z = lax.axis_index("zh")
+    for step in (2, 1):
+        high = (z // step) % 2
+        halves = part.reshape(2, step, 4, WIDTH)
+        away = lax.dynamic_index_in_dim(halves, 1 - high, 0, keepdims=False)
+        kept = lax.dynamic_index_in_dim(halves, high, 0, keepdims=False)
+        part = kept + lax.ppermute(away, "zh", [(i, i ^ step) for i in range(4)])
+    d_weight = part.reshape(4, WIDTH) * (1.0 / math.sqrt(32768))
 
     d_query, d_key, d_value = call(finish_kernel, "finish", (shape((BLOCK, WIDTH)),) * 3, [VMEM], (got,))
     return d_query, d_key, d_value, d_gate, d_weight
 
 
 def solution(mesh):
-    axes = ("dp", "x", "y", "core")
-    inner = Mesh(mesh.devices.reshape(8, 4, 4, 2), axes)
+    axes = ("zh", "zl", "x", "y", "core")
+    inner = Mesh(mesh.devices.reshape(4, 2, 4, 4, 2), axes)
     rows = P(axes, None)
     return jax.shard_map(
         on_device,
         mesh=inner,
-        in_specs=(rows, rows, rows, rows, P(), rows, P("dp", None)),
+        in_specs=(rows, rows, rows, rows, P(), rows, P(("zh", "zl"), None)),
         out_specs=(rows, rows, rows, rows, rows),
         check_vma=False,
     )

time: 125 us -> 118 us (0.944)
  waiting for transfers between devices: 37.2 us -> 23.4 us
  Pallas kernels: 25.9 us -> 31.2 us
  starting transfers between devices: 39.1 us -> 40.4 us
    all_to_all x4 -> x3, waiting for transfers between devices: 25.4 us -> 15 us  [chips(): return lax.all_to_all(x, CHIP, 0, 0, tiled=True)]
    all_to_all x0 -> x1, starting transfers between devices: none -> 8.85 us  [on_device(): lax.all_to_all(part.reshape(32, 16, WIDTH), ('zl',) + CHIP, 0, 0, tiled=T...]
    all_to_all x4 -> x3, starting transfers between devices: 27.4 us -> 20.8 us  [chips(): return lax.all_to_all(x, CHIP, 0, 0, tiled=True)]
    pallas_call x11, Pallas kernels: 25.9 us -> 31.2 us  [call(): pl.pallas_call(kernel, out_shape=out_shape, in_specs=in_specs, out_specs=...]
    ppermute x4 -> x2, waiting for transfers between devices: 7.21 us -> 2.61 us  [on_device(): part = kept + lax.ppermute(away, 'zh', [(i, i ^ step) for i in range(4)])]
    ppermute x4 -> x2, starting transfers between devices: 10.7 us -> 9.4 us  [on_device(): part = kept + lax.ppermute(away, 'zh', [(i, i ^ step) for i in range(4)])]
    unnamed x36 -> x32, local copies, waits for them, and re-layouts: 18.5 us -> 19 us
  transfers between devices with their start and end apart: 13 -> 11, of which waited for: 8 -> 7; matrix products, arithmetic and copies ran while one was open for 1% -> 1% of each run, Pallas kernels for 13% -> 16%
where the time goes in v3:
time: 118 us; the launch traced here: 117 us
  starting transfers between devices  40.4 us (34%)
  Pallas kernels  31.2 us (26%)
  waiting for transfers between devices  23.4 us (20%)
  local copies, waits for them, and re-layouts  19.1 us (16%)
  other arithmetic  2.09 us (2%)
    pallas_call x11, Pallas kernels, call(): pl.pallas_call(kernel, out_shape=out_shape, in_specs=in_specs, out_specs=...  31.2 us
    all_to_all x3, starting transfers between devices, chips(): return lax.all_to_all(x, CHIP, 0, 0, tiled=True)  20.8 us
    unnamed x32, local copies, waits for them, and re-layouts  19 us
    all_to_all x3, waiting for transfers between devices, chips(): return lax.all_to_all(x, CHIP, 0, 0, tiled=True)  15 us
    ppermute x2, starting transfers between devices, on_device(): part = kept + lax.ppermute(away, 'zh', [(i, i ^ step) for i in range(4)])  9.4 us
    all_to_all x1, starting transfers between devices, on_device(): lax.all_to_all(part.reshape(32, 16, WIDTH), ('zl',) + CHIP, 0, 0, tiled=T...  8.85 us
    ppermute x5, waiting for transfers between devices, swap(): return lax.ppermute(x, 'core', SWAP)  5.8 us
    ppermute x2, waiting for transfers between devices, on_device(): part = kept + lax.ppermute(away, 'zh', [(i, i ^ step) for i in range(4)])  2.61 us
  transfers between devices with their start and end apart: 11, of which 7 were waited for; matrix products, arithmetic and copies ran while one was open for 1% of the time, Pallas kernels for 16%

profile of v3, /device:TPU:2, one launch (start us, length us, event | category | flops | bytes accessed | tf_op | source)
XLA Modules:
  0.0 116.9 jit_solution(4336696820686001140)
XLA Ops:
  0.6 0.0 copy-start
  0.6 1.6 %copy-done = bf16[1024,1024]{1,0:T(8,128)(2,1)S(1)} copy-done((bf16[1024,1024]{1,0:T(8,128)(2,1)S(1)}, bf16[1024,1024]{1,0:T(8,128)(2,1)}, u32[]{:S(2)}) %copy-start) | copy-done | bytes 2097176
  2.2 0.0 copy-start.1
  2.2 0.9 copy-done.1
  3.2 0.0 copy-start.3
  3.2 0.9 copy-done.3
  4.1 0.0 copy-start.4
  4.1 0.9 copy-done.4
  5.1 0.0 copy-start.5
  5.1 0.9 copy-done.5
  6.0 0.0 copy-start.6
  6.0 0.9 copy-done.6
  7.0 0.0 copy-start.15
  7.0 4.2 %prepare.1 = (bf16[16,256,128]{2,1,0:T(8,128)(2,1)}, bf16[1024,128]{1,0:T(8,128)(2,1)S(1)}, f32[1024,128]{1,0:T(8,128)S(1)}) custom-call(bf16[128,1024]{1,0:T(8,128)(2,1)S(1)} %copy-done.3, bf16[128,1024]{1,0:T(8,128)(2,1)S(1)} %copy-done.4, bf16[128,1024]{1,0:T(8,128)(2,1)S(1)} %copy-done.5, bf16[128,1024]{1,0:T(8,128)(2,1)S(1)} %copy-done.6, ...), custom_call_target="tpu_custom_call" | custom-call | flops 67108864 | bytes 2097152 | tf_op jit(solution)/shard_map/prepare/pallas_call | solution.py:378
  11.2 7.5 %all-to-all-start = ((bf16[16,256,128]{2,1,0:T(8,128)(2,1)}), bf16[16,256,128]{2,1,0:T(8,128)(2,1)S(1)}, u32[]{:S(2)}, u32[]{:S(2)}) async-start(bf16[16,256,128]{2,1,0:T(8,128)(2,1)} %get-tuple-element.31), calls=%async_computation | async-start | bytes 2097152 | tf_op jit(solution)/shard_map/all_to_all | solution.py:484
  18.7 0.0 copy-done.15
  18.7 0.1 pad_add_fusion.place_ref
  18.8 15.0 %all-to-all-done.got_ref = bf16[16,256,128]{2,1,0:T(8,128)(2,1)S(1)} async-done(((bf16[16,256,128]{2,1,0:T(8,128)(2,1)}), bf16[16,256,128]{2,1,0:T(8,128)(2,1)S(1)}, u32[]{:S(2)}, u32[]{:S(2)}) %all-to-all-start) | async-done | bytes 1048608 | tf_op jit(solution)/shard_map/all_to_all | solution.py:484
  33.7 0.7 other_half.1
  34.4 0.0 copy-start.2
  34.4 0.1 collective-permute-start
  34.5 1.9 %collective-permute-done.other_ref = bf16[8,256,128]{2,1,0:T(8,128)(2,1)S(1)} collective-permute-done((bf16[8,256,128]{2,1,0:T(8,128)(2,1)S(1)}, bf16[8,256,128]{2,1,0:T(8,128)(2,1)S(1)}, u32[]{:S(2)}, u32[]{:S(2)}) %collective-permute-start) | collective-permute-done | bytes 524320 | tf_op jit(solution)/shard_map/ppermute | solution.py:481
  36.4 4.9 %attend_forward.1 = (bf16[256,2048]{1,0:T(8,128)(2,1)S(1)}, bf16[64,2048]{1,0:T(8,128)(2,1)S(1)}, bf16[8,64,128]{2,1,0:T(8,128)(2,1)S(1)}, bf16[8,64,128]{2,1,0:T(8,128)(2,1)S(1)}, bf16[80,128]{1,0:T(8,128)(2,1)S(1)}) custom-call(s32[5]{0:T(128)S(1)} %pad_add_fusion.place_ref, bf16[16,256,128]{2,1,0:T(8,128)(2,1)S(1)} %all-to-all-done.got_ref, ...), custom_call_target="tpu_custom_call" | custom-call | flops 1073741824 | bytes 2097152 | tf_op jit(solution)/shard_map/attend_forward/pallas_call | solution.py:378
  41.3 0.2 collective-permute-start.1
  41.5 1.2 %collective-permute-done.1.theirs_ref = bf16[8,64,128]{2,1,0:T(8,128)(2,1)S(1)} collective-permute-done((bf16[8,64,128]{2,1,0:T(8,128)(2,1)S(1)}, bf16[8,64,128]{2,1,0:T(8,128)(2,1)S(1)}, u32[]{:S(2)}, u32[]{:S(2)}) %collective-permute-start.1) | collective-permute-done | bytes 131104 | tf_op jit(solution)/shard_map/ppermute | solution.py:481
  42.7 1.4 %attn_to_owners.1 = bf16[16,144,128]{2,1,0:T(8,128)(2,1)} custom-call(s32[5]{0:T(128)S(1)} %pad_add_fusion.place_ref, bf16[8,64,128]{2,1,0:T(8,128)(2,1)S(1)} %get-tuple-element.34.mine_ref, bf16[8,64,128]{2,1,0:T(8,128)(2,1)S(1)} %collective-permute-done.1.theirs_ref, bf16[80,128]{1,0:T(8,128)(2,1)S(1)} %get-tuple-element.36.stat_ref), custom_call_target="tpu_custom_call" | custom-call | flops 67108864 | bytes 2097152 | tf_op jit(solution)/shard_map/attn_to_owners/pallas_call | solution.py:378
  44.2 6.1 %all-to-all-start.1 = ((bf16[16,144,128]{2,1,0:T(8,128)(2,1)}), bf16[16,144,128]{2,1,0:T(8,128)(2,1)S(1)}, u32[]{:S(2)}, u32[]{:S(2)}) async-start(bf16[16,144,128]{2,1,0:T(8,128)(2,1)} %attn_to_owners.1), calls=%async_computation.1 | async-start | bytes 1179648 | tf_op jit(solution)/shard_map/all_to_all | solution.py:484
  50.3 0.0 copy-done.2
  50.3 0.3 collective-permute-start.4
  50.6 6.3 %derive.1 = (bf16[36,256,256]{2,1,0:T(8,128)(2,1)S(1)}, bf16[36,256,256]{2,1,0:T(8,128)(2,1)S(1)}, bf16[2048,64]{1,0:T(8,128)(2,1)S(1)}, bf16[2048,64]{1,0:T(8,128)(2,1)S(1)}) custom-call(s32[5]{0:T(128)S(1)} %pad_add_fusion.place_ref, bf16[256,2048]{1,0:T(8,128)(2,1)S(1)} %get-tuple-element.32.x_ref), custom_call_target="tpu_custom_call" | custom-call | flops 2147483648 | bytes 2097152 | tf_op jit(solution)/shard_map/derive/pallas_call | solution.py:378
  56.9 0.0 copy-start.7
  56.9 2.1 %copy-done.7 = bf16[36,256,256]{2,1,0:T(8,128)(2,1)} copy-done((bf16[36,256,256]{2,1,0:T(8,128)(2,1)}, bf16[36,256,256]{2,1,0:T(8,128)(2,1)S(1)}, u32[]{:S(2)}) %copy-start.7) | copy-done | bytes 4718616
  59.0 0.0 copy-start.9
  59.0 2.2 %copy-done.9 = bf16[36,256,256]{2,1,0:T(8,128)(2,1)} copy-done((bf16[36,256,256]{2,1,0:T(8,128)(2,1)}, bf16[36,256,256]{2,1,0:T(8,128)(2,1)S(1)}, u32[]{:S(2)}) %copy-start.9) | copy-done | bytes 4718616
  61.2 0.0 copy-start.11
  61.2 0.8 copy-done.11
  62.0 0.8 copy-done.13
  62.8 0.0 all-to-all-done.1.got_ref
  62.8 1.0 gated.1
  63.8 0.6 collective-permute-start.3
  64.4 0.0 collective-permute-done.4.d_ref
  64.4 1.0 collective-permute-done.3.b_ref
  65.3 1.7 %product.1 = bf16[512,1024]{1,0:T(8,128)(2,1)} custom-call(bf16[512,128]{1,0:T(8,128)(2,1)S(1)} %get-tuple-element.52.a_ref, bf16[512,128]{1,0:T(8,128)(2,1)S(1)} %collective-permute-done.3.b_ref, bf16[128,1024]{1,0:T(8,128)(2,1)S(1)} %copy-done.2, bf16[128,1024]{1,0:T(8,128)(2,1)S(1)} %collective-permute-done.4.d_ref), custom_call_target="tpu_custom_call" | custom-call | flops 67108864 | bytes 2097152 | tf_op jit(solution)/shard_map/product/pallas_call | solution.py:378
  67.0 8.9 %all-to-all-start.3 = ((bf16[32,16,1024]{2,1,0:T(8,128)(2,1)}), bf16[32,16,1024]{2,1,0:T(8,128)(2,1)}, u32[]{:S(2)}, u32[]{:S(2)}) async-start(bf16[32,16,1024]{2,1,0:T(8,128)(2,1)} %bitcast.2), calls=%async_computation.3 | async-start | bytes 2097152 | tf_op jit(solution)/shard_map/all_to_all | solution.py:517
  75.9 0.0 copy-start.8
  75.9 2.3 %copy-done.8 = bf16[36,256,256]{2,1,0:T(8,128)(2,1)S(1)} copy-done((bf16[36,256,256]{2,1,0:T(8,128)(2,1)S(1)}, bf16[36,256,256]{2,1,0:T(8,128)(2,1)}, u32[]{:S(2)}) %copy-start.8) | copy-done | bytes 4718616
  78.2 2.3 %copy-done.10 = bf16[36,256,256]{2,1,0:T(8,128)(2,1)S(1)} copy-done((bf16[36,256,256]{2,1,0:T(8,128)(2,1)S(1)}, bf16[36,256,256]{2,1,0:T(8,128)(2,1)}, u32[]{:S(2)}) %copy-start.10) | copy-done | bytes 4718616
  80.6 1.0 copy-done.12
  81.6 1.0 copy-done.14
  82.6 7.4 %attend_backward.1 = (bf16[8,192,128]{2,1,0:T(8,128)(2,1)S(1)}, bf16[8,192,128]{2,1,0:T(8,128)(2,1)S(1)}) custom-call(s32[5]{0:T(128)S(1)} %pad_add_fusion.place_ref, bf16[256,2048]{1,0:T(8,128)(2,1)S(1)} %get-tuple-element.32.x_ref, bf16[64,2048]{1,0:T(8,128)(2,1)S(1)} %get-tuple-element.33.attn_ref, bf16[16,144,128]{2,1,0:T(8,128)(2,1)S(1)} %all-to-all-done.1.got_ref, ...), custom_call_target="tpu_custom_call" | custom-call | flops 8589934592 | bytes 2097152 | tf_op jit(solution)/shard_map/attend_backward/pallas_call | solution.py:378
  90.0 0.1 collective-permute-start.2
  90.1 1.7 %collective-permute-done.2.theirs_ref = bf16[8,192,128]{2,1,0:T(8,128)(2,1)S(1)} collective-permute-done((bf16[8,192,128]{2,1,0:T(8,128)(2,1)S(1)}, bf16[8,192,128]{2,1,0:T(8,128)(2,1)S(1)}, u32[]{:S(2)}, u32[]{:S(2)}) %collective-permute-start.2) | collective-permute-done | bytes 393248 | tf_op jit(solution)/shard_map/ppermute | solution.py:481
  91.8 1.6 %grads_to_owners.1.after_ref = bf16[16,192,128]{2,1,0:T(8,128)(2,1)} custom-call(s32[5]{0:T(128)S(1)} %pad_add_fusion.place_ref, bf16[8,192,128]{2,1,0:T(8,128)(2,1)S(1)} %get-tuple-element.46.mine_ref, bf16[8,192,128]{2,1,0:T(8,128)(2,1)S(1)} %collective-permute-done.2.theirs_ref), custom_call_target="tpu_custom_call" | custom-call | flops 67108864 | bytes 2097152 | tf_op jit(solution)/shard_map/grads_to_owners/pallas_call | solution.py:378
  93.4 0.0 all-to-all-done.3
  93.4 7.2 %all-to-all-start.2 = ((bf16[16,192,128]{2,1,0:T(8,128)(2,1)}), bf16[16,192,128]{2,1,0:T(8,128)(2,1)S(1)}, u32[]{:S(2)}, u32[]{:S(2)}) async-start(bf16[16,192,128]{2,1,0:T(8,128)(2,1)} %grads_to_owners.1.after_ref), calls=%async_computation.2 | async-start | bytes 1572864 | tf_op jit(solution)/shard_map/all_to_all | solution.py:484
  100.6 1.1 d_gate.1
  101.8 1.4 %convert_reduce_fusion = f32[16,1024]{1,0:T(8,128)S(1)} fusion(bf16[32,16,1024]{2,1,0:T(8,128)(2,1)} %all-to-all-done.3), kind=kLoop, calls=%fused_computation | loop fusion | flops 1032192 | bytes 1114112 | tf_op jit(solution)/shard_map/reduce_sum | solution.py:538
  103.2 6.4 %collective-permute-start.5 = (f32[2,4,1024]{2,1,0:T(4,128)S(1)}, f32[2,4,1024]{2,1,0:T(4,128)S(1)}, u32[]{:S(2)}, u32[]{:S(2)}) collective-permute-start(f32[2,4,1024]{2,1,0:T(4,128)S(1)} %dynamic-slice_bitcast_fusion), channel_id=1, source_target_pairs={{0,128},{64,192},{128,0},{192,64},{1,129},{65,193},{129,1},{193,65... | collective-permute-start | bytes 98312 | tf_op jit(solution)/shard_map/ppermute | solution.py:545
  109.6 1.9 %collective-permute-done.5 = f32[2,4,1024]{2,1,0:T(4,128)S(1)} collective-permute-done((f32[2,4,1024]{2,1,0:T(4,128)S(1)}, f32[2,4,1024]{2,1,0:T(4,128)S(1)}, u32[]{:S(2)}, u32[]{:S(2)}) %collective-permute-start.5) | collective-permute-done | bytes 32800 | tf_op jit(solution)/shard_map/ppermute | solution.py:545
  111.5 3.0 %collective-permute-start.6 = (f32[1,4,1024]{2,1,0:T(4,128)S(1)}, f32[1,4,1024]{2,1,0:T(4,128)S(1)}, u32[]{:S(2)}, u32[]{:S(2)}) collective-permute-start(f32[1,4,1024]{2,1,0:T(4,128)S(1)} %constant_dynamic-slice_fusion), channel_id=1, source_target_pairs={{0,64},{64,0},{128,192},{192,128},{1,65},{65,1},{129,193},{193,129... | collective-permute-start | bytes 49160 | tf_op jit(solution)/shard_map/ppermute | solution.py:545
  114.5 0.0 all-to-all-done.2.got_ref
  114.5 1.0 finish.1
  115.5 0.7 collective-permute-done.6
  116.2 0.6 multiply_bitcast_fusion
  (8 shorter events, 0.1 us)
Async XLA Ops:
  0.6 1.6 %copy-start = (bf16[1024,1024]{1,0:T(8,128)(2,1)S(1)}, bf16[1024,1024]{1,0:T(8,128)(2,1)}, u32[]{:S(2)}) copy-start(bf16[1024,1024]{1,0:T(8,128)(2,1)} %w_in.1) | copy-start | bytes 6291460
  2.2 0.9 copy-start.1
  3.2 0.9 copy-start.3
  4.1 0.9 copy-start.4
  5.1 0.9 copy-start.5
  6.0 0.9 copy-start.6
  7.0 11.7 %copy-start.15 = (s32[1,4]{1,0:T(1,128)S(1)}, s32[1,4]{1,0:T(1,128)}, u32[]{:S(2)}) copy-start(s32[1,4]{1,0:T(1,128)} %param.13) | copy-start | bytes 52
  11.2 22.5 %all-to-all-start = ((bf16[16,256,128]{2,1,0:T(8,128)(2,1)}), bf16[16,256,128]{2,1,0:T(8,128)(2,1)S(1)}, u32[]{:S(2)}, u32[]{:S(2)}) async-start(bf16[16,256,128]{2,1,0:T(8,128)(2,1)} %get-tuple-element.31), calls=%async_computation | async-start | bytes 2097152 | tf_op jit(solution)/shard_map/all_to_all | solution.py:484
  34.4 15.9 %copy-start.2 = (bf16[128,1024]{1,0:T(8,128)(2,1)S(1)}, bf16[128,1024]{1,0:T(8,128)(2,1)}, u32[]{:S(2)}) copy-start(bf16[128,1024]{1,0:T(8,128)(2,1)} %c_ref.1) | copy-start | bytes 786436
  34.4 2.0 %collective-permute-start = (bf16[8,256,128]{2,1,0:T(8,128)(2,1)S(1)}, bf16[8,256,128]{2,1,0:T(8,128)(2,1)S(1)}, u32[]{:S(2)}, u32[]{:S(2)}) collective-permute-start(bf16[8,256,128]{2,1,0:T(8,128)(2,1)S(1)} %other_half.1), channel_id=1, source_target_pairs={{0,1},{1,0},{2,3},{3,2},{4,5},{5,4},{6,7},{7,6},{8,9},{9,8},{10,11... | collective-permute-start | bytes 1572872 | tf_op jit(solution)/shard_map/ppermute | solution.py:481
  41.3 1.4 %collective-permute-start.1 = (bf16[8,64,128]{2,1,0:T(8,128)(2,1)S(1)}, bf16[8,64,128]{2,1,0:T(8,128)(2,1)S(1)}, u32[]{:S(2)}, u32[]{:S(2)}) collective-permute-start(bf16[8,64,128]{2,1,0:T(8,128)(2,1)S(1)} %get-tuple-element.35), channel_id=1, source_target_pairs={{0,1},{1,0},{2,3},{3,2},{4,5},{5,4},{6,7},{7,6},{8,9},{9,8},{10,11... | collective-permute-start | bytes 393224 | tf_op jit(solution)/shard_map/ppermute | solution.py:481
  44.2 18.6 %all-to-all-start.1 = ((bf16[16,144,128]{2,1,0:T(8,128)(2,1)}), bf16[16,144,128]{2,1,0:T(8,128)(2,1)S(1)}, u32[]{:S(2)}, u32[]{:S(2)}) async-start(bf16[16,144,128]{2,1,0:T(8,128)(2,1)} %attn_to_owners.1), calls=%async_computation.1 | async-start | bytes 1179648 | tf_op jit(solution)/shard_map/all_to_all | solution.py:484
  50.3 14.1 %collective-permute-start.4 = (bf16[128,1024]{1,0:T(8,128)(2,1)S(1)}, bf16[128,1024]{1,0:T(8,128)(2,1)S(1)}, u32[]{:S(2)}, u32[]{:S(2)}) collective-permute-start(bf16[128,1024]{1,0:T(8,128)(2,1)S(1)} %copy-done.2), channel_id=1, source_target_pairs={{0,1},{1,0},{2,3},{3,2},{4,5},{5,4},{6,7},{7,6},{8,9},{9,8},{10,11... | collective-permute-start | bytes 786440 | tf_op jit(solution)/shard_map/ppermute | solution.py:481
  56.9 2.1 %copy-start.7 = (bf16[36,256,256]{2,1,0:T(8,128)(2,1)}, bf16[36,256,256]{2,1,0:T(8,128)(2,1)S(1)}, u32[]{:S(2)}) copy-start(bf16[36,256,256]{2,1,0:T(8,128)(2,1)S(1)} %get-tuple-element.42.silu_in) | copy-start | bytes 14155780
  59.0 2.2 %copy-start.9 = (bf16[36,256,256]{2,1,0:T(8,128)(2,1)}, bf16[36,256,256]{2,1,0:T(8,128)(2,1)S(1)}, u32[]{:S(2)}) copy-start(bf16[36,256,256]{2,1,0:T(8,128)(2,1)S(1)} %get-tuple-element.43.slope_in) | copy-start | bytes 14155780
  61.2 0.8 copy-start.11
  62.0 0.8 copy-start.13
  63.8 1.6 %collective-permute-start.3 = (bf16[512,128]{1,0:T(8,128)(2,1)S(1)}, bf16[512,128]{1,0:T(8,128)(2,1)S(1)}, u32[]{:S(2)}, u32[]{:S(2)}) collective-permute-start(bf16[512,128]{1,0:T(8,128)(2,1)S(1)} %get-tuple-element.53), channel_id=1, source_target_pairs={{0,1},{1,0},{2,3},{3,2},{4,5},{5,4},{6,7},{7,6},{8,9},{9,8},{10,11... | collective-permute-start | bytes 393224 | tf_op jit(solution)/shard_map/ppermute | solution.py:481
  67.0 26.4 %all-to-all-start.3 = ((bf16[32,16,1024]{2,1,0:T(8,128)(2,1)}), bf16[32,16,1024]{2,1,0:T(8,128)(2,1)}, u32[]{:S(2)}, u32[]{:S(2)}) async-start(bf16[32,16,1024]{2,1,0:T(8,128)(2,1)} %bitcast.2), calls=%async_computation.3 | async-start | bytes 2097152 | tf_op jit(solution)/shard_map/all_to_all | solution.py:517
  75.9 2.3 %copy-start.8 = (bf16[36,256,256]{2,1,0:T(8,128)(2,1)S(1)}, bf16[36,256,256]{2,1,0:T(8,128)(2,1)}, u32[]{:S(2)}) copy-start(bf16[36,256,256]{2,1,0:T(8,128)(2,1)} %copy-done.7) | copy-start | bytes 14155780
  78.2 2.3 %copy-start.10 = (bf16[36,256,256]{2,1,0:T(8,128)(2,1)S(1)}, bf16[36,256,256]{2,1,0:T(8,128)(2,1)}, u32[]{:S(2)}) copy-start(bf16[36,256,256]{2,1,0:T(8,128)(2,1)} %copy-done.9) | copy-start | bytes 14155780
  80.6 1.0 copy-start.12
  81.6 1.0 copy-start.14
  90.0 1.8 %collective-permute-start.2 = (bf16[8,192,128]{2,1,0:T(8,128)(2,1)S(1)}, bf16[8,192,128]{2,1,0:T(8,128)(2,1)S(1)}, u32[]{:S(2)}, u32[]{:S(2)}) collective-permute-start(bf16[8,192,128]{2,1,0:T(8,128)(2,1)S(1)} %get-tuple-element.47), channel_id=1, source_target_pairs={{0,1},{1,0},{2,3},{3,2},{4,5},{5,4},{6,7},{7,6},{8,9},{9,8},{10,11... | collective-permute-start | bytes 1179656 | tf_op jit(solution)/shard_map/ppermute | solution.py:481
  93.4 21.1 %all-to-all-start.2 = ((bf16[16,192,128]{2,1,0:T(8,128)(2,1)}), bf16[16,192,128]{2,1,0:T(8,128)(2,1)S(1)}, u32[]{:S(2)}, u32[]{:S(2)}) async-start(bf16[16,192,128]{2,1,0:T(8,128)(2,1)} %grads_to_owners.1.after_ref), calls=%async_computation.2 | async-start | bytes 1572864 | tf_op jit(solution)/shard_map/all_to_all | solution.py:484
  103.2 8.3 %collective-permute-start.5 = (f32[2,4,1024]{2,1,0:T(4,128)S(1)}, f32[2,4,1024]{2,1,0:T(4,128)S(1)}, u32[]{:S(2)}, u32[]{:S(2)}) collective-permute-start(f32[2,4,1024]{2,1,0:T(4,128)S(1)} %dynamic-slice_bitcast_fusion), channel_id=1, source_target_pairs={{0,128},{64,192},{128,0},{192,64},{1,129},{65,193},{129,1},{193,65... | collective-permute-start | bytes 98312 | tf_op jit(solution)/shard_map/ppermute | solution.py:545
  111.5 4.7 %collective-permute-start.6 = (f32[1,4,1024]{2,1,0:T(4,128)S(1)}, f32[1,4,1024]{2,1,0:T(4,128)S(1)}, u32[]{:S(2)}, u32[]{:S(2)}) collective-permute-start(f32[1,4,1024]{2,1,0:T(4,128)S(1)} %constant_dynamic-slice_fusion), channel_id=1, source_target_pairs={{0,64},{64,0},{128,192},{192,128},{1,65},{65,1},{129,193},{193,129... | collective-permute-start | bytes 49160 | tf_op jit(solution)/shard_map/ppermute | solution.py:545

commit v4 on v3

--- a/solution.py
+++ b/solution.py
@@ -17,6 +17,7 @@
 F_TILE = 2048
 B_TILE = 1024
 STATS = 5
+TILES_MIB = 45
 CHIP = ("x", "y")
 SWAP = ((0, 1), (1, 0))
 BF16 = jnp.bfloat16
@@ -71,7 +72,7 @@
 
 
 def forward_kernel(
-    place_ref, got_ref, other_ref, x_ref, attn_ref, mine_ref, theirs_ref, stat_ref, k_ref, slot_ref, stats_ref
+    place_ref, got_ref, other_ref, x_ref, mine_ref, theirs_ref, stat_ref, k_ref, slot_ref, stats_ref
 ):
     core, begin, turn, end1, end2 = place_of(place_ref)
     whole, rest = turn // BLOCK, turn % BLOCK
@@ -102,12 +103,12 @@
                 if (q, k) in weights:
                     k_sub = k_at + k * SUB
                     acc += dot(x_ref[128:192, k_sub : k_sub + SUB], weights[q, k])
-            attn_ref[:, q_sub : q_sub + SUB] = acc.astype(BF16)
+            x_ref[256:320, q_sub : q_sub + SUB] = acc.astype(BF16)
 
     turned = []
     for b in range(N_BLOCKS):
         cols = slice(b * BLOCK, (b + 1) * BLOCK)
-        attn = attn_ref[:, cols].astype(F32)
+        attn = x_ref[256:320, cols].astype(F32)
         g = x_ref[192:256, cols].astype(F32)
         mean = jnp.mean(attn, axis=0, keepdims=True)
         centre = attn - mean
@@ -141,62 +142,55 @@
 GROUPS = [[(q_at // SUB + q, k_at // SUB + k) for q, k in subs] for q_at, k_at, subs in below(HALF // B_TILE, B_TILE)]
 PAIRS = [pair for group in GROUPS for pair in group]
 AT = {pair: i for i, pair in enumerate(PAIRS)}
+ROWS_AT = 2 * len(PAIRS)
+Q_LANES, V_LANES = slice(0, 64), slice(128, 192)
 
 
 def group_copies(from_ref, to_ref, sems):
-    copies, at = [], 0
+    silu, slope, at = [], [], 0
     for i, group in enumerate(GROUPS):
-        part = pl.ds(at, len(group))
-        copies.append(pltpu.make_async_copy(from_ref.at[part], to_ref.at[part], sems.at[i]))
+        for j, copies in enumerate((silu, slope)):
+            part = pl.ds(j * len(PAIRS) + at, len(group))
+            copies.append(pltpu.make_async_copy(from_ref.at[part], to_ref.at[part], sems.at[j, i]))
         at += len(group)
-    return copies
+    part = pl.ds(ROWS_AT, HALF // SUB)
+    return silu, slope, pltpu.make_async_copy(from_ref.at[part], to_ref.at[part], sems.at[0, len(GROUPS)])
 
 
 def derive_kernel(
-    place_ref, x_ref, silu_out, slope_out, q_out, v_out,
-    silu_ref, slope_ref, qn_ref, kn_ref, vn_ref, silu_sems, slope_sems, sems,
+    place_ref, x_ref, tile_out, tile_ref, kn_ref, tile_sems
 ):
     end1, end2 = place_of(place_ref)[3:]
     for b in range(N_BLOCKS):
         cols = slice(b * BLOCK, (b + 1) * BLOCK)
-        for i, out_ref in enumerate((qn_ref, kn_ref, vn_ref)):
-            out_ref[cols, :] = x_ref[i * 64 : (i + 1) * 64, cols].T
-    copies = [
-        pltpu.make_async_copy(qn_ref, q_out, sems.at[0]),
-        pltpu.make_async_copy(vn_ref, v_out, sems.at[1]),
-    ]
-    for copy in copies:
-        copy.start()
-    silu_copies = group_copies(silu_ref, silu_out, silu_sems)
-    slope_copies = group_copies(slope_ref, slope_out, slope_sems)
+        rows = slice((b % 2) * BLOCK, (b % 2 + 1) * BLOCK)
+        tile_ref[ROWS_AT + b // 2, rows, Q_LANES] = x_ref[0:64, cols].T
+        tile_ref[ROWS_AT + b // 2, rows, V_LANES] = x_ref[128:192, cols].T
+        kn_ref[cols, :] = x_ref[64:128, cols].T
+    silu_copies, slope_copies, rows_copy = group_copies(tile_ref, tile_out, tile_sems)
+    rows_copy.start()
     for i, group in enumerate(GROUPS):
         for q, k in group:
             q_cols, k_cols = slice(q * SUB, (q + 1) * SUB), slice(k * SUB, (k + 1) * SUB)
             s = dot(kn_ref[k_cols, :], x_ref[0:64, q_cols])
             sigma = jnp.where(live_of(q * SUB, k * SUB, end1, end2, q == k), sigmoid(s), 0.0)
             silu = s * sigma
-            silu_ref[AT[q, k]] = silu.astype(BF16)
-            slope_ref[AT[q, k]] = (sigma + silu * (1.0 - sigma)).astype(BF16)
+            tile_ref[AT[q, k]] = silu.astype(BF16)
+            tile_ref[len(PAIRS) + AT[q, k]] = (sigma + silu * (1.0 - sigma)).astype(BF16)
         silu_copies[i].start()
         slope_copies[i].start()
-    for copy in copies + silu_copies + slope_copies:
+    for copy in [rows_copy] + silu_copies + slope_copies:
         copy.wait()
 
 
 def backward_kernel(
-    place_ref, x_ref, attn_ref, got_ref, silu_in, slope_in, q_in, v_in, mine_ref, theirs_ref,
-    silu_ref, slope_ref, qn_ref, vn_ref, dn_ref, dt_ref, dq_ref, dk_ref, dv_ref, slot_ref,
-    silu_sems, slope_sems, sems,
+    place_ref, x_ref, got_ref, tile_in, mine_ref, theirs_ref,
+    tile_ref, dn_ref, dt_ref, dq_ref, dk_ref, dv_ref, slot_ref,
+    tile_sems,
 ):
-    v_copy = pltpu.make_async_copy(v_in, vn_ref, sems.at[1])
-    q_copy = pltpu.make_async_copy(q_in, qn_ref, sems.at[0])
-    silu_copies = group_copies(silu_in, silu_ref, silu_sems)
-    slope_copies = group_copies(slope_in, slope_ref, slope_sems)
-    v_copy.start()
-    slope_copies[0].start()
-    silu_copies[0].start()
-    q_copy.start()
-    for i in range(1, len(GROUPS)):
+    silu_copies, slope_copies, rows_copy = group_copies(tile_in, tile_ref, tile_sems)
+    rows_copy.start()
+    for i in range(len(GROUPS)):
         slope_copies[i].start()
         silu_copies[i].start()
     core, _, turn, end1, end2 = place_of(place_ref)
@@ -212,12 +206,12 @@
     for b in range(N_BLOCKS):
         cols = slice(b * BLOCK, (b + 1) * BLOCK)
         r = rstd[b : b + 1]
-        normed = (attn_ref[:, cols].astype(F32) - mean[b : b + 1]) * r
+        normed = (x_ref[256:320, cols].astype(F32) - mean[b : b + 1]) * r
         d = (r * (x_ref[192:256, cols].astype(F32) - g_mean[b : b + 1] - normed * both[b : b + 1])).astype(BF16)
         dt_ref[:, cols] = d
         dn_ref[cols, :] = d.T
 
-    v_copy.wait()
+    rows_copy.wait()
     for i, (q_at, k_at, subs) in enumerate(below(HALF // B_TILE, B_TILE)):
         slope_copies[i].wait()
         n = B_TILE // SUB
@@ -226,19 +220,17 @@
         for q, k in subs:
             q_cols = slice(q_at + q * SUB, q_at + (q + 1) * SUB)
             k_cols = slice(k_at + k * SUB, k_at + (k + 1) * SUB)
-            d_p = dot(vn_ref[k_cols, :], dt_ref[:, q_cols])
-            made[q, k] = (d_p * slope_ref[AT[q_first + q, k_first + k]].astype(F32)).astype(BF16)
+            d_p = dot(tile_ref[ROWS_AT + k_first + k, :, V_LANES], dt_ref[:, q_cols])
+            made[q, k] = (d_p * tile_ref[len(PAIRS) + AT[q_first + q, k_first + k]].astype(F32)).astype(BF16)
         silu_copies[i].wait()
-        if i == 0:
-            q_copy.wait()
         for k in range(n):
             k_cols = slice(k_at + k * SUB, k_at + (k + 1) * SUB)
             d_v, d_k = [], []
             for q in range(n):
                 if (q, k) in made:
                     q_cols = slice(q_at + q * SUB, q_at + (q + 1) * SUB)
-                    d_v.append(dot(silu_ref[AT[q_first + q, k_first + k]], dn_ref[q_cols, :]))
-                    d_k.append(dot(made[q, k], qn_ref[q_cols, :]))
+                    d_v.append(dot(tile_ref[AT[q_first + q, k_first + k]], dn_ref[q_cols, :]))
+                    d_k.append(dot(made[q, k], tile_ref[ROWS_AT + q_first + q, :, Q_LANES]))
             if q_at == k_at:
                 dv_ref[k_cols, :], dk_ref[k_cols, :] = sum(d_v), sum(d_k)
             else:
@@ -381,7 +373,7 @@
         in_specs=in_specs,
         out_specs=jax.tree.map(lambda _: out, out_shape),
         scratch_shapes=list(scratch),
-        compiler_params=pltpu.CompilerParams(vmem_limit_bytes=mib * 1024 * 1024),
+        compiler_params=pltpu.CompilerParams(vmem_limit_bytes=None if mib is None else mib * 1024 * 1024),
         cost_estimate=pl.CostEstimate(flops=flops, bytes_accessed=1 << 21, transcendentals=transcendentals),
         name=name,
     )(*args)
@@ -404,7 +396,7 @@
         + [pltpu.VMEM(s.shape, s.dtype) for s in shapes]
         + [DMA((5,)), DMA((4,)), DMA((3, 4))],
         out=ANY,
-        mib=12,
+        mib=None,
     )
 
 
@@ -413,8 +405,7 @@
         forward_kernel,
         "attend_forward",
         (
-            shape((256, HALF)),
-            shape((HEAD_DIM, HALF)),
+            shape((320, HALF)),
             shape((8, HEAD_DIM, BLOCK)),
             shape((8, HEAD_DIM, BLOCK)),
             shape((STATS * N_BLOCKS, BLOCK)),
@@ -433,33 +424,31 @@
 
 
 def derive(place, x):
-    tiles, rows = (len(PAIRS), SUB, SUB), (HALF, HEAD_DIM)
+    tiles, rows = (ROWS_AT + HALF // SUB, SUB, SUB), (HALF, HEAD_DIM)
     return call(
         derive_kernel,
         "derive",
-        (shape(tiles), shape(tiles), shape(rows), shape(rows)),
+        shape(tiles),
         [SMEM, VMEM],
         (place, x),
-        [pltpu.VMEM(tiles, BF16)] * 2
-        + [pltpu.VMEM(rows, BF16)] * 3
-        + [DMA((len(GROUPS),)), DMA((len(GROUPS),)), DMA((2,))],
+        [pltpu.VMEM(tiles, BF16)]
+        + [pltpu.VMEM(rows, BF16), DMA((2, len(GROUPS) + 1))],
         out=ANY,
-        mib=24,
+        mib=TILES_MIB,
         flops=1 << 31,
         transcendentals=1 << 22,
     )
 
 
-def attend_backward(place, x, attn, got, derived):
-    tiles, rows = (len(PAIRS), SUB, SUB), (HALF, HEAD_DIM)
+def attend_backward(place, x, got, derived):
+    tiles, rows = (ROWS_AT + HALF // SUB, SUB, SUB), (HALF, HEAD_DIM)
     return call(
         backward_kernel,
         "attend_backward",
         (shape((8, 192, BLOCK)), shape((8, 192, BLOCK))),
-        [SMEM] + [VMEM] * 3 + [ANY] * 4,
-        (place, x, attn, got) + derived,
-        [pltpu.VMEM(tiles, BF16)] * 2
-        + [pltpu.VMEM(rows, BF16)] * 3
+        [SMEM, VMEM, VMEM, ANY],
+        (place, x, got, derived),
+        [pltpu.VMEM(tiles, BF16), pltpu.VMEM(rows, BF16)]
         + [
             pltpu.VMEM((HEAD_DIM, HALF), BF16),
             pltpu.VMEM((HEAD_DIM, HALF), F32),
@@ -467,8 +456,8 @@
             pltpu.VMEM(rows, F32),
             pltpu.VMEM((N_BLOCKS, 192, BLOCK), F32),
         ]
-        + [DMA((len(GROUPS),)), DMA((len(GROUPS),)), DMA((2,))],
-        mib=32,
+        + [DMA((2, len(GROUPS) + 1))],
+        mib=TILES_MIB,
         flops=1 << 33,
     )
 
@@ -486,7 +475,7 @@
     send, u_t, d_gated_t = prepare(query, key, value, gate_u, cotangent, out_weight)
     got = chips(send)
     theirs = call(other_half_kernel, "other_half", shape((8, 256, BLOCK)), [SMEM, VMEM], (place, got))
-    x, attn, mine, theirs, stat = attend_forward(place, got, swap(theirs))
+    x, mine, theirs, stat = attend_forward(place, got, swap(theirs))
 
     rows = HEAD_DIM + STATS * N_BLOCKS
     send = call(
@@ -516,7 +505,7 @@
     )
     parts = lax.all_to_all(part.reshape(32, 16, WIDTH), ("zl",) + CHIP, 0, 0, tiled=True)
 
-    mine, theirs = attend_backward(place, x, attn, got_attn, derived)
+    mine, theirs = attend_backward(place, x, got_attn, derived)
     send = call(
         to_owners_kernel,
         "grads_to_owners",

time: 118 us -> 105 us (0.89)
  local copies, waits for them, and re-layouts: 19.1 us -> 0.07 us
  waiting for transfers between devices: 23.4 us -> 31.6 us
  starting transfers between devices: 40.4 us -> 36.7 us
  Pallas kernels: 31.2 us -> 33 us
    unnamed x32 -> x8, local copies, waits for them, and re-layouts: 19 us -> 0.02 us
    all_to_all x1, waiting for transfers between devices: 0.01 us -> 4.38 us  [on_device(): lax.all_to_all(part.reshape(32, 16, WIDTH), ('zl',) + CHIP, 0, 0, tiled=T...]
    all_to_all x3, waiting for transfers between devices: 15 us -> 18.2 us  [chips(): return lax.all_to_all(x, CHIP, 0, 0, tiled=True)]
    all_to_all x3, starting transfers between devices: 20.8 us -> 18.6 us  [chips(): return lax.all_to_all(x, CHIP, 0, 0, tiled=True)]
    pallas_call x11, Pallas kernels: 31.2 us -> 33 us  [call(): pl.pallas_call(kernel, out_shape=out_shape, in_specs=in_specs, out_specs=...]
    all_to_all x1, starting transfers between devices: 8.85 us -> 7.42 us  [on_device(): lax.all_to_all(part.reshape(32, 16, WIDTH), ('zl',) + CHIP, 0, 0, tiled=T...]
  transfers between devices with their start and end apart: 11 -> 11, of which waited for: 7 -> 9; matrix products, arithmetic and copies ran while one was open for 1% -> 1% of each run, Pallas kernels for 16% -> 19%
where the time goes in v4:
time: 105 us; the launch traced here: 104 us
  starting transfers between devices  36.7 us (35%)
  Pallas kernels  33 us (31%)
  waiting for transfers between devices  31.6 us (30%)
  other arithmetic  2.09 us (2%)
    pallas_call x11, Pallas kernels, call(): pl.pallas_call(kernel, out_shape=out_shape, in_specs=in_specs, out_specs=...  33 us
    all_to_all x3, starting transfers between devices, chips(): return lax.all_to_all(x, CHIP, 0, 0, tiled=True)  18.6 us
    all_to_all x3, waiting for transfers between devices, chips(): return lax.all_to_all(x, CHIP, 0, 0, tiled=True)  18.2 us
    ppermute x2, starting transfers between devices, on_device(): part = kept + lax.ppermute(away, 'zh', [(i, i ^ step) for i in range(4)])  9.7 us
    all_to_all x1, starting transfers between devices, on_device(): lax.all_to_all(part.reshape(32, 16, WIDTH), ('zl',) + CHIP, 0, 0, tiled=T...  7.42 us
    ppermute x5, waiting for transfers between devices, swap(): return lax.ppermute(x, 'core', SWAP)  6.14 us
    all_to_all x1, waiting for transfers between devices, on_device(): lax.all_to_all(part.reshape(32, 16, WIDTH), ('zl',) + CHIP, 0, 0, tiled=T...  4.38 us
    ppermute x2, waiting for transfers between devices, on_device(): part = kept + lax.ppermute(away, 'zh', [(i, i ^ step) for i in range(4)])  2.87 us
  transfers between devices with their start and end apart: 11, of which 9 were waited for; matrix products, arithmetic and copies ran while one was open for 1% of the time, Pallas kernels for 19%

profile of v4, /device:TPU:2, one launch (start us, length us, event | category | flops | bytes accessed | tf_op | source)
XLA Modules:
  0.0 104.2 jit_solution(877925202085005365)
XLA Ops:
  0.6 0.0 copy-start.3
  0.6 4.4 %prepare.1 = (bf16[16,256,128]{2,1,0:T(8,128)(2,1)}, bf16[1024,128]{1,0:T(8,128)(2,1)}, f32[1024,128]{1,0:T(8,128)}) custom-call(bf16[128,1024]{1,0:T(8,128)(2,1)} %q_in.1, bf16[128,1024]{1,0:T(8,128)(2,1)} %k_in.1, bf16[128,1024]{1,0:T(8,128)(2,1)} %v_in.1, bf16[128,1024]{1,0:T(8,128)(2,1)} %u_in.1, bf16[128,1024]{1,0:T(8,128)(2,1)} %c_ref.1, ...), custom_call_target="tpu_custom_call" | custom-call | flops 67108864 | bytes 2097152 | tf_op jit(solution)/shard_map/prepare/pallas_call | solution.py:370
  5.1 7.5 %all-to-all-start = ((bf16[16,256,128]{2,1,0:T(8,128)(2,1)}), bf16[16,256,128]{2,1,0:T(8,128)(2,1)S(1)}, u32[]{:S(2)}, u32[]{:S(2)}) async-start(bf16[16,256,128]{2,1,0:T(8,128)(2,1)} %get-tuple-element.23), calls=%async_computation | async-start | bytes 2097152 | tf_op jit(solution)/shard_map/all_to_all | solution.py:473
  12.6 0.0 copy-done.3
  12.6 0.1 pad_add_fusion.place_ref
  12.7 15.0 %all-to-all-done.got_ref = bf16[16,256,128]{2,1,0:T(8,128)(2,1)S(1)} async-done(((bf16[16,256,128]{2,1,0:T(8,128)(2,1)}), bf16[16,256,128]{2,1,0:T(8,128)(2,1)S(1)}, u32[]{:S(2)}, u32[]{:S(2)}) %all-to-all-start) | async-done | bytes 1048608 | tf_op jit(solution)/shard_map/all_to_all | solution.py:473
  27.6 0.7 other_half.1
  28.3 0.0 copy-start
  28.3 0.1 collective-permute-start
  28.4 1.9 %collective-permute-done.other_ref = bf16[8,256,128]{2,1,0:T(8,128)(2,1)S(1)} collective-permute-done((bf16[8,256,128]{2,1,0:T(8,128)(2,1)S(1)}, bf16[8,256,128]{2,1,0:T(8,128)(2,1)S(1)}, u32[]{:S(2)}, u32[]{:S(2)}) %collective-permute-start) | collective-permute-done | bytes 524320 | tf_op jit(solution)/shard_map/ppermute | solution.py:470
  30.3 4.9 %attend_forward.1 = (bf16[320,2048]{1,0:T(8,128)(2,1)S(1)}, bf16[8,64,128]{2,1,0:T(8,128)(2,1)S(1)}, bf16[8,64,128]{2,1,0:T(8,128)(2,1)S(1)}, bf16[80,128]{1,0:T(8,128)(2,1)S(1)}) custom-call(s32[5]{0:T(128)S(1)} %pad_add_fusion.place_ref, bf16[16,256,128]{2,1,0:T(8,128)(2,1)S(1)} %all-to-all-done.got_ref, ...), custom_call_target="tpu_custom_call" | custom-call | flops 1073741824 | bytes 2097152 | tf_op jit(solution)/shard_map/attend_forward/pallas_call | solution.py:370
  35.3 0.2 collective-permute-start.1
  35.5 1.2 %collective-permute-done.1.theirs_ref = bf16[8,64,128]{2,1,0:T(8,128)(2,1)S(1)} collective-permute-done((bf16[8,64,128]{2,1,0:T(8,128)(2,1)S(1)}, bf16[8,64,128]{2,1,0:T(8,128)(2,1)S(1)}, u32[]{:S(2)}, u32[]{:S(2)}) %collective-permute-start.1) | collective-permute-done | bytes 131104 | tf_op jit(solution)/shard_map/ppermute | solution.py:470
  36.7 1.5 %attn_to_owners.1 = bf16[16,144,128]{2,1,0:T(8,128)(2,1)} custom-call(s32[5]{0:T(128)S(1)} %pad_add_fusion.place_ref, bf16[8,64,128]{2,1,0:T(8,128)(2,1)S(1)} %get-tuple-element.25.mine_ref, bf16[8,64,128]{2,1,0:T(8,128)(2,1)S(1)} %collective-permute-done.1.theirs_ref, bf16[80,128]{1,0:T(8,128)(2,1)S(1)} %get-tuple-element.27.stat_ref), custom_call_target="tpu_custom_call" | custom-call | flops 67108864 | bytes 2097152 | tf_op jit(solution)/shard_map/attn_to_owners/pallas_call | solution.py:370
  38.2 6.1 %all-to-all-start.1 = ((bf16[16,144,128]{2,1,0:T(8,128)(2,1)}), bf16[16,144,128]{2,1,0:T(8,128)(2,1)S(1)}, u32[]{:S(2)}, u32[]{:S(2)}) async-start(bf16[16,144,128]{2,1,0:T(8,128)(2,1)} %attn_to_owners.1), calls=%async_computation.1 | async-start | bytes 1179648 | tf_op jit(solution)/shard_map/all_to_all | solution.py:473
  44.3 0.0 copy-done
  44.3 0.3 collective-permute-start.4
  44.6 0.0 copy-start.2
  44.6 7.0 %derive.1.tile_in = bf16[80,256,256]{2,1,0:T(8,128)(2,1)} custom-call(s32[5]{0:T(128)S(1)} %pad_add_fusion.place_ref, bf16[320,2048]{1,0:T(8,128)(2,1)S(1)} %get-tuple-element.24.x_ref), custom_call_target="tpu_custom_call" | custom-call | flops 2147483648 | bytes 2097152 | tf_op jit(solution)/shard_map/derive/pallas_call | solution.py:370
  51.6 3.2 %all-to-all-done.1.got_ref = bf16[16,144,128]{2,1,0:T(8,128)(2,1)S(1)} async-done(((bf16[16,144,128]{2,1,0:T(8,128)(2,1)}), bf16[16,144,128]{2,1,0:T(8,128)(2,1)S(1)}, u32[]{:S(2)}, u32[]{:S(2)}) %all-to-all-start.1) | async-done | bytes 589856 | tf_op jit(solution)/shard_map/all_to_all | solution.py:473
  54.8 0.0 copy-done.2
  54.8 1.0 gated.1
  55.8 0.1 collective-permute-start.3
  55.9 0.0 collective-permute-done.4.d_ref
  55.9 1.3 %collective-permute-done.3.b_ref = bf16[512,128]{1,0:T(8,128)(2,1)S(1)} collective-permute-done((bf16[512,128]{1,0:T(8,128)(2,1)S(1)}, bf16[512,128]{1,0:T(8,128)(2,1)S(1)}, u32[]{:S(2)}, u32[]{:S(2)}) %collective-permute-start.3) | collective-permute-done | bytes 131104 | tf_op jit(solution)/shard_map/ppermute | solution.py:470
  57.2 1.7 %product.1 = bf16[512,1024]{1,0:T(8,128)(2,1)} custom-call(bf16[512,128]{1,0:T(8,128)(2,1)S(1)} %get-tuple-element.36.a_ref, bf16[512,128]{1,0:T(8,128)(2,1)S(1)} %collective-permute-done.3.b_ref, bf16[128,1024]{1,0:T(8,128)(2,1)S(1)} %copy-done, bf16[128,1024]{1,0:T(8,128)(2,1)S(1)} %collective-permute-done.4.d_ref), custom_call_target="tpu_custom_call" | custom-call | flops 67108864 | bytes 2097152 | tf_op jit(solution)/shard_map/product/pallas_call | solution.py:370
  58.9 7.4 %all-to-all-start.3 = ((bf16[32,16,1024]{2,1,0:T(8,128)(2,1)}), bf16[32,16,1024]{2,1,0:T(8,128)(2,1)}, u32[]{:S(2)}, u32[]{:S(2)}) async-start(bf16[32,16,1024]{2,1,0:T(8,128)(2,1)} %bitcast.2), calls=%async_computation.3 | async-start | bytes 2097152 | tf_op jit(solution)/shard_map/all_to_all | solution.py:506
  66.3 8.1 %attend_backward.1 = (bf16[8,192,128]{2,1,0:T(8,128)(2,1)S(1)}, bf16[8,192,128]{2,1,0:T(8,128)(2,1)S(1)}) custom-call(s32[5]{0:T(128)S(1)} %pad_add_fusion.place_ref, bf16[320,2048]{1,0:T(8,128)(2,1)S(1)} %get-tuple-element.24.x_ref, bf16[16,144,128]{2,1,0:T(8,128)(2,1)S(1)} %all-to-all-done.1.got_ref, bf16[80,256,256]{2,1,0:T(8,128)(2,1)} %derive.1.tile_in), custom_call_target="tpu_custom_call" | custom-call | flops 8589934592 | bytes 2097152 | tf_op jit(solution)/shard_map/attend_backward/pallas_call | solution.py:370
  74.5 0.0 copy-start.1
  74.5 0.3 collective-permute-start.2
  74.8 1.7 %collective-permute-done.2.theirs_ref = bf16[8,192,128]{2,1,0:T(8,128)(2,1)S(1)} collective-permute-done((bf16[8,192,128]{2,1,0:T(8,128)(2,1)S(1)}, bf16[8,192,128]{2,1,0:T(8,128)(2,1)S(1)}, u32[]{:S(2)}, u32[]{:S(2)}) %collective-permute-start.2) | collective-permute-done | bytes 393248 | tf_op jit(solution)/shard_map/ppermute | solution.py:470
  76.5 1.6 %grads_to_owners.1.after_ref = bf16[16,192,128]{2,1,0:T(8,128)(2,1)} custom-call(s32[5]{0:T(128)S(1)} %pad_add_fusion.place_ref, bf16[8,192,128]{2,1,0:T(8,128)(2,1)S(1)} %get-tuple-element.30.mine_ref, bf16[8,192,128]{2,1,0:T(8,128)(2,1)S(1)} %collective-permute-done.2.theirs_ref), custom_call_target="tpu_custom_call" | custom-call | flops 67108864 | bytes 2097152 | tf_op jit(solution)/shard_map/grads_to_owners/pallas_call | solution.py:370
  78.1 4.4 %all-to-all-done.3 = bf16[32,16,1024]{2,1,0:T(8,128)(2,1)} async-done(((bf16[32,16,1024]{2,1,0:T(8,128)(2,1)}), bf16[32,16,1024]{2,1,0:T(8,128)(2,1)}, u32[]{:S(2)}, u32[]{:S(2)}) %all-to-all-start.3) | async-done | bytes 1048608 | tf_op jit(solution)/shard_map/all_to_all | solution.py:506
  82.4 4.9 %all-to-all-start.2 = ((bf16[16,192,128]{2,1,0:T(8,128)(2,1)}), bf16[16,192,128]{2,1,0:T(8,128)(2,1)S(1)}, u32[]{:S(2)}, u32[]{:S(2)}) async-start(bf16[16,192,128]{2,1,0:T(8,128)(2,1)} %grads_to_owners.1.after_ref), calls=%async_computation.2 | async-start | bytes 1572864 | tf_op jit(solution)/shard_map/all_to_all | solution.py:473
  87.4 0.0 copy-done.1
  87.4 1.1 %d_gate.1 = bf16[128,1024]{1,0:T(8,128)(2,1)} custom-call(bf16[16,144,128]{2,1,0:T(8,128)(2,1)S(1)} %all-to-all-done.1.got_ref, f32[1024,128]{1,0:T(8,128)S(1)} %copy-done.1, bf16[16,192,128]{2,1,0:T(8,128)(2,1)} %grads_to_owners.1.after_ref), custom_call_target="tpu_custom_call" | custom-call | flops 1048576 | bytes 2097152 | tf_op jit(solution)/shard_map/d_gate/pallas_call | solution.py:370
  88.5 1.4 %convert_reduce_fusion = f32[16,1024]{1,0:T(8,128)S(1)} fusion(bf16[32,16,1024]{2,1,0:T(8,128)(2,1)} %all-to-all-done.3), kind=kLoop, calls=%fused_computation | loop fusion | flops 1032192 | bytes 1114112 | tf_op jit(solution)/shard_map/reduce_sum | solution.py:527
  89.9 6.9 %collective-permute-start.5 = (f32[2,4,1024]{2,1,0:T(4,128)S(1)}, f32[2,4,1024]{2,1,0:T(4,128)S(1)}, u32[]{:S(2)}, u32[]{:S(2)}) collective-permute-start(f32[2,4,1024]{2,1,0:T(4,128)S(1)} %dynamic-slice_bitcast_fusion), channel_id=1, source_target_pairs={{0,128},{64,192},{128,0},{192,64},{1,129},{65,193},{129,1},{193,65... | collective-permute-start | bytes 98312 | tf_op jit(solution)/shard_map/ppermute | solution.py:534
  96.9 1.9 %collective-permute-done.5 = f32[2,4,1024]{2,1,0:T(4,128)S(1)} collective-permute-done((f32[2,4,1024]{2,1,0:T(4,128)S(1)}, f32[2,4,1024]{2,1,0:T(4,128)S(1)}, u32[]{:S(2)}, u32[]{:S(2)}) %collective-permute-start.5) | collective-permute-done | bytes 32800 | tf_op jit(solution)/shard_map/ppermute | solution.py:534
  98.8 2.8 %collective-permute-start.6 = (f32[1,4,1024]{2,1,0:T(4,128)S(1)}, f32[1,4,1024]{2,1,0:T(4,128)S(1)}, u32[]{:S(2)}, u32[]{:S(2)}) collective-permute-start(f32[1,4,1024]{2,1,0:T(4,128)S(1)} %constant_dynamic-slice_fusion), channel_id=1, source_target_pairs={{0,64},{64,0},{128,192},{192,128},{1,65},{65,1},{129,193},{193,129... | collective-permute-start | bytes 49160 | tf_op jit(solution)/shard_map/ppermute | solution.py:534
  101.6 0.0 all-to-all-done.2.got_ref
  101.6 1.0 finish.1
  102.6 0.9 collective-permute-done.6
  103.6 0.6 multiply_bitcast_fusion
  (4 shorter events, 0.1 us)
Async XLA Ops:
  0.6 12.0 %copy-start.3 = (s32[1,4]{1,0:T(1,128)S(1)}, s32[1,4]{1,0:T(1,128)}, u32[]{:S(2)}) copy-start(s32[1,4]{1,0:T(1,128)} %param.13) | copy-start | bytes 52
  5.1 22.5 %all-to-all-start = ((bf16[16,256,128]{2,1,0:T(8,128)(2,1)}), bf16[16,256,128]{2,1,0:T(8,128)(2,1)S(1)}, u32[]{:S(2)}, u32[]{:S(2)}) async-start(bf16[16,256,128]{2,1,0:T(8,128)(2,1)} %get-tuple-element.23), calls=%async_computation | async-start | bytes 2097152 | tf_op jit(solution)/shard_map/all_to_all | solution.py:473
  28.3 16.0 %copy-start = (bf16[128,1024]{1,0:T(8,128)(2,1)S(1)}, bf16[128,1024]{1,0:T(8,128)(2,1)}, u32[]{:S(2)}) copy-start(bf16[128,1024]{1,0:T(8,128)(2,1)} %c_ref.1) | copy-start | bytes 786436
  28.3 2.0 %collective-permute-start = (bf16[8,256,128]{2,1,0:T(8,128)(2,1)S(1)}, bf16[8,256,128]{2,1,0:T(8,128)(2,1)S(1)}, u32[]{:S(2)}, u32[]{:S(2)}) collective-permute-start(bf16[8,256,128]{2,1,0:T(8,128)(2,1)S(1)} %other_half.1), channel_id=1, source_target_pairs={{0,1},{1,0},{2,3},{3,2},{4,5},{5,4},{6,7},{7,6},{8,9},{9,8},{10,11... | collective-permute-start | bytes 1572872 | tf_op jit(solution)/shard_map/ppermute | solution.py:470
  35.3 1.4 %collective-permute-start.1 = (bf16[8,64,128]{2,1,0:T(8,128)(2,1)S(1)}, bf16[8,64,128]{2,1,0:T(8,128)(2,1)S(1)}, u32[]{:S(2)}, u32[]{:S(2)}) collective-permute-start(bf16[8,64,128]{2,1,0:T(8,128)(2,1)S(1)} %get-tuple-element.26), channel_id=1, source_target_pairs={{0,1},{1,0},{2,3},{3,2},{4,5},{5,4},{6,7},{7,6},{8,9},{9,8},{10,11... | collective-permute-start | bytes 393224 | tf_op jit(solution)/shard_map/ppermute | solution.py:470
  38.2 16.6 %all-to-all-start.1 = ((bf16[16,144,128]{2,1,0:T(8,128)(2,1)}), bf16[16,144,128]{2,1,0:T(8,128)(2,1)S(1)}, u32[]{:S(2)}, u32[]{:S(2)}) async-start(bf16[16,144,128]{2,1,0:T(8,128)(2,1)} %attn_to_owners.1), calls=%async_computation.1 | async-start | bytes 1179648 | tf_op jit(solution)/shard_map/all_to_all | solution.py:473
  44.3 11.6 %collective-permute-start.4 = (bf16[128,1024]{1,0:T(8,128)(2,1)S(1)}, bf16[128,1024]{1,0:T(8,128)(2,1)S(1)}, u32[]{:S(2)}, u32[]{:S(2)}) collective-permute-start(bf16[128,1024]{1,0:T(8,128)(2,1)S(1)} %copy-done), channel_id=1, source_target_pairs={{0,1},{1,0},{2,3},{3,2},{4,5},{5,4},{6,7},{7,6},{8,9},{9,8},{10,11... | collective-permute-start | bytes 786440 | tf_op jit(solution)/shard_map/ppermute | solution.py:470
  44.6 10.2 %copy-start.2 = (bf16[1024,128]{1,0:T(8,128)(2,1)S(1)}, bf16[1024,128]{1,0:T(8,128)(2,1)}, u32[]{:S(2)}) copy-start(bf16[1024,128]{1,0:T(8,128)(2,1)} %get-tuple-element.35.ut_ref) | copy-start | bytes 786436
  55.8 1.4 %collective-permute-start.3 = (bf16[512,128]{1,0:T(8,128)(2,1)S(1)}, bf16[512,128]{1,0:T(8,128)(2,1)S(1)}, u32[]{:S(2)}, u32[]{:S(2)}) collective-permute-start(bf16[512,128]{1,0:T(8,128)(2,1)S(1)} %get-tuple-element.37), channel_id=1, source_target_pairs={{0,1},{1,0},{2,3},{3,2},{4,5},{5,4},{6,7},{7,6},{8,9},{9,8},{10,11... | collective-permute-start | bytes 393224 | tf_op jit(solution)/shard_map/ppermute | solution.py:470
  58.9 23.5 %all-to-all-start.3 = ((bf16[32,16,1024]{2,1,0:T(8,128)(2,1)}), bf16[32,16,1024]{2,1,0:T(8,128)(2,1)}, u32[]{:S(2)}, u32[]{:S(2)}) async-start(bf16[32,16,1024]{2,1,0:T(8,128)(2,1)} %bitcast.2), calls=%async_computation.3 | async-start | bytes 2097152 | tf_op jit(solution)/shard_map/all_to_all | solution.py:506
  74.5 12.9 %copy-start.1 = (f32[1024,128]{1,0:T(8,128)S(1)}, f32[1024,128]{1,0:T(8,128)}, u32[]{:S(2)}) copy-start(f32[1024,128]{1,0:T(8,128)} %get-tuple-element.38.dg_ref) | copy-start | bytes 1572868
  74.5 2.0 %collective-permute-start.2 = (bf16[8,192,128]{2,1,0:T(8,128)(2,1)S(1)}, bf16[8,192,128]{2,1,0:T(8,128)(2,1)S(1)}, u32[]{:S(2)}, u32[]{:S(2)}) collective-permute-start(bf16[8,192,128]{2,1,0:T(8,128)(2,1)S(1)} %get-tuple-element.31), channel_id=1, source_target_pairs={{0,1},{1,0},{2,3},{3,2},{4,5},{5,4},{6,7},{7,6},{8,9},{9,8},{10,11... | collective-permute-start | bytes 1179656 | tf_op jit(solution)/shard_map/ppermute | solution.py:470
  82.4 19.2 %all-to-all-start.2 = ((bf16[16,192,128]{2,1,0:T(8,128)(2,1)}), bf16[16,192,128]{2,1,0:T(8,128)(2,1)S(1)}, u32[]{:S(2)}, u32[]{:S(2)}) async-start(bf16[16,192,128]{2,1,0:T(8,128)(2,1)} %grads_to_owners.1.after_ref), calls=%async_computation.2 | async-start | bytes 1572864 | tf_op jit(solution)/shard_map/all_to_all | solution.py:473
  89.9 8.8 %collective-permute-start.5 = (f32[2,4,1024]{2,1,0:T(4,128)S(1)}, f32[2,4,1024]{2,1,0:T(4,128)S(1)}, u32[]{:S(2)}, u32[]{:S(2)}) collective-permute-start(f32[2,4,1024]{2,1,0:T(4,128)S(1)} %dynamic-slice_bitcast_fusion), channel_id=1, source_target_pairs={{0,128},{64,192},{128,0},{192,64},{1,129},{65,193},{129,1},{193,65... | collective-permute-start | bytes 98312 | tf_op jit(solution)/shard_map/ppermute | solution.py:534
  98.8 4.7 %collective-permute-start.6 = (f32[1,4,1024]{2,1,0:T(4,128)S(1)}, f32[1,4,1024]{2,1,0:T(4,128)S(1)}, u32[]{:S(2)}, u32[]{:S(2)}) collective-permute-start(f32[1,4,1024]{2,1,0:T(4,128)S(1)} %constant_dynamic-slice_fusion), channel_id=1, source_target_pairs={{0,64},{64,0},{128,192},{192,128},{1,65},{65,1},{129,193},{193,129... | collective-permute-start | bytes 49160 | tf_op jit(solution)/shard_map/ppermute | solution.py:534

commit v5 on v4

--- a/solution.py
+++ b/solution.py
@@ -313,10 +313,19 @@
         out_ref[8 + j] = jnp.where(low_mine, theirs, mine)
 
 
-def attn_to_owners_kernel(place_ref, mine_ref, theirs_ref, stat_ref, out_ref):
-    to_owners_kernel(place_ref, mine_ref, theirs_ref, out_ref.at[:, 0:64, :])
-    for j in range(HEADS):
-        out_ref[j, 64:, :] = stat_ref[...]
+def attn_to_owners_kernel(place_ref, mine_ref, theirs_ref, stat_ref, out, out_ref, sems):
+    core, begin = place_of(place_ref)[:2]
+    copies = [pltpu.make_async_copy(out_ref.at[j], out.at[j], sems.at[j]) for j in range(HEADS)]
+    for j in range(8):
+        low_mine = low_is_mine(j, core, begin)
+        mine, theirs = mine_ref[j], theirs_ref[j]
+        out_ref[j, 0:64, :] = jnp.where(low_mine, mine, theirs)
+        out_ref[8 + j, 0:64, :] = jnp.where(low_mine, theirs, mine)
+        for i in (j, 8 + j):
+            out_ref[i, 64:, :] = stat_ref[...]
+            copies[i].start()
+    for copy in copies:
+        copy.wait()
 
 
 def normalised(got_ref):
@@ -325,8 +334,8 @@
     return centre * lax.rsqrt(jnp.mean(centre * centre, axis=0, keepdims=True) + 1e-05)
 
 
-def gated_kernel(place_ref, got_ref, ut_ref, mine_ref, theirs_ref, zero_ref, one_ref):
-    core = place_ref[4]
+def gated_kernel(place_ref, got_ref, ut_ref, keep_ref, core_ref, z_ref, both_ref, half_ref):
+    core, zl = place_ref[4], place_ref[5]
     gated = normalised(got_ref) * ut_ref[...].astype(F32)
     for z in (0, 1, 4, 5):
         for chip in range(HEADS):
@@ -334,11 +343,10 @@
             one, two = gated[at : at + 8], gated[at + 2 * BLOCK : at + 2 * BLOCK + 8]
             row = (z % 2) * 256 + chip * 16 + (z // 2) * 4
             rows = slice(row, row + 8)
-            zero_ref[rows, :] = jnp.concatenate([one[0:4], two[0:4]], axis=0)
-            one_ref[rows, :] = jnp.concatenate([one[4:8], two[4:8]], axis=0)
-    zero, one = zero_ref[...].astype(BF16), one_ref[...].astype(BF16)
-    mine_ref[...] = jnp.where(core == 0, zero, one)
-    theirs_ref[...] = jnp.where(core == 0, one, zero)
+            half_ref[0, rows, :] = jnp.concatenate([one[0:4], two[0:4]], axis=0)
+            half_ref[1, rows, :] = jnp.concatenate([one[4:8], two[4:8]], axis=0)
+    for c, z, out_ref in ((core, zl, keep_ref), (1 - core, zl, core_ref), (core, 1 - zl, z_ref), (1 - core, 1 - zl, both_ref)):
+        out_ref[...] = half_ref[c, pl.ds(pl.multiple_of(z * 256, 256), 256), :].astype(BF16)
 
 
 def d_gate_kernel(got_ref, dg_ref, after_ref, out_ref):
@@ -347,10 +355,17 @@
         out_ref[:, i * BLOCK : (i + 1) * BLOCK] = d_gate[i * BLOCK : (i + 1) * BLOCK].T
 
 
-def product_kernel(a_ref, b_ref, c_ref, d_ref, out_ref):
-    for at in range(0, 512, 128):
-        rows = slice(at, at + 128)
-        out_ref[rows, :] = (dot(a_ref[rows, :], c_ref[...]) + dot(b_ref[rows, :], d_ref[...])).astype(BF16)
+def product_kernel(*refs):
+    gated, cotangent, (out, out_ref, sems) = refs[0:4], refs[4:8], refs[8:]
+    copies = []
+    for i in range(2):
+        rows = slice(i * 128, (i + 1) * 128)
+        out_ref[rows, :] = sum(dot(a[rows, :], b[...]) for a, b in zip(gated, cotangent)).astype(BF16)
+        part = pl.ds(i * 128, 128)
+        copies.append(pltpu.make_async_copy(out_ref.at[part], out.at[part], sems.at[i]))
+        copies[i].start()
+    for copy in copies:
+        copy.wait()
 
 
 def finish_kernel(got_ref, dq_ref, dk_ref, dv_ref):
@@ -464,7 +479,7 @@
 
 def on_device(query, key, value, gate_u, out_weight, cotangent, hist_lengths):
     core = lax.axis_index("core")
-    place = jnp.concatenate([hist_lengths[0], core[None]]).astype(jnp.int32)
+    place = jnp.concatenate([hist_lengths[0], core[None], lax.axis_index("zl")[None]]).astype(jnp.int32)
 
     def swap(x):
         return lax.ppermute(x, "core", SWAP)
@@ -484,26 +499,36 @@
         shape((HEADS, rows, BLOCK)),
         [SMEM] + [VMEM] * 3,
         (place, mine, swap(theirs), stat),
+        [pltpu.VMEM((HEADS, rows, BLOCK), BF16), DMA((HEADS,))],
+        out=ANY,
     )
     got_attn = chips(send)
     got_attn, derived = lax.optimization_barrier((got_attn, derive(place, x)))
 
-    mine, theirs = call(
+    def four(parts):
+        return [parts[0]] + [
+            lax.ppermute(part, ("zl", "core"), [(i, i ^ step) for i in range(4)])
+            for step, part in zip((1, 2, 3), parts[1:])
+        ]
+
+    gated = call(
         gated_kernel,
         "gated",
-        (shape((512, BLOCK)), shape((512, BLOCK))),
+        (shape((256, BLOCK)),) * 4,
         [SMEM] + [VMEM] * 2,
         (place, got_attn, u_t),
-        [pltpu.VMEM((512, BLOCK), F32)] * 2,
+        [pltpu.VMEM((2, 512, BLOCK), F32)],
     )
     part = call(
         product_kernel,
         "product",
-        shape((512, WIDTH)),
-        [VMEM] * 4,
-        (mine, swap(theirs), cotangent, swap(cotangent)),
-    )
-    parts = lax.all_to_all(part.reshape(32, 16, WIDTH), ("zl",) + CHIP, 0, 0, tiled=True)
+        shape((256, WIDTH)),
+        [VMEM] * 8,
+        four(gated) + four([cotangent] * 4),
+        [pltpu.VMEM((256, WIDTH), BF16), DMA((2,))],
+        out=ANY,
+    )
+    parts = chips(part.reshape(HEADS, 16, WIDTH))
 
     mine, theirs = attend_backward(place, x, got_attn, derived)
     send = call(
@@ -523,7 +548,7 @@
         flops=1 << 20,
     )
 
-    parts, d_gate = lax.optimization_barrier((parts, d_gate))
+    parts, _ = lax.optimization_barrier((parts, send))
     part = jnp.sum(parts.astype(F32), axis=0).reshape(4, 4, WIDTH)
     z = lax.axis_index("zh")
     for step in (2, 1):

time: 105 us -> 105 us (level)
  starting transfers between devices: 36.7 us -> 41.9 us
  waiting for transfers between devices: 31.6 us -> 28 us
  other arithmetic: 2.09 us -> 0.78 us
    all_to_all x3 -> x4, starting transfers between devices: 18.6 us -> 27.6 us  [chips(): return lax.all_to_all(x, CHIP, 0, 0, tiled=True)]
    all_to_all x1 -> x0, starting transfers between devices: 7.42 us -> none  [on_device(): lax.all_to_all(part.reshape(32, 16, WIDTH), ('zl',) + CHIP, 0, 0, tiled=T...]
    all_to_all x1 -> x0, waiting for transfers between devices: 4.38 us -> none  [on_device(): lax.all_to_all(part.reshape(32, 16, WIDTH), ('zl',) + CHIP, 0, 0, tiled=T...]
    ppermute x0 -> x6, starting transfers between devices: none -> 4.28 us  [four(): lax.ppermute(part, ('zl', 'core'), [(i, i ^ step) for i in range(4)])]
    ppermute x0 -> x6, waiting for transfers between devices: none -> 4.02 us  [four(): lax.ppermute(part, ('zl', 'core'), [(i, i ^ step) for i in range(4)])]
    all_to_all x3 -> x4, waiting for transfers between devices: 18.2 us -> 16.3 us  [chips(): return lax.all_to_all(x, CHIP, 0, 0, tiled=True)]
    ppermute x5 -> x3, waiting for transfers between devices: 6.14 us -> 4.78 us  [swap(): return lax.ppermute(x, 'core', SWAP)]
    reduce_sum x1, other arithmetic: 1.39 us -> 0.08 us  [on_device(): part = jnp.sum(parts.astype(F32), axis=0).reshape(4, 4, WIDTH)]
  transfers between devices with their start and end apart: 11 -> 15, of which waited for: 9 -> 10; matrix products, arithmetic and copies ran while one was open for 1% -> 1% of each run, Pallas kernels for 19% -> 18%
where the time goes in v5:
time: 105 us; the launch traced here: 104 us
  starting transfers between devices  41.9 us (40%)
  Pallas kernels  32.7 us (31%)
  waiting for transfers between devices  28 us (27%)
    pallas_call x11, Pallas kernels, call(): pl.pallas_call(kernel, out_shape=out_shape, in_specs=in_specs, out_specs=...  32.7 us
    all_to_all x4, starting transfers between devices, chips(): return lax.all_to_all(x, CHIP, 0, 0, tiled=True)  27.6 us
    all_to_all x4, waiting for transfers between devices, chips(): return lax.all_to_all(x, CHIP, 0, 0, tiled=True)  16.3 us
    ppermute x2, starting transfers between devices, on_device(): part = kept + lax.ppermute(away, 'zh', [(i, i ^ step) for i in range(4)])  9.64 us
    ppermute x3, waiting for transfers between devices, swap(): return lax.ppermute(x, 'core', SWAP)  4.78 us
    ppermute x6, starting transfers between devices, four(): lax.ppermute(part, ('zl', 'core'), [(i, i ^ step) for i in range(4)])  4.28 us
    ppermute x6, waiting for transfers between devices, four(): lax.ppermute(part, ('zl', 'core'), [(i, i ^ step) for i in range(4)])  4.02 us
    ppermute x2, waiting for transfers between devices, on_device(): part = kept + lax.ppermute(away, 'zh', [(i, i ^ step) for i in range(4)])  2.91 us
  transfers between devices with their start and end apart: 15, of which 10 were waited for; matrix products, arithmetic and copies ran while one was open for 1% of the time, Pallas kernels for 18%

profile of v5, /device:TPU:2, one launch (start us, length us, event | category | flops | bytes accessed | tf_op | source)
XLA Modules:
  0.0 104.3 jit_solution(16887477432893454656)
XLA Ops:
  0.6 0.0 copy-start.3
  0.6 4.4 %prepare.1 = (bf16[16,256,128]{2,1,0:T(8,128)(2,1)}, bf16[1024,128]{1,0:T(8,128)(2,1)}, f32[1024,128]{1,0:T(8,128)}) custom-call(bf16[128,1024]{1,0:T(8,128)(2,1)} %q_in.1, bf16[128,1024]{1,0:T(8,128)(2,1)} %k_in.1, bf16[128,1024]{1,0:T(8,128)(2,1)} %v_in.1, bf16[128,1024]{1,0:T(8,128)(2,1)} %u_in.1, bf16[128,1024]{1,0:T(8,128)(2,1)} %refs_4_.1, ...), custom_call_target="tpu_custom_call" | custom-call | flops 67108864 | bytes 2097152 | tf_op jit(solution)/shard_map/prepare/pallas_call | solution.py:385
  5.1 7.5 %all-to-all-start = ((bf16[16,256,128]{2,1,0:T(8,128)(2,1)}), bf16[16,256,128]{2,1,0:T(8,128)(2,1)S(1)}, u32[]{:S(2)}, u32[]{:S(2)}) async-start(bf16[16,256,128]{2,1,0:T(8,128)(2,1)} %get-tuple-element.24), calls=%async_computation | async-start | bytes 2097152 | tf_op jit(solution)/shard_map/all_to_all | solution.py:488
  12.6 0.0 copy-done.3
  12.6 0.1 pad_add_fusion.place_ref
  12.7 15.0 %all-to-all-done.got_ref = bf16[16,256,128]{2,1,0:T(8,128)(2,1)S(1)} async-done(((bf16[16,256,128]{2,1,0:T(8,128)(2,1)}), bf16[16,256,128]{2,1,0:T(8,128)(2,1)S(1)}, u32[]{:S(2)}, u32[]{:S(2)}) %all-to-all-start) | async-done | bytes 1048608 | tf_op jit(solution)/shard_map/all_to_all | solution.py:488
  27.6 0.7 other_half.1
  28.3 0.0 copy-start
  28.3 0.1 collective-permute-start
  28.4 1.9 %collective-permute-done.other_ref = bf16[8,256,128]{2,1,0:T(8,128)(2,1)S(1)} collective-permute-done((bf16[8,256,128]{2,1,0:T(8,128)(2,1)S(1)}, bf16[8,256,128]{2,1,0:T(8,128)(2,1)S(1)}, u32[]{:S(2)}, u32[]{:S(2)}) %collective-permute-start) | collective-permute-done | bytes 524320 | tf_op jit(solution)/shard_map/ppermute | solution.py:485
  30.3 4.9 %attend_forward.1 = (bf16[320,2048]{1,0:T(8,128)(2,1)S(1)}, bf16[8,64,128]{2,1,0:T(8,128)(2,1)S(1)}, bf16[8,64,128]{2,1,0:T(8,128)(2,1)S(1)}, bf16[80,128]{1,0:T(8,128)(2,1)S(1)}) custom-call(s32[6]{0:T(128)S(1)} %pad_add_fusion.place_ref, bf16[16,256,128]{2,1,0:T(8,128)(2,1)S(1)} %all-to-all-done.got_ref, ...), custom_call_target="tpu_custom_call" | custom-call | flops 1073741824 | bytes 2097152 | tf_op jit(solution)/shard_map/attend_forward/pallas_call | solution.py:385
  35.2 0.2 collective-permute-start.1
  35.4 1.2 %collective-permute-done.1.theirs_ref = bf16[8,64,128]{2,1,0:T(8,128)(2,1)S(1)} collective-permute-done((bf16[8,64,128]{2,1,0:T(8,128)(2,1)S(1)}, bf16[8,64,128]{2,1,0:T(8,128)(2,1)S(1)}, u32[]{:S(2)}, u32[]{:S(2)}) %collective-permute-start.1) | collective-permute-done | bytes 131104 | tf_op jit(solution)/shard_map/ppermute | solution.py:485
  36.6 1.5 %attn_to_owners.1 = bf16[16,144,128]{2,1,0:T(8,128)(2,1)} custom-call(s32[6]{0:T(128)S(1)} %pad_add_fusion.place_ref, bf16[8,64,128]{2,1,0:T(8,128)(2,1)S(1)} %get-tuple-element.26.mine_ref, bf16[8,64,128]{2,1,0:T(8,128)(2,1)S(1)} %collective-permute-done.1.theirs_ref, bf16[80,128]{1,0:T(8,128)(2,1)S(1)} %get-tuple-element.28.stat_ref), custom_call_target="tpu_custom_call" | custom-call | flops 67108864 | bytes 2097152 | tf_op jit(solution)/shard_map/attn_to_owners/pallas_call | solution.py:385
  38.2 6.1 %all-to-all-start.1 = ((bf16[16,144,128]{2,1,0:T(8,128)(2,1)}), bf16[16,144,128]{2,1,0:T(8,128)(2,1)S(1)}, u32[]{:S(2)}, u32[]{:S(2)}) async-start(bf16[16,144,128]{2,1,0:T(8,128)(2,1)} %attn_to_owners.1), calls=%async_computation.1 | async-start | bytes 1179648 | tf_op jit(solution)/shard_map/all_to_all | solution.py:488
  44.3 0.0 copy-done
  44.3 0.1 collective-permute-start.6
  44.4 2.0 %collective-permute-start.7 = (bf16[128,1024]{1,0:T(8,128)(2,1)S(1)}, bf16[128,1024]{1,0:T(8,128)(2,1)S(1)}, u32[]{:S(2)}, u32[]{:S(2)}) collective-permute-start(bf16[128,1024]{1,0:T(8,128)(2,1)S(1)} %copy-done), channel_id=1, source_target_pairs={{0,32},{1,33},{32,0},{33,1},{2,34},{3,35},{34,2},{35,3},{4,36},{5,... | collective-permute-start | bytes 786440 | tf_op jit(solution)/shard_map/ppermute | solution.py:510
  46.4 0.1 collective-permute-start.8
  46.5 0.0 copy-start.2
  46.5 7.0 %derive.1.tile_in = bf16[80,256,256]{2,1,0:T(8,128)(2,1)} custom-call(s32[6]{0:T(128)S(1)} %pad_add_fusion.place_ref, bf16[320,2048]{1,0:T(8,128)(2,1)S(1)} %get-tuple-element.25.x_ref), custom_call_target="tpu_custom_call" | custom-call | flops 2147483648 | bytes 2097152 | tf_op jit(solution)/shard_map/derive/pallas_call | solution.py:385
  53.5 1.3 %all-to-all-done.1.got_ref = bf16[16,144,128]{2,1,0:T(8,128)(2,1)S(1)} async-done(((bf16[16,144,128]{2,1,0:T(8,128)(2,1)}), bf16[16,144,128]{2,1,0:T(8,128)(2,1)S(1)}, u32[]{:S(2)}, u32[]{:S(2)}) %all-to-all-start.1) | async-done | bytes 589856 | tf_op jit(solution)/shard_map/all_to_all | solution.py:488
  54.8 0.0 copy-done.2
  54.8 1.0 gated.1
  55.8 0.1 collective-permute-start.3
  55.9 2.0 %collective-permute-start.4 = (bf16[256,128]{1,0:T(8,128)(2,1)S(1)}, bf16[256,128]{1,0:T(8,128)(2,1)S(1)}, u32[]{:S(2)}, u32[]{:S(2)}) collective-permute-start(bf16[256,128]{1,0:T(8,128)(2,1)S(1)} %get-tuple-element.40), channel_id=1, source_target_pairs={{0,32},{1,33},{32,0},{33,1},{2,34},{3,35},{34,2},{35,3},{4,36},{5,... | collective-permute-start | bytes 196616 | tf_op jit(solution)/shard_map/ppermute | solution.py:510
  57.9 0.0 collective-permute-done.6.refs_5_
  57.9 0.0 collective-permute-start.5
  58.0 0.0 collective-permute-done.7.refs_6_
  58.0 0.6 collective-permute-done.8.refs_7_
  58.6 0.0 collective-permute-done.3.refs_1_
  58.6 2.0 %collective-permute-done.4.refs_2_ = bf16[256,128]{1,0:T(8,128)(2,1)S(1)} collective-permute-done((bf16[256,128]{1,0:T(8,128)(2,1)S(1)}, bf16[256,128]{1,0:T(8,128)(2,1)S(1)}, u32[]{:S(2)}, u32[]{:S(2)}) %collective-permute-start.4) | collective-permute-done | bytes 65568 | tf_op jit(solution)/shard_map/ppermute | solution.py:510
  60.6 1.4 %collective-permute-done.5.refs_3_ = bf16[256,128]{1,0:T(8,128)(2,1)S(1)} collective-permute-done((bf16[256,128]{1,0:T(8,128)(2,1)S(1)}, bf16[256,128]{1,0:T(8,128)(2,1)S(1)}, u32[]{:S(2)}, u32[]{:S(2)}) %collective-permute-start.5) | collective-permute-done | bytes 65568 | tf_op jit(solution)/shard_map/ppermute | solution.py:510
  62.0 1.4 %product.1 = bf16[256,1024]{1,0:T(8,128)(2,1)} custom-call(bf16[256,128]{1,0:T(8,128)(2,1)S(1)} %get-tuple-element.38.refs_0_, bf16[256,128]{1,0:T(8,128)(2,1)S(1)} %collective-permute-done.3.refs_1_, bf16[256,128]{1,0:T(8,128)(2,1)S(1)} %collective-permute-done.4.refs_2_, bf16[256,128]{1,0:T(8,128)(2,1)S(1)} %collective-permute-done.5.refs_3_, ...), custom_call_target="tpu_custom_call" | custom-call | flops 67108864 | bytes 2097152 | tf_op jit(solution)/shard_map/product/pallas_call | solution.py:385
  63.4 6.7 %all-to-all-start.3 = ((bf16[16,16,1024]{2,1,0:T(8,128)(2,1)}), bf16[16,16,1024]{2,1,0:T(8,128)(2,1)S(1)}, u32[]{:S(2)}, u32[]{:S(2)}) async-start(bf16[16,16,1024]{2,1,0:T(8,128)(2,1)} %bitcast.3), calls=%async_computation.3 | async-start | bytes 1048576 | tf_op jit(solution)/shard_map/all_to_all | solution.py:488
  70.1 8.1 %attend_backward.1 = (bf16[8,192,128]{2,1,0:T(8,128)(2,1)S(1)}, bf16[8,192,128]{2,1,0:T(8,128)(2,1)S(1)}) custom-call(s32[6]{0:T(128)S(1)} %pad_add_fusion.place_ref, bf16[320,2048]{1,0:T(8,128)(2,1)S(1)} %get-tuple-element.25.x_ref, bf16[16,144,128]{2,1,0:T(8,128)(2,1)S(1)} %all-to-all-done.1.got_ref, bf16[80,256,256]{2,1,0:T(8,128)(2,1)} %derive.1.tile_in), custom_call_target="tpu_custom_call" | custom-call | flops 8589934592 | bytes 2097152 | tf_op jit(solution)/shard_map/attend_backward/pallas_call | solution.py:385
  78.2 0.0 copy-start.1
  78.2 0.1 collective-permute-start.2
  78.3 1.7 %collective-permute-done.2.theirs_ref = bf16[8,192,128]{2,1,0:T(8,128)(2,1)S(1)} collective-permute-done((bf16[8,192,128]{2,1,0:T(8,128)(2,1)S(1)}, bf16[8,192,128]{2,1,0:T(8,128)(2,1)S(1)}, u32[]{:S(2)}, u32[]{:S(2)}) %collective-permute-start.2) | collective-permute-done | bytes 393248 | tf_op jit(solution)/shard_map/ppermute | solution.py:485
  80.0 1.6 %grads_to_owners.1.after_ref = bf16[16,192,128]{2,1,0:T(8,128)(2,1)} custom-call(s32[6]{0:T(128)S(1)} %pad_add_fusion.place_ref, bf16[8,192,128]{2,1,0:T(8,128)(2,1)S(1)} %get-tuple-element.31.mine_ref, bf16[8,192,128]{2,1,0:T(8,128)(2,1)S(1)} %collective-permute-done.2.theirs_ref), custom_call_target="tpu_custom_call" | custom-call | flops 67108864 | bytes 2097152 | tf_op jit(solution)/shard_map/grads_to_owners/pallas_call | solution.py:385
  81.6 0.0 all-to-all-done.3
  81.6 7.2 %all-to-all-start.2 = ((bf16[16,192,128]{2,1,0:T(8,128)(2,1)}), bf16[16,192,128]{2,1,0:T(8,128)(2,1)S(1)}, u32[]{:S(2)}, u32[]{:S(2)}) async-start(bf16[16,192,128]{2,1,0:T(8,128)(2,1)} %grads_to_owners.1.after_ref), calls=%async_computation.2 | async-start | bytes 1572864 | tf_op jit(solution)/shard_map/all_to_all | solution.py:488
  88.8 0.1 convert_reduce_fusion
  88.9 7.0 %collective-permute-start.9 = (f32[2,4,1024]{2,1,0:T(4,128)S(1)}, f32[2,4,1024]{2,1,0:T(4,128)S(1)}, u32[]{:S(2)}, u32[]{:S(2)}) collective-permute-start(f32[2,4,1024]{2,1,0:T(4,128)S(1)} %dynamic-slice_bitcast_fusion), channel_id=1, source_target_pairs={{0,128},{64,192},{128,0},{192,64},{1,129},{65,193},{129,1},{193,65... | collective-permute-start | bytes 98312 | tf_op jit(solution)/shard_map/ppermute | solution.py:559
  95.9 2.0 %collective-permute-done.9 = f32[2,4,1024]{2,1,0:T(4,128)S(1)} collective-permute-done((f32[2,4,1024]{2,1,0:T(4,128)S(1)}, f32[2,4,1024]{2,1,0:T(4,128)S(1)}, u32[]{:S(2)}, u32[]{:S(2)}) %collective-permute-start.9) | collective-permute-done | bytes 32800 | tf_op jit(solution)/shard_map/ppermute | solution.py:559
  97.9 2.7 %collective-permute-start.10 = (f32[1,4,1024]{2,1,0:T(4,128)S(1)}, f32[1,4,1024]{2,1,0:T(4,128)S(1)}, u32[]{:S(2)}, u32[]{:S(2)}) collective-permute-start(f32[1,4,1024]{2,1,0:T(4,128)S(1)} %constant_dynamic-slice_fusion), channel_id=1, source_target_pairs={{0,64},{64,0},{128,192},{192,128},{1,65},{65,1},{129,193},{193,129... | collective-permute-start | bytes 49160 | tf_op jit(solution)/shard_map/ppermute | solution.py:559
  100.6 0.0 copy-done.1
  100.6 1.1 %d_gate.1 = bf16[128,1024]{1,0:T(8,128)(2,1)} custom-call(bf16[16,144,128]{2,1,0:T(8,128)(2,1)S(1)} %all-to-all-done.1.got_ref, f32[1024,128]{1,0:T(8,128)S(1)} %copy-done.1, bf16[16,192,128]{2,1,0:T(8,128)(2,1)} %grads_to_owners.1.after_ref), custom_call_target="tpu_custom_call" | custom-call | flops 1048576 | bytes 2097152 | tf_op jit(solution)/shard_map/d_gate/pallas_call | solution.py:385
  101.7 0.9 collective-permute-done.10
  102.6 0.6 multiply_bitcast_fusion
  103.3 0.0 all-to-all-done.2.got_ref
  103.3 1.0 finish.1
  (4 shorter events, 0.1 us)
Async XLA Ops:
  0.6 11.9 %copy-start.3 = (s32[1,4]{1,0:T(1,128)S(1)}, s32[1,4]{1,0:T(1,128)}, u32[]{:S(2)}) copy-start(s32[1,4]{1,0:T(1,128)} %param.13) | copy-start | bytes 52
  5.1 22.5 %all-to-all-start = ((bf16[16,256,128]{2,1,0:T(8,128)(2,1)}), bf16[16,256,128]{2,1,0:T(8,128)(2,1)S(1)}, u32[]{:S(2)}, u32[]{:S(2)}) async-start(bf16[16,256,128]{2,1,0:T(8,128)(2,1)} %get-tuple-element.24), calls=%async_computation | async-start | bytes 2097152 | tf_op jit(solution)/shard_map/all_to_all | solution.py:488
  28.3 16.0 %copy-start = (bf16[128,1024]{1,0:T(8,128)(2,1)S(1)}, bf16[128,1024]{1,0:T(8,128)(2,1)}, u32[]{:S(2)}) copy-start(bf16[128,1024]{1,0:T(8,128)(2,1)} %refs_4_.1) | copy-start | bytes 786436
  28.3 2.0 %collective-permute-start = (bf16[8,256,128]{2,1,0:T(8,128)(2,1)S(1)}, bf16[8,256,128]{2,1,0:T(8,128)(2,1)S(1)}, u32[]{:S(2)}, u32[]{:S(2)}) collective-permute-start(bf16[8,256,128]{2,1,0:T(8,128)(2,1)S(1)} %other_half.1), channel_id=1, source_target_pairs={{0,1},{1,0},{2,3},{3,2},{4,5},{5,4},{6,7},{7,6},{8,9},{9,8},{10,11... | collective-permute-start | bytes 1572872 | tf_op jit(solution)/shard_map/ppermute | solution.py:485
  35.2 1.4 %collective-permute-start.1 = (bf16[8,64,128]{2,1,0:T(8,128)(2,1)S(1)}, bf16[8,64,128]{2,1,0:T(8,128)(2,1)S(1)}, u32[]{:S(2)}, u32[]{:S(2)}) collective-permute-start(bf16[8,64,128]{2,1,0:T(8,128)(2,1)S(1)} %get-tuple-element.27), channel_id=1, source_target_pairs={{0,1},{1,0},{2,3},{3,2},{4,5},{5,4},{6,7},{7,6},{8,9},{9,8},{10,11... | collective-permute-start | bytes 393224 | tf_op jit(solution)/shard_map/ppermute | solution.py:485
  38.2 16.7 %all-to-all-start.1 = ((bf16[16,144,128]{2,1,0:T(8,128)(2,1)}), bf16[16,144,128]{2,1,0:T(8,128)(2,1)S(1)}, u32[]{:S(2)}, u32[]{:S(2)}) async-start(bf16[16,144,128]{2,1,0:T(8,128)(2,1)} %attn_to_owners.1), calls=%async_computation.1 | async-start | bytes 1179648 | tf_op jit(solution)/shard_map/all_to_all | solution.py:488
  44.3 13.6 %collective-permute-start.6 = (bf16[128,1024]{1,0:T(8,128)(2,1)S(1)}, bf16[128,1024]{1,0:T(8,128)(2,1)S(1)}, u32[]{:S(2)}, u32[]{:S(2)}) collective-permute-start(bf16[128,1024]{1,0:T(8,128)(2,1)S(1)} %copy-done), channel_id=1, source_target_pairs={{0,1},{1,0},{32,33},{33,32},{2,3},{3,2},{34,35},{35,34},{4,5},{5,4... | collective-permute-start | bytes 786440 | tf_op jit(solution)/shard_map/ppermute | solution.py:510
  44.4 13.5 %collective-permute-start.7 = (bf16[128,1024]{1,0:T(8,128)(2,1)S(1)}, bf16[128,1024]{1,0:T(8,128)(2,1)S(1)}, u32[]{:S(2)}, u32[]{:S(2)}) collective-permute-start(bf16[128,1024]{1,0:T(8,128)(2,1)S(1)} %copy-done), channel_id=1, source_target_pairs={{0,32},{1,33},{32,0},{33,1},{2,34},{3,35},{34,2},{35,3},{4,36},{5,... | collective-permute-start | bytes 786440 | tf_op jit(solution)/shard_map/ppermute | solution.py:510
  46.4 12.2 %collective-permute-start.8 = (bf16[128,1024]{1,0:T(8,128)(2,1)S(1)}, bf16[128,1024]{1,0:T(8,128)(2,1)S(1)}, u32[]{:S(2)}, u32[]{:S(2)}) collective-permute-start(bf16[128,1024]{1,0:T(8,128)(2,1)S(1)} %copy-done), channel_id=1, source_target_pairs={{0,33},{1,32},{32,1},{33,0},{2,35},{3,34},{34,3},{35,2},{4,37},{5,... | collective-permute-start | bytes 786440 | tf_op jit(solution)/shard_map/ppermute | solution.py:510
  46.5 8.4 %copy-start.2 = (bf16[1024,128]{1,0:T(8,128)(2,1)S(1)}, bf16[1024,128]{1,0:T(8,128)(2,1)}, u32[]{:S(2)}) copy-start(bf16[1024,128]{1,0:T(8,128)(2,1)} %get-tuple-element.37.ut_ref) | copy-start | bytes 786436
  55.8 2.8 %collective-permute-start.3 = (bf16[256,128]{1,0:T(8,128)(2,1)S(1)}, bf16[256,128]{1,0:T(8,128)(2,1)S(1)}, u32[]{:S(2)}, u32[]{:S(2)}) collective-permute-start(bf16[256,128]{1,0:T(8,128)(2,1)S(1)} %get-tuple-element.39), channel_id=1, source_target_pairs={{0,1},{1,0},{32,33},{33,32},{2,3},{3,2},{34,35},{35,34},{4,5},{5,4... | collective-permute-start | bytes 196616 | tf_op jit(solution)/shard_map/ppermute | solution.py:510
  55.9 4.7 %collective-permute-start.4 = (bf16[256,128]{1,0:T(8,128)(2,1)S(1)}, bf16[256,128]{1,0:T(8,128)(2,1)S(1)}, u32[]{:S(2)}, u32[]{:S(2)}) collective-permute-start(bf16[256,128]{1,0:T(8,128)(2,1)S(1)} %get-tuple-element.40), channel_id=1, source_target_pairs={{0,32},{1,33},{32,0},{33,1},{2,34},{3,35},{34,2},{35,3},{4,36},{5,... | collective-permute-start | bytes 196616 | tf_op jit(solution)/shard_map/ppermute | solution.py:510
  57.9 4.1 %collective-permute-start.5 = (bf16[256,128]{1,0:T(8,128)(2,1)S(1)}, bf16[256,128]{1,0:T(8,128)(2,1)S(1)}, u32[]{:S(2)}, u32[]{:S(2)}) collective-permute-start(bf16[256,128]{1,0:T(8,128)(2,1)S(1)} %get-tuple-element.41), channel_id=1, source_target_pairs={{0,33},{1,32},{32,1},{33,0},{2,35},{3,34},{34,3},{35,2},{4,37},{5,... | collective-permute-start | bytes 196616 | tf_op jit(solution)/shard_map/ppermute | solution.py:510
  63.4 18.2 %all-to-all-start.3 = ((bf16[16,16,1024]{2,1,0:T(8,128)(2,1)}), bf16[16,16,1024]{2,1,0:T(8,128)(2,1)S(1)}, u32[]{:S(2)}, u32[]{:S(2)}) async-start(bf16[16,16,1024]{2,1,0:T(8,128)(2,1)} %bitcast.3), calls=%async_computation.3 | async-start | bytes 1048576 | tf_op jit(solution)/shard_map/all_to_all | solution.py:488
  78.2 22.4 %copy-start.1 = (f32[1024,128]{1,0:T(8,128)S(1)}, f32[1024,128]{1,0:T(8,128)}, u32[]{:S(2)}) copy-start(f32[1024,128]{1,0:T(8,128)} %get-tuple-element.36.dg_ref) | copy-start | bytes 1572868
  78.2 1.8 %collective-permute-start.2 = (bf16[8,192,128]{2,1,0:T(8,128)(2,1)S(1)}, bf16[8,192,128]{2,1,0:T(8,128)(2,1)S(1)}, u32[]{:S(2)}, u32[]{:S(2)}) collective-permute-start(bf16[8,192,128]{2,1,0:T(8,128)(2,1)S(1)} %get-tuple-element.32), channel_id=1, source_target_pairs={{0,1},{1,0},{2,3},{3,2},{4,5},{5,4},{6,7},{7,6},{8,9},{9,8},{10,11... | collective-permute-start | bytes 1179656 | tf_op jit(solution)/shard_map/ppermute | solution.py:485
  81.6 21.7 %all-to-all-start.2 = ((bf16[16,192,128]{2,1,0:T(8,128)(2,1)}), bf16[16,192,128]{2,1,0:T(8,128)(2,1)S(1)}, u32[]{:S(2)}, u32[]{:S(2)}) async-start(bf16[16,192,128]{2,1,0:T(8,128)(2,1)} %grads_to_owners.1.after_ref), calls=%async_computation.2 | async-start | bytes 1572864 | tf_op jit(solution)/shard_map/all_to_all | solution.py:488
  88.9 8.9 %collective-permute-start.9 = (f32[2,4,1024]{2,1,0:T(4,128)S(1)}, f32[2,4,1024]{2,1,0:T(4,128)S(1)}, u32[]{:S(2)}, u32[]{:S(2)}) collective-permute-start(f32[2,4,1024]{2,1,0:T(4,128)S(1)} %dynamic-slice_bitcast_fusion), channel_id=1, source_target_pairs={{0,128},{64,192},{128,0},{192,64},{1,129},{65,193},{129,1},{193,65... | collective-permute-start | bytes 98312 | tf_op jit(solution)/shard_map/ppermute | solution.py:559
  97.9 4.7 %collective-permute-start.10 = (f32[1,4,1024]{2,1,0:T(4,128)S(1)}, f32[1,4,1024]{2,1,0:T(4,128)S(1)}, u32[]{:S(2)}, u32[]{:S(2)}) collective-permute-start(f32[1,4,1024]{2,1,0:T(4,128)S(1)} %constant_dynamic-slice_fusion), channel_id=1, source_target_pairs={{0,64},{64,0},{128,192},{192,128},{1,65},{65,1},{129,193},{193,129... | collective-permute-start | bytes 49160 | tf_op jit(solution)/shard_map/ppermute | solution.py:559

commit v6 on v5

--- a/solution.py
+++ b/solution.py
@@ -255,30 +255,23 @@
 
 
 def prepare_kernel(
-    q_in, k_in, v_in, u_in, cot_in, w_in, send_out, ut_out, dg_out,
-    q_ref, k_ref, v_ref, u_ref, cot_ref, w_ref, send_ref, ut_ref, dg_ref, in_sems, w_sems, out_sems,
+    q_in, k_in, v_in, u_in, cot_in, w_in, send_out, dg_out,
+    q_ref, k_ref, v_ref, u_ref, cot_ref, w_ref, qkv_ref, g_ref, dg_ref, in_sems, w_sems, qkv_sems, g_sems, dg_sems,
 ):
     pairs = (q_in, q_ref), (k_in, k_ref), (v_in, v_ref), (cot_in, cot_ref), (u_in, u_ref)
     copies = [pltpu.make_async_copy(a, b, in_sems.at[i]) for i, (a, b) in enumerate(pairs)]
     parts = [pl.ds(at, 256) for at in range(0, WIDTH, 256)]
-    heads = [pl.ds(at, 4) for at in range(0, HEADS, 4)]
     w_copies = [pltpu.make_async_copy(w_in.at[part], w_ref.at[part], w_sems.at[i]) for i, part in enumerate(parts)]
-    outs = [
-        [
-            pltpu.make_async_copy(send_ref.at[heads[i]], send_out.at[heads[i]], out_sems.at[0, i]),
-            pltpu.make_async_copy(ut_ref.at[parts[i]], ut_out.at[parts[i]], out_sems.at[1, i]),
-            pltpu.make_async_copy(dg_ref.at[parts[i]], dg_out.at[parts[i]], out_sems.at[2, i]),
-        ]
+    qkv_copies = [
+        pltpu.make_async_copy(qkv_ref.at[i], send_out.at[:, pl.ds(i * 64, 64), :], qkv_sems.at[i]) for i in range(3)
+    ]
+    g_copies = [
+        pltpu.make_async_copy(g_ref.at[pl.ds(i * 4, 4)], send_out.at[pl.ds(i * 4, 4), pl.ds(192, 64), :], g_sems.at[i])
         for i in range(4)
     ]
-    for copy in copies + w_copies:
+    dg_copies = [pltpu.make_async_copy(dg_ref.at[part], dg_out.at[part], dg_sems.at[i]) for i, part in enumerate(parts)]
+    for copy in copies[3:] + w_copies + copies[:3]:
         copy.start()
-    for i, ref in enumerate((q_ref, k_ref, v_ref)):
-        copies[i].wait()
-        for at in range(0, WIDTH, 256):
-            rows = ref[:, at : at + 256].T
-            for h in range(4):
-                send_ref[at // 64 + h, i * 64 : (i + 1) * 64, :] = rows[h * 64 : (h + 1) * 64]
     copies[3].wait()
     copies[4].wait()
     for i in range(4):
@@ -286,16 +279,17 @@
         u_t = u_ref[:, cols].T
         w_copies[i].wait()
         d_gated = dot_nt(w_ref[cols, :], cot_ref[...])
+        g_ref[i * 4 : (i + 1) * 4] = (d_gated * u_t.astype(F32)).astype(BF16).reshape(4, 64, BLOCK)
+        g_copies[i].start()
         dg_ref[cols, :] = d_gated
-        ut_ref[cols, :] = u_t
-        g_t = (d_gated * u_t.astype(F32)).astype(BF16)
-        for h in range(4):
-            send_ref[4 * i + h, 192:256, :] = g_t[h * 64 : (h + 1) * 64]
-        for copy in outs[i]:
-            copy.start()
-    for out in outs:
-        for copy in out:
-            copy.wait()
+        dg_copies[i].start()
+    for i, ref in enumerate((q_ref, k_ref, v_ref)):
+        copies[i].wait()
+        for at in range(0, WIDTH, 256):
+            qkv_ref[i, at // 64 : at // 64 + 4] = ref[:, at : at + 256].T.reshape(4, 64, BLOCK)
+        qkv_copies[i].start()
+    for copy in qkv_copies + g_copies + dg_copies:
+        copy.wait()
 
 
 def other_half_kernel(place_ref, got_ref, out_ref):
@@ -334,9 +328,9 @@
     return centre * lax.rsqrt(jnp.mean(centre * centre, axis=0, keepdims=True) + 1e-05)
 
 
-def gated_kernel(place_ref, got_ref, ut_ref, keep_ref, core_ref, z_ref, both_ref, half_ref):
+def gated_kernel(place_ref, got_ref, u_ref, keep_ref, core_ref, z_ref, both_ref, half_ref):
     core, zl = place_ref[4], place_ref[5]
-    gated = normalised(got_ref) * ut_ref[...].astype(F32)
+    gated = normalised(got_ref) * u_ref[...].T.astype(F32)
     for z in (0, 1, 4, 5):
         for chip in range(HEADS):
             at = z * BLOCK + chip * 8
@@ -399,17 +393,20 @@
 
 
 def prepare(*args):
-    shapes = shape((HEADS, 256, BLOCK)), shape((WIDTH, BLOCK)), shape((WIDTH, BLOCK), F32)
     return call(
         prepare_kernel,
         "prepare",
-        shapes,
+        (shape((HEADS, 256, BLOCK)), shape((WIDTH, BLOCK), F32)),
         [ANY] * 6,
         args,
         [pltpu.VMEM((BLOCK, WIDTH), BF16)] * 5
-        + [pltpu.VMEM((WIDTH, WIDTH), BF16)]
-        + [pltpu.VMEM(s.shape, s.dtype) for s in shapes]
-        + [DMA((5,)), DMA((4,)), DMA((3, 4))],
+        + [
+            pltpu.VMEM((WIDTH, WIDTH), BF16),
+            pltpu.VMEM((3, HEADS, 64, BLOCK), BF16),
+            pltpu.VMEM((HEADS, 64, BLOCK), BF16),
+            pltpu.VMEM((WIDTH, BLOCK), F32),
+        ]
+        + [DMA((5,)), DMA((4,)), DMA((3,)), DMA((4,)), DMA((4,))],
         out=ANY,
         mib=None,
     )
@@ -487,7 +484,7 @@
     def chips(x):
         return lax.all_to_all(x, CHIP, 0, 0, tiled=True)
 
-    send, u_t, d_gated_t = prepare(query, key, value, gate_u, cotangent, out_weight)
+    send, d_gated_t = prepare(query, key, value, gate_u, cotangent, out_weight)
     got = chips(send)
     theirs = call(other_half_kernel, "other_half", shape((8, 256, BLOCK)), [SMEM, VMEM], (place, got))
     x, mine, theirs, stat = attend_forward(place, got, swap(theirs))
@@ -516,7 +513,7 @@
         "gated",
         (shape((256, BLOCK)),) * 4,
         [SMEM] + [VMEM] * 2,
-        (place, got_attn, u_t),
+        (place, got_attn, gate_u),
         [pltpu.VMEM((2, 512, BLOCK), F32)],
     )
     part = call(

time: 105 us -> 104 us (level)
  no operation moved by 1% of the time
where the time goes in v6:
time: 104 us
  starting transfers between devices  41.9 us (40%)
  Pallas kernels  32.4 us (31%)
  waiting for transfers between devices  28 us (27%)
    pallas_call x11, Pallas kernels, call(): pl.pallas_call(kernel, out_shape=out_shape, in_specs=in_specs, out_specs=...  32.4 us
    all_to_all x4, starting transfers between devices, chips(): return lax.all_to_all(x, CHIP, 0, 0, tiled=True)  27.6 us
    all_to_all x4, waiting for transfers between devices, chips(): return lax.all_to_all(x, CHIP, 0, 0, tiled=True)  16.3 us
    ppermute x2, starting transfers between devices, on_device(): part = kept + lax.ppermute(away, 'zh', [(i, i ^ step) for i in range(4)])  9.63 us
    ppermute x3, waiting for transfers between devices, swap(): return lax.ppermute(x, 'core', SWAP)  4.78 us
    ppermute x6, starting transfers between devices, four(): lax.ppermute(part, ('zl', 'core'), [(i, i ^ step) for i in range(4)])  4.29 us
    ppermute x6, waiting for transfers between devices, four(): lax.ppermute(part, ('zl', 'core'), [(i, i ^ step) for i in range(4)])  4.02 us
    ppermute x2, waiting for transfers between devices, on_device(): part = kept + lax.ppermute(away, 'zh', [(i, i ^ step) for i in range(4)])  2.91 us
  transfers between devices with their start and end apart: 15, of which 10 were waited for; matrix products, arithmetic and copies ran while one was open for 1% of the time, Pallas kernels for 18%

profile of v6, /device:TPU:2, one launch (start us, length us, event | category | flops | bytes accessed | tf_op | source)
XLA Modules:
  0.0 104.0 jit_solution(12747696342029989238)
XLA Ops:
  0.6 0.0 copy-start.3
  0.6 4.2 %prepare.1 = (bf16[16,256,128]{2,1,0:T(8,128)(2,1)}, f32[1024,128]{1,0:T(8,128)}) custom-call(bf16[128,1024]{1,0:T(8,128)(2,1)} %q_in.1, bf16[128,1024]{1,0:T(8,128)(2,1)} %k_in.1, bf16[128,1024]{1,0:T(8,128)(2,1)} %v_in.1, bf16[128,1024]{1,0:T(8,128)(2,1)} %u_ref.1, bf16[128,1024]{1,0:T(8,128)(2,1)} %refs_4_.1, bf16[1024,1024]{1,0:T(8,128)(2,1)} %w_in.1), custom_call_target="tpu_custom_call" | custom-call | flops 67108864 | bytes 2097152 | tf_op jit(solution)/shard_map/prepare/pallas_call | solution.py:379
  4.8 7.5 %all-to-all-start = ((bf16[16,256,128]{2,1,0:T(8,128)(2,1)}), bf16[16,256,128]{2,1,0:T(8,128)(2,1)S(1)}, u32[]{:S(2)}, u32[]{:S(2)}) async-start(bf16[16,256,128]{2,1,0:T(8,128)(2,1)} %get-tuple-element.23), calls=%async_computation | async-start | bytes 2097152 | tf_op jit(solution)/shard_map/all_to_all | solution.py:485
  12.3 0.0 copy-done.3
  12.3 0.1 pad_add_fusion.place_ref
  12.4 15.0 %all-to-all-done.got_ref = bf16[16,256,128]{2,1,0:T(8,128)(2,1)S(1)} async-done(((bf16[16,256,128]{2,1,0:T(8,128)(2,1)}), bf16[16,256,128]{2,1,0:T(8,128)(2,1)S(1)}, u32[]{:S(2)}, u32[]{:S(2)}) %all-to-all-start) | async-done | bytes 1048608 | tf_op jit(solution)/shard_map/all_to_all | solution.py:485
  27.4 0.7 other_half.1
  28.1 0.0 copy-start.1
  28.1 0.1 collective-permute-start
  28.2 1.9 %collective-permute-done.other_ref = bf16[8,256,128]{2,1,0:T(8,128)(2,1)S(1)} collective-permute-done((bf16[8,256,128]{2,1,0:T(8,128)(2,1)S(1)}, bf16[8,256,128]{2,1,0:T(8,128)(2,1)S(1)}, u32[]{:S(2)}, u32[]{:S(2)}) %collective-permute-start) | collective-permute-done | bytes 524320 | tf_op jit(solution)/shard_map/ppermute | solution.py:482
  30.1 4.9 %attend_forward.1 = (bf16[320,2048]{1,0:T(8,128)(2,1)S(1)}, bf16[8,64,128]{2,1,0:T(8,128)(2,1)S(1)}, bf16[8,64,128]{2,1,0:T(8,128)(2,1)S(1)}, bf16[80,128]{1,0:T(8,128)(2,1)S(1)}) custom-call(s32[6]{0:T(128)S(1)} %pad_add_fusion.place_ref, bf16[16,256,128]{2,1,0:T(8,128)(2,1)S(1)} %all-to-all-done.got_ref, ...), custom_call_target="tpu_custom_call" | custom-call | flops 1073741824 | bytes 2097152 | tf_op jit(solution)/shard_map/attend_forward/pallas_call | solution.py:379
  34.9 0.2 collective-permute-start.1
  35.2 1.2 %collective-permute-done.1.theirs_ref = bf16[8,64,128]{2,1,0:T(8,128)(2,1)S(1)} collective-permute-done((bf16[8,64,128]{2,1,0:T(8,128)(2,1)S(1)}, bf16[8,64,128]{2,1,0:T(8,128)(2,1)S(1)}, u32[]{:S(2)}, u32[]{:S(2)}) %collective-permute-start.1) | collective-permute-done | bytes 131104 | tf_op jit(solution)/shard_map/ppermute | solution.py:482
  36.4 1.5 %attn_to_owners.1 = bf16[16,144,128]{2,1,0:T(8,128)(2,1)} custom-call(s32[6]{0:T(128)S(1)} %pad_add_fusion.place_ref, bf16[8,64,128]{2,1,0:T(8,128)(2,1)S(1)} %get-tuple-element.25.mine_ref, bf16[8,64,128]{2,1,0:T(8,128)(2,1)S(1)} %collective-permute-done.1.theirs_ref, bf16[80,128]{1,0:T(8,128)(2,1)S(1)} %get-tuple-element.27.stat_ref), custom_call_target="tpu_custom_call" | custom-call | flops 67108864 | bytes 2097152 | tf_op jit(solution)/shard_map/attn_to_owners/pallas_call | solution.py:379
  37.9 6.1 %all-to-all-start.1 = ((bf16[16,144,128]{2,1,0:T(8,128)(2,1)}), bf16[16,144,128]{2,1,0:T(8,128)(2,1)S(1)}, u32[]{:S(2)}, u32[]{:S(2)}) async-start(bf16[16,144,128]{2,1,0:T(8,128)(2,1)} %attn_to_owners.1), calls=%async_computation.1 | async-start | bytes 1179648 | tf_op jit(solution)/shard_map/all_to_all | solution.py:485
  44.1 0.0 copy-done.1
  44.1 0.1 collective-permute-start.6
  44.2 2.0 %collective-permute-start.7 = (bf16[128,1024]{1,0:T(8,128)(2,1)S(1)}, bf16[128,1024]{1,0:T(8,128)(2,1)S(1)}, u32[]{:S(2)}, u32[]{:S(2)}) collective-permute-start(bf16[128,1024]{1,0:T(8,128)(2,1)S(1)} %copy-done.1), channel_id=1, source_target_pairs={{0,32},{1,33},{32,0},{33,1},{2,34},{3,35},{34,2},{35,3},{4,36},{5,... | collective-permute-start | bytes 786440 | tf_op jit(solution)/shard_map/ppermute | solution.py:507
  46.2 0.1 collective-permute-start.8
  46.2 0.0 copy-start
  46.2 7.0 %derive.1.tile_in = bf16[80,256,256]{2,1,0:T(8,128)(2,1)} custom-call(s32[6]{0:T(128)S(1)} %pad_add_fusion.place_ref, bf16[320,2048]{1,0:T(8,128)(2,1)S(1)} %get-tuple-element.24.x_ref), custom_call_target="tpu_custom_call" | custom-call | flops 2147483648 | bytes 2097152 | tf_op jit(solution)/shard_map/derive/pallas_call | solution.py:379
  53.3 1.3 %all-to-all-done.1.got_ref = bf16[16,144,128]{2,1,0:T(8,128)(2,1)S(1)} async-done(((bf16[16,144,128]{2,1,0:T(8,128)(2,1)}), bf16[16,144,128]{2,1,0:T(8,128)(2,1)S(1)}, u32[]{:S(2)}, u32[]{:S(2)}) %all-to-all-start.1) | async-done | bytes 589856 | tf_op jit(solution)/shard_map/all_to_all | solution.py:485
  54.6 0.0 copy-done
  54.6 1.0 gated.1
  55.6 0.1 collective-permute-start.3
  55.7 2.0 %collective-permute-start.4 = (bf16[256,128]{1,0:T(8,128)(2,1)S(1)}, bf16[256,128]{1,0:T(8,128)(2,1)S(1)}, u32[]{:S(2)}, u32[]{:S(2)}) collective-permute-start(bf16[256,128]{1,0:T(8,128)(2,1)S(1)} %get-tuple-element.38), channel_id=1, source_target_pairs={{0,32},{1,33},{32,0},{33,1},{2,34},{3,35},{34,2},{35,3},{4,36},{5,... | collective-permute-start | bytes 196616 | tf_op jit(solution)/shard_map/ppermute | solution.py:507
  57.7 0.0 collective-permute-done.6.refs_5_
  57.7 0.0 collective-permute-start.5
  57.7 0.0 collective-permute-done.7.refs_6_
  57.7 0.7 collective-permute-done.8.refs_7_
  58.4 0.0 collective-permute-done.3.refs_1_
  58.4 2.0 %collective-permute-done.4.refs_2_ = bf16[256,128]{1,0:T(8,128)(2,1)S(1)} collective-permute-done((bf16[256,128]{1,0:T(8,128)(2,1)S(1)}, bf16[256,128]{1,0:T(8,128)(2,1)S(1)}, u32[]{:S(2)}, u32[]{:S(2)}) %collective-permute-start.4) | collective-permute-done | bytes 65568 | tf_op jit(solution)/shard_map/ppermute | solution.py:507
  60.3 1.4 %collective-permute-done.5.refs_3_ = bf16[256,128]{1,0:T(8,128)(2,1)S(1)} collective-permute-done((bf16[256,128]{1,0:T(8,128)(2,1)S(1)}, bf16[256,128]{1,0:T(8,128)(2,1)S(1)}, u32[]{:S(2)}, u32[]{:S(2)}) %collective-permute-start.5) | collective-permute-done | bytes 65568 | tf_op jit(solution)/shard_map/ppermute | solution.py:507
  61.7 1.4 %product.1 = bf16[256,1024]{1,0:T(8,128)(2,1)} custom-call(bf16[256,128]{1,0:T(8,128)(2,1)S(1)} %get-tuple-element.36.refs_0_, bf16[256,128]{1,0:T(8,128)(2,1)S(1)} %collective-permute-done.3.refs_1_, bf16[256,128]{1,0:T(8,128)(2,1)S(1)} %collective-permute-done.4.refs_2_, bf16[256,128]{1,0:T(8,128)(2,1)S(1)} %collective-permute-done.5.refs_3_, ...), custom_call_target="tpu_custom_call" | custom-call | flops 67108864 | bytes 2097152 | tf_op jit(solution)/shard_map/product/pallas_call | solution.py:379
  63.2 6.7 %all-to-all-start.3 = ((bf16[16,16,1024]{2,1,0:T(8,128)(2,1)}), bf16[16,16,1024]{2,1,0:T(8,128)(2,1)S(1)}, u32[]{:S(2)}, u32[]{:S(2)}) async-start(bf16[16,16,1024]{2,1,0:T(8,128)(2,1)} %bitcast.3), calls=%async_computation.3 | async-start | bytes 1048576 | tf_op jit(solution)/shard_map/all_to_all | solution.py:485
  69.9 8.1 %attend_backward.1 = (bf16[8,192,128]{2,1,0:T(8,128)(2,1)S(1)}, bf16[8,192,128]{2,1,0:T(8,128)(2,1)S(1)}) custom-call(s32[6]{0:T(128)S(1)} %pad_add_fusion.place_ref, bf16[320,2048]{1,0:T(8,128)(2,1)S(1)} %get-tuple-element.24.x_ref, bf16[16,144,128]{2,1,0:T(8,128)(2,1)S(1)} %all-to-all-done.1.got_ref, bf16[80,256,256]{2,1,0:T(8,128)(2,1)} %derive.1.tile_in), custom_call_target="tpu_custom_call" | custom-call | flops 8589934592 | bytes 2097152 | tf_op jit(solution)/shard_map/attend_backward/pallas_call | solution.py:379
  78.0 0.0 copy-start.2
  78.0 0.1 collective-permute-start.2
  78.1 1.7 %collective-permute-done.2.theirs_ref = bf16[8,192,128]{2,1,0:T(8,128)(2,1)S(1)} collective-permute-done((bf16[8,192,128]{2,1,0:T(8,128)(2,1)S(1)}, bf16[8,192,128]{2,1,0:T(8,128)(2,1)S(1)}, u32[]{:S(2)}, u32[]{:S(2)}) %collective-permute-start.2) | collective-permute-done | bytes 393248 | tf_op jit(solution)/shard_map/ppermute | solution.py:482
  79.8 1.6 %grads_to_owners.1.after_ref = bf16[16,192,128]{2,1,0:T(8,128)(2,1)} custom-call(s32[6]{0:T(128)S(1)} %pad_add_fusion.place_ref, bf16[8,192,128]{2,1,0:T(8,128)(2,1)S(1)} %get-tuple-element.30.mine_ref, bf16[8,192,128]{2,1,0:T(8,128)(2,1)S(1)} %collective-permute-done.2.theirs_ref), custom_call_target="tpu_custom_call" | custom-call | flops 67108864 | bytes 2097152 | tf_op jit(solution)/shard_map/grads_to_owners/pallas_call | solution.py:379
  81.3 0.0 all-to-all-done.3
  81.3 7.2 %all-to-all-start.2 = ((bf16[16,192,128]{2,1,0:T(8,128)(2,1)}), bf16[16,192,128]{2,1,0:T(8,128)(2,1)S(1)}, u32[]{:S(2)}, u32[]{:S(2)}) async-start(bf16[16,192,128]{2,1,0:T(8,128)(2,1)} %grads_to_owners.1.after_ref), calls=%async_computation.2 | async-start | bytes 1572864 | tf_op jit(solution)/shard_map/all_to_all | solution.py:485
  88.6 0.1 convert_reduce_fusion
  88.7 6.9 %collective-permute-start.9 = (f32[2,4,1024]{2,1,0:T(4,128)S(1)}, f32[2,4,1024]{2,1,0:T(4,128)S(1)}, u32[]{:S(2)}, u32[]{:S(2)}) collective-permute-start(f32[2,4,1024]{2,1,0:T(4,128)S(1)} %dynamic-slice_bitcast_fusion), channel_id=1, source_target_pairs={{0,128},{64,192},{128,0},{192,64},{1,129},{65,193},{129,1},{193,65... | collective-permute-start | bytes 98312 | tf_op jit(solution)/shard_map/ppermute | solution.py:556
  95.6 2.0 %collective-permute-done.9 = f32[2,4,1024]{2,1,0:T(4,128)S(1)} collective-permute-done((f32[2,4,1024]{2,1,0:T(4,128)S(1)}, f32[2,4,1024]{2,1,0:T(4,128)S(1)}, u32[]{:S(2)}, u32[]{:S(2)}) %collective-permute-start.9) | collective-permute-done | bytes 32800 | tf_op jit(solution)/shard_map/ppermute | solution.py:556
  97.7 2.7 %collective-permute-start.10 = (f32[1,4,1024]{2,1,0:T(4,128)S(1)}, f32[1,4,1024]{2,1,0:T(4,128)S(1)}, u32[]{:S(2)}, u32[]{:S(2)}) collective-permute-start(f32[1,4,1024]{2,1,0:T(4,128)S(1)} %constant_dynamic-slice_fusion), channel_id=1, source_target_pairs={{0,64},{64,0},{128,192},{192,128},{1,65},{65,1},{129,193},{193,129... | collective-permute-start | bytes 49160 | tf_op jit(solution)/shard_map/ppermute | solution.py:556
  100.4 0.0 copy-done.2
  100.4 1.1 %d_gate.1 = bf16[128,1024]{1,0:T(8,128)(2,1)} custom-call(bf16[16,144,128]{2,1,0:T(8,128)(2,1)S(1)} %all-to-all-done.1.got_ref, f32[1024,128]{1,0:T(8,128)S(1)} %copy-done.2, bf16[16,192,128]{2,1,0:T(8,128)(2,1)} %grads_to_owners.1.after_ref), custom_call_target="tpu_custom_call" | custom-call | flops 1048576 | bytes 2097152 | tf_op jit(solution)/shard_map/d_gate/pallas_call | solution.py:379
  101.5 0.9 collective-permute-done.10
  102.4 0.6 multiply_bitcast_fusion
  103.0 0.0 all-to-all-done.2.got_ref
  103.0 1.0 finish.1
  (4 shorter events, 0.1 us)
Async XLA Ops:
  0.6 11.7 %copy-start.3 = (s32[1,4]{1,0:T(1,128)S(1)}, s32[1,4]{1,0:T(1,128)}, u32[]{:S(2)}) copy-start(s32[1,4]{1,0:T(1,128)} %param.13) | copy-start | bytes 52
  4.8 22.5 %all-to-all-start = ((bf16[16,256,128]{2,1,0:T(8,128)(2,1)}), bf16[16,256,128]{2,1,0:T(8,128)(2,1)S(1)}, u32[]{:S(2)}, u32[]{:S(2)}) async-start(bf16[16,256,128]{2,1,0:T(8,128)(2,1)} %get-tuple-element.23), calls=%async_computation | async-start | bytes 2097152 | tf_op jit(solution)/shard_map/all_to_all | solution.py:485
  28.1 16.0 %copy-start.1 = (bf16[128,1024]{1,0:T(8,128)(2,1)S(1)}, bf16[128,1024]{1,0:T(8,128)(2,1)}, u32[]{:S(2)}) copy-start(bf16[128,1024]{1,0:T(8,128)(2,1)} %refs_4_.1) | copy-start | bytes 786436
  28.1 2.0 %collective-permute-start = (bf16[8,256,128]{2,1,0:T(8,128)(2,1)S(1)}, bf16[8,256,128]{2,1,0:T(8,128)(2,1)S(1)}, u32[]{:S(2)}, u32[]{:S(2)}) collective-permute-start(bf16[8,256,128]{2,1,0:T(8,128)(2,1)S(1)} %other_half.1), channel_id=1, source_target_pairs={{0,1},{1,0},{2,3},{3,2},{4,5},{5,4},{6,7},{7,6},{8,9},{9,8},{10,11... | collective-permute-start | bytes 1572872 | tf_op jit(solution)/shard_map/ppermute | solution.py:482
  34.9 1.4 %collective-permute-start.1 = (bf16[8,64,128]{2,1,0:T(8,128)(2,1)S(1)}, bf16[8,64,128]{2,1,0:T(8,128)(2,1)S(1)}, u32[]{:S(2)}, u32[]{:S(2)}) collective-permute-start(bf16[8,64,128]{2,1,0:T(8,128)(2,1)S(1)} %get-tuple-element.26), channel_id=1, source_target_pairs={{0,1},{1,0},{2,3},{3,2},{4,5},{5,4},{6,7},{7,6},{8,9},{9,8},{10,11... | collective-permute-start | bytes 393224 | tf_op jit(solution)/shard_map/ppermute | solution.py:482
  37.9 16.7 %all-to-all-start.1 = ((bf16[16,144,128]{2,1,0:T(8,128)(2,1)}), bf16[16,144,128]{2,1,0:T(8,128)(2,1)S(1)}, u32[]{:S(2)}, u32[]{:S(2)}) async-start(bf16[16,144,128]{2,1,0:T(8,128)(2,1)} %attn_to_owners.1), calls=%async_computation.1 | async-start | bytes 1179648 | tf_op jit(solution)/shard_map/all_to_all | solution.py:485
  44.1 13.6 %collective-permute-start.6 = (bf16[128,1024]{1,0:T(8,128)(2,1)S(1)}, bf16[128,1024]{1,0:T(8,128)(2,1)S(1)}, u32[]{:S(2)}, u32[]{:S(2)}) collective-permute-start(bf16[128,1024]{1,0:T(8,128)(2,1)S(1)} %copy-done.1), channel_id=1, source_target_pairs={{0,1},{1,0},{32,33},{33,32},{2,3},{3,2},{34,35},{35,34},{4,5},{5,4... | collective-permute-start | bytes 786440 | tf_op jit(solution)/shard_map/ppermute | solution.py:507
  44.2 13.5 %collective-permute-start.7 = (bf16[128,1024]{1,0:T(8,128)(2,1)S(1)}, bf16[128,1024]{1,0:T(8,128)(2,1)S(1)}, u32[]{:S(2)}, u32[]{:S(2)}) collective-permute-start(bf16[128,1024]{1,0:T(8,128)(2,1)S(1)} %copy-done.1), channel_id=1, source_target_pairs={{0,32},{1,33},{32,0},{33,1},{2,34},{3,35},{34,2},{35,3},{4,36},{5,... | collective-permute-start | bytes 786440 | tf_op jit(solution)/shard_map/ppermute | solution.py:507
  46.2 12.2 %collective-permute-start.8 = (bf16[128,1024]{1,0:T(8,128)(2,1)S(1)}, bf16[128,1024]{1,0:T(8,128)(2,1)S(1)}, u32[]{:S(2)}, u32[]{:S(2)}) collective-permute-start(bf16[128,1024]{1,0:T(8,128)(2,1)S(1)} %copy-done.1), channel_id=1, source_target_pairs={{0,33},{1,32},{32,1},{33,0},{2,35},{3,34},{34,3},{35,2},{4,37},{5,... | collective-permute-start | bytes 786440 | tf_op jit(solution)/shard_map/ppermute | solution.py:507
  46.2 8.4 %copy-start = (bf16[128,1024]{1,0:T(8,128)(2,1)S(1)}, bf16[128,1024]{1,0:T(8,128)(2,1)}, u32[]{:S(2)}) copy-start(bf16[128,1024]{1,0:T(8,128)(2,1)} %u_ref.1) | copy-start | bytes 786436
  55.6 2.8 %collective-permute-start.3 = (bf16[256,128]{1,0:T(8,128)(2,1)S(1)}, bf16[256,128]{1,0:T(8,128)(2,1)S(1)}, u32[]{:S(2)}, u32[]{:S(2)}) collective-permute-start(bf16[256,128]{1,0:T(8,128)(2,1)S(1)} %get-tuple-element.37), channel_id=1, source_target_pairs={{0,1},{1,0},{32,33},{33,32},{2,3},{3,2},{34,35},{35,34},{4,5},{5,4... | collective-permute-start | bytes 196616 | tf_op jit(solution)/shard_map/ppermute | solution.py:507
  55.7 4.7 %collective-permute-start.4 = (bf16[256,128]{1,0:T(8,128)(2,1)S(1)}, bf16[256,128]{1,0:T(8,128)(2,1)S(1)}, u32[]{:S(2)}, u32[]{:S(2)}) collective-permute-start(bf16[256,128]{1,0:T(8,128)(2,1)S(1)} %get-tuple-element.38), channel_id=1, source_target_pairs={{0,32},{1,33},{32,0},{33,1},{2,34},{3,35},{34,2},{35,3},{4,36},{5,... | collective-permute-start | bytes 196616 | tf_op jit(solution)/shard_map/ppermute | solution.py:507
  57.7 4.1 %collective-permute-start.5 = (bf16[256,128]{1,0:T(8,128)(2,1)S(1)}, bf16[256,128]{1,0:T(8,128)(2,1)S(1)}, u32[]{:S(2)}, u32[]{:S(2)}) collective-permute-start(bf16[256,128]{1,0:T(8,128)(2,1)S(1)} %get-tuple-element.39), channel_id=1, source_target_pairs={{0,33},{1,32},{32,1},{33,0},{2,35},{3,34},{34,3},{35,2},{4,37},{5,... | collective-permute-start | bytes 196616 | tf_op jit(solution)/shard_map/ppermute | solution.py:507
  63.2 18.2 %all-to-all-start.3 = ((bf16[16,16,1024]{2,1,0:T(8,128)(2,1)}), bf16[16,16,1024]{2,1,0:T(8,128)(2,1)S(1)}, u32[]{:S(2)}, u32[]{:S(2)}) async-start(bf16[16,16,1024]{2,1,0:T(8,128)(2,1)} %bitcast.3), calls=%async_computation.3 | async-start | bytes 1048576 | tf_op jit(solution)/shard_map/all_to_all | solution.py:485
  78.0 22.4 %copy-start.2 = (f32[1024,128]{1,0:T(8,128)S(1)}, f32[1024,128]{1,0:T(8,128)}, u32[]{:S(2)}) copy-start(f32[1024,128]{1,0:T(8,128)} %get-tuple-element.35.dg_ref) | copy-start | bytes 1572868
  78.0 1.8 %collective-permute-start.2 = (bf16[8,192,128]{2,1,0:T(8,128)(2,1)S(1)}, bf16[8,192,128]{2,1,0:T(8,128)(2,1)S(1)}, u32[]{:S(2)}, u32[]{:S(2)}) collective-permute-start(bf16[8,192,128]{2,1,0:T(8,128)(2,1)S(1)} %get-tuple-element.31), channel_id=1, source_target_pairs={{0,1},{1,0},{2,3},{3,2},{4,5},{5,4},{6,7},{7,6},{8,9},{9,8},{10,11... | collective-permute-start | bytes 1179656 | tf_op jit(solution)/shard_map/ppermute | solution.py:482
  81.3 21.7 %all-to-all-start.2 = ((bf16[16,192,128]{2,1,0:T(8,128)(2,1)}), bf16[16,192,128]{2,1,0:T(8,128)(2,1)S(1)}, u32[]{:S(2)}, u32[]{:S(2)}) async-start(bf16[16,192,128]{2,1,0:T(8,128)(2,1)} %grads_to_owners.1.after_ref), calls=%async_computation.2 | async-start | bytes 1572864 | tf_op jit(solution)/shard_map/all_to_all | solution.py:485
  88.7 8.9 %collective-permute-start.9 = (f32[2,4,1024]{2,1,0:T(4,128)S(1)}, f32[2,4,1024]{2,1,0:T(4,128)S(1)}, u32[]{:S(2)}, u32[]{:S(2)}) collective-permute-start(f32[2,4,1024]{2,1,0:T(4,128)S(1)} %dynamic-slice_bitcast_fusion), channel_id=1, source_target_pairs={{0,128},{64,192},{128,0},{192,64},{1,129},{65,193},{129,1},{193,65... | collective-permute-start | bytes 98312 | tf_op jit(solution)/shard_map/ppermute | solution.py:556
  97.7 4.7 %collective-permute-start.10 = (f32[1,4,1024]{2,1,0:T(4,128)S(1)}, f32[1,4,1024]{2,1,0:T(4,128)S(1)}, u32[]{:S(2)}, u32[]{:S(2)}) collective-permute-start(f32[1,4,1024]{2,1,0:T(4,128)S(1)} %constant_dynamic-slice_fusion), channel_id=1, source_target_pairs={{0,64},{64,0},{128,192},{192,128},{1,65},{65,1},{129,193},{193,129... | collective-permute-start | bytes 49160 | tf_op jit(solution)/shard_map/ppermute | solution.py:556

commit v7 on v6

--- a/solution.py
+++ b/solution.py
@@ -328,8 +328,8 @@
     return centre * lax.rsqrt(jnp.mean(centre * centre, axis=0, keepdims=True) + 1e-05)
 
 
-def gated_kernel(place_ref, got_ref, u_ref, keep_ref, core_ref, z_ref, both_ref, half_ref):
-    core, zl = place_ref[4], place_ref[5]
+def gated_kernel(place_ref, got_ref, u_ref, mine_ref, theirs_ref, half_ref):
+    core = place_ref[4]
     gated = normalised(got_ref) * u_ref[...].T.astype(F32)
     for z in (0, 1, 4, 5):
         for chip in range(HEADS):
@@ -339,8 +339,8 @@
             rows = slice(row, row + 8)
             half_ref[0, rows, :] = jnp.concatenate([one[0:4], two[0:4]], axis=0)
             half_ref[1, rows, :] = jnp.concatenate([one[4:8], two[4:8]], axis=0)
-    for c, z, out_ref in ((core, zl, keep_ref), (1 - core, zl, core_ref), (core, 1 - zl, z_ref), (1 - core, 1 - zl, both_ref)):
-        out_ref[...] = half_ref[c, pl.ds(pl.multiple_of(z * 256, 256), 256), :].astype(BF16)
+    mine_ref[...] = half_ref[core].astype(BF16)
+    theirs_ref[...] = half_ref[1 - core].astype(BF16)
 
 
 def d_gate_kernel(got_ref, dg_ref, after_ref, out_ref):
@@ -350,9 +350,9 @@
 
 
 def product_kernel(*refs):
-    gated, cotangent, (out, out_ref, sems) = refs[0:4], refs[4:8], refs[8:]
+    gated, cotangent, (out, out_ref, sems) = refs[0:2], refs[2:4], refs[4:]
     copies = []
-    for i in range(2):
+    for i in range(4):
         rows = slice(i * 128, (i + 1) * 128)
         out_ref[rows, :] = sum(dot(a[rows, :], b[...]) for a, b in zip(gated, cotangent)).astype(BF16)
         part = pl.ds(i * 128, 128)
@@ -476,7 +476,7 @@
 
 def on_device(query, key, value, gate_u, out_weight, cotangent, hist_lengths):
     core = lax.axis_index("core")
-    place = jnp.concatenate([hist_lengths[0], core[None], lax.axis_index("zl")[None]]).astype(jnp.int32)
+    place = jnp.concatenate([hist_lengths[0], core[None]]).astype(jnp.int32)
 
     def swap(x):
         return lax.ppermute(x, "core", SWAP)
@@ -502,16 +502,10 @@
     got_attn = chips(send)
     got_attn, derived = lax.optimization_barrier((got_attn, derive(place, x)))
 
-    def four(parts):
-        return [parts[0]] + [
-            lax.ppermute(part, ("zl", "core"), [(i, i ^ step) for i in range(4)])
-            for step, part in zip((1, 2, 3), parts[1:])
-        ]
-
-    gated = call(
+    mine, theirs = call(
         gated_kernel,
         "gated",
-        (shape((256, BLOCK)),) * 4,
+        (shape((512, BLOCK)),) * 2,
         [SMEM] + [VMEM] * 2,
         (place, got_attn, gate_u),
         [pltpu.VMEM((2, 512, BLOCK), F32)],
@@ -519,13 +513,13 @@
     part = call(
         product_kernel,
         "product",
-        shape((256, WIDTH)),
-        [VMEM] * 8,
-        four(gated) + four([cotangent] * 4),
-        [pltpu.VMEM((256, WIDTH), BF16), DMA((2,))],
+        shape((512, WIDTH)),
+        [VMEM] * 4,
+        (mine, swap(theirs), cotangent, swap(cotangent)),
+        [pltpu.VMEM((512, WIDTH), BF16), DMA((4,))],
         out=ANY,
     )
-    parts = chips(part.reshape(HEADS, 16, WIDTH))
+    parts = lax.all_to_all(part.reshape(32, 16, WIDTH), ("zl",) + CHIP, 0, 0, tiled=True)
 
     mine, theirs = attend_backward(place, x, got_attn, derived)
     send = call(

time: 104 us -> 103 us (level)
  starting transfers between devices: 41.9 us -> 36.7 us
  waiting for transfers between devices: 28 us -> 30.6 us
  other arithmetic: 0.78 us -> 2.09 us
    all_to_all x4 -> x3, starting transfers between devices: 27.6 us -> 18.6 us  [chips(): return lax.all_to_all(x, CHIP, 0, 0, tiled=True)]
    all_to_all x0 -> x1, starting transfers between devices: none -> 7.43 us  [on_device(): lax.all_to_all(part.reshape(32, 16, WIDTH), ('zl',) + CHIP, 0, 0, tiled=T...]
    all_to_all x0 -> x1, waiting for transfers between devices: none -> 4.39 us  [on_device(): lax.all_to_all(part.reshape(32, 16, WIDTH), ('zl',) + CHIP, 0, 0, tiled=T...]
    ppermute x6 -> x0, starting transfers between devices: 4.29 us -> none  [four(): lax.ppermute(part, ('zl', 'core'), [(i, i ^ step) for i in range(4)])]
    ppermute x6 -> x0, waiting for transfers between devices: 4.02 us -> none  [four(): lax.ppermute(part, ('zl', 'core'), [(i, i ^ step) for i in range(4)])]
    all_to_all x4 -> x3, waiting for transfers between devices: 16.3 us -> 18.2 us  [chips(): return lax.all_to_all(x, CHIP, 0, 0, tiled=True)]
    ppermute x3 -> x5, waiting for transfers between devices: 4.78 us -> 6.14 us  [swap(): return lax.ppermute(x, 'core', SWAP)]
    reduce_sum x1, other arithmetic: 0.08 us -> 1.39 us  [on_device(): part = jnp.sum(parts.astype(F32), axis=0).reshape(4, 4, WIDTH)]
  transfers between devices with their start and end apart: 15 -> 11, of which waited for: 10 -> 8; matrix products, arithmetic and copies ran while one was open for 1% -> 1% of each run, Pallas kernels for 18% -> 19%
where the time goes in v7:
time: 103 us
  starting transfers between devices  36.7 us (36%)
  Pallas kernels  32.5 us (32%)
  waiting for transfers between devices  30.6 us (30%)
  other arithmetic  2.09 us (2%)
    pallas_call x11, Pallas kernels, call(): pl.pallas_call(kernel, out_shape=out_shape, in_specs=in_specs, out_specs=...  32.5 us
    all_to_all x3, starting transfers between devices, chips(): return lax.all_to_all(x, CHIP, 0, 0, tiled=True)  18.6 us
    all_to_all x3, waiting for transfers between devices, chips(): return lax.all_to_all(x, CHIP, 0, 0, tiled=True)  18.2 us
    ppermute x2, starting transfers between devices, on_device(): part = kept + lax.ppermute(away, 'zh', [(i, i ^ step) for i in range(4)])  9.7 us
    all_to_all x1, starting transfers between devices, on_device(): lax.all_to_all(part.reshape(32, 16, WIDTH), ('zl',) + CHIP, 0, 0, tiled=T...  7.43 us
    ppermute x5, waiting for transfers between devices, swap(): return lax.ppermute(x, 'core', SWAP)  6.14 us
    all_to_all x1, waiting for transfers between devices, on_device(): lax.all_to_all(part.reshape(32, 16, WIDTH), ('zl',) + CHIP, 0, 0, tiled=T...  4.39 us
  transfers between devices with their start and end apart: 11, of which 8 were waited for; matrix products, arithmetic and copies ran while one was open for 1% of the time, Pallas kernels for 19%

profile of v7, /device:TPU:2, one launch (start us, length us, event | category | flops | bytes accessed | tf_op | source)
XLA Modules:
  0.0 102.8 jit_solution(1504918432839137484)
XLA Ops:
  0.6 0.0 copy-start.3
  0.6 4.2 %prepare.1 = (bf16[16,256,128]{2,1,0:T(8,128)(2,1)}, f32[1024,128]{1,0:T(8,128)}) custom-call(bf16[128,1024]{1,0:T(8,128)(2,1)} %q_in.1, bf16[128,1024]{1,0:T(8,128)(2,1)} %k_in.1, bf16[128,1024]{1,0:T(8,128)(2,1)} %v_in.1, bf16[128,1024]{1,0:T(8,128)(2,1)} %u_ref.1, bf16[128,1024]{1,0:T(8,128)(2,1)} %refs_2_.1, bf16[1024,1024]{1,0:T(8,128)(2,1)} %w_in.1), custom_call_target="tpu_custom_call" | custom-call | flops 67108864 | bytes 2097152 | tf_op jit(solution)/shard_map/prepare/pallas_call | solution.py:379
  4.8 7.5 %all-to-all-start = ((bf16[16,256,128]{2,1,0:T(8,128)(2,1)}), bf16[16,256,128]{2,1,0:T(8,128)(2,1)S(1)}, u32[]{:S(2)}, u32[]{:S(2)}) async-start(bf16[16,256,128]{2,1,0:T(8,128)(2,1)} %get-tuple-element.21), calls=%async_computation | async-start | bytes 2097152 | tf_op jit(solution)/shard_map/all_to_all | solution.py:485
  12.3 0.0 copy-done.3
  12.3 0.1 pad_add_fusion.place_ref
  12.4 15.0 %all-to-all-done.got_ref = bf16[16,256,128]{2,1,0:T(8,128)(2,1)S(1)} async-done(((bf16[16,256,128]{2,1,0:T(8,128)(2,1)}), bf16[16,256,128]{2,1,0:T(8,128)(2,1)S(1)}, u32[]{:S(2)}, u32[]{:S(2)}) %all-to-all-start) | async-done | bytes 1048608 | tf_op jit(solution)/shard_map/all_to_all | solution.py:485
  27.4 0.7 other_half.1
  28.1 0.0 copy-start.1
  28.1 0.1 collective-permute-start
  28.2 1.9 %collective-permute-done.other_ref = bf16[8,256,128]{2,1,0:T(8,128)(2,1)S(1)} collective-permute-done((bf16[8,256,128]{2,1,0:T(8,128)(2,1)S(1)}, bf16[8,256,128]{2,1,0:T(8,128)(2,1)S(1)}, u32[]{:S(2)}, u32[]{:S(2)}) %collective-permute-start) | collective-permute-done | bytes 524320 | tf_op jit(solution)/shard_map/ppermute | solution.py:482
  30.1 4.9 %attend_forward.1 = (bf16[320,2048]{1,0:T(8,128)(2,1)S(1)}, bf16[8,64,128]{2,1,0:T(8,128)(2,1)S(1)}, bf16[8,64,128]{2,1,0:T(8,128)(2,1)S(1)}, bf16[80,128]{1,0:T(8,128)(2,1)S(1)}) custom-call(s32[5]{0:T(128)S(1)} %pad_add_fusion.place_ref, bf16[16,256,128]{2,1,0:T(8,128)(2,1)S(1)} %all-to-all-done.got_ref, ...), custom_call_target="tpu_custom_call" | custom-call | flops 1073741824 | bytes 2097152 | tf_op jit(solution)/shard_map/attend_forward/pallas_call | solution.py:379
  35.0 0.2 collective-permute-start.1
  35.2 1.2 %collective-permute-done.1.theirs_ref = bf16[8,64,128]{2,1,0:T(8,128)(2,1)S(1)} collective-permute-done((bf16[8,64,128]{2,1,0:T(8,128)(2,1)S(1)}, bf16[8,64,128]{2,1,0:T(8,128)(2,1)S(1)}, u32[]{:S(2)}, u32[]{:S(2)}) %collective-permute-start.1) | collective-permute-done | bytes 131104 | tf_op jit(solution)/shard_map/ppermute | solution.py:482
  36.5 1.5 %attn_to_owners.1 = bf16[16,144,128]{2,1,0:T(8,128)(2,1)} custom-call(s32[5]{0:T(128)S(1)} %pad_add_fusion.place_ref, bf16[8,64,128]{2,1,0:T(8,128)(2,1)S(1)} %get-tuple-element.23.mine_ref, bf16[8,64,128]{2,1,0:T(8,128)(2,1)S(1)} %collective-permute-done.1.theirs_ref, bf16[80,128]{1,0:T(8,128)(2,1)S(1)} %get-tuple-element.25.stat_ref), custom_call_target="tpu_custom_call" | custom-call | flops 67108864 | bytes 2097152 | tf_op jit(solution)/shard_map/attn_to_owners/pallas_call | solution.py:379
  38.0 6.1 %all-to-all-start.1 = ((bf16[16,144,128]{2,1,0:T(8,128)(2,1)}), bf16[16,144,128]{2,1,0:T(8,128)(2,1)S(1)}, u32[]{:S(2)}, u32[]{:S(2)}) async-start(bf16[16,144,128]{2,1,0:T(8,128)(2,1)} %attn_to_owners.1), calls=%async_computation.1 | async-start | bytes 1179648 | tf_op jit(solution)/shard_map/all_to_all | solution.py:485
  44.1 0.0 copy-done.1
  44.1 0.3 collective-permute-start.4
  44.4 0.0 copy-start
  44.4 7.0 %derive.1.tile_in = bf16[80,256,256]{2,1,0:T(8,128)(2,1)} custom-call(s32[5]{0:T(128)S(1)} %pad_add_fusion.place_ref, bf16[320,2048]{1,0:T(8,128)(2,1)S(1)} %get-tuple-element.22.x_ref), custom_call_target="tpu_custom_call" | custom-call | flops 2147483648 | bytes 2097152 | tf_op jit(solution)/shard_map/derive/pallas_call | solution.py:379
  51.5 3.2 %all-to-all-done.1.got_ref = bf16[16,144,128]{2,1,0:T(8,128)(2,1)S(1)} async-done(((bf16[16,144,128]{2,1,0:T(8,128)(2,1)}), bf16[16,144,128]{2,1,0:T(8,128)(2,1)S(1)}, u32[]{:S(2)}, u32[]{:S(2)}) %all-to-all-start.1) | async-done | bytes 589856 | tf_op jit(solution)/shard_map/all_to_all | solution.py:485
  54.6 0.0 copy-done
  54.6 1.0 gated.1
  55.6 0.1 collective-permute-start.3
  55.7 0.0 collective-permute-done.4.refs_3_
  55.7 1.3 %collective-permute-done.3.refs_1_ = bf16[512,128]{1,0:T(8,128)(2,1)S(1)} collective-permute-done((bf16[512,128]{1,0:T(8,128)(2,1)S(1)}, bf16[512,128]{1,0:T(8,128)(2,1)S(1)}, u32[]{:S(2)}, u32[]{:S(2)}) %collective-permute-start.3) | collective-permute-done | bytes 131104 | tf_op jit(solution)/shard_map/ppermute | solution.py:482
  57.1 1.4 %product.1 = bf16[512,1024]{1,0:T(8,128)(2,1)} custom-call(bf16[512,128]{1,0:T(8,128)(2,1)S(1)} %get-tuple-element.34.refs_0_, bf16[512,128]{1,0:T(8,128)(2,1)S(1)} %collective-permute-done.3.refs_1_, bf16[128,1024]{1,0:T(8,128)(2,1)S(1)} %copy-done.1, bf16[128,1024]{1,0:T(8,128)(2,1)S(1)} %collective-permute-done.4.refs_3_), custom_call_target="tpu_custom_call" | custom-call | flops 67108864 | bytes 2097152 | tf_op jit(solution)/shard_map/product/pallas_call | solution.py:379
  58.5 7.4 %all-to-all-start.3 = ((bf16[32,16,1024]{2,1,0:T(8,128)(2,1)}), bf16[32,16,1024]{2,1,0:T(8,128)(2,1)}, u32[]{:S(2)}, u32[]{:S(2)}) async-start(bf16[32,16,1024]{2,1,0:T(8,128)(2,1)} %bitcast.2), calls=%async_computation.3 | async-start | bytes 2097152 | tf_op jit(solution)/shard_map/all_to_all | solution.py:522
  65.9 8.1 %attend_backward.1 = (bf16[8,192,128]{2,1,0:T(8,128)(2,1)S(1)}, bf16[8,192,128]{2,1,0:T(8,128)(2,1)S(1)}) custom-call(s32[5]{0:T(128)S(1)} %pad_add_fusion.place_ref, bf16[320,2048]{1,0:T(8,128)(2,1)S(1)} %get-tuple-element.22.x_ref, bf16[16,144,128]{2,1,0:T(8,128)(2,1)S(1)} %all-to-all-done.1.got_ref, bf16[80,256,256]{2,1,0:T(8,128)(2,1)} %derive.1.tile_in), custom_call_target="tpu_custom_call" | custom-call | flops 8589934592 | bytes 2097152 | tf_op jit(solution)/shard_map/attend_backward/pallas_call | solution.py:379
  74.1 0.3 collective-permute-start.2
  74.4 1.7 %collective-permute-done.2.theirs_ref = bf16[8,192,128]{2,1,0:T(8,128)(2,1)S(1)} collective-permute-done((bf16[8,192,128]{2,1,0:T(8,128)(2,1)S(1)}, bf16[8,192,128]{2,1,0:T(8,128)(2,1)S(1)}, u32[]{:S(2)}, u32[]{:S(2)}) %collective-permute-start.2) | collective-permute-done | bytes 393248 | tf_op jit(solution)/shard_map/ppermute | solution.py:482
  76.1 0.0 copy-start.2
  76.1 1.6 %grads_to_owners.1.after_ref = bf16[16,192,128]{2,1,0:T(8,128)(2,1)} custom-call(s32[5]{0:T(128)S(1)} %pad_add_fusion.place_ref, bf16[8,192,128]{2,1,0:T(8,128)(2,1)S(1)} %get-tuple-element.28.mine_ref, bf16[8,192,128]{2,1,0:T(8,128)(2,1)S(1)} %collective-permute-done.2.theirs_ref), custom_call_target="tpu_custom_call" | custom-call | flops 67108864 | bytes 2097152 | tf_op jit(solution)/shard_map/grads_to_owners/pallas_call | solution.py:379
  77.6 4.4 %all-to-all-done.3 = bf16[32,16,1024]{2,1,0:T(8,128)(2,1)} async-done(((bf16[32,16,1024]{2,1,0:T(8,128)(2,1)}), bf16[32,16,1024]{2,1,0:T(8,128)(2,1)}, u32[]{:S(2)}, u32[]{:S(2)}) %all-to-all-start.3) | async-done | bytes 1048608 | tf_op jit(solution)/shard_map/all_to_all | solution.py:522
  82.0 4.9 %all-to-all-start.2 = ((bf16[16,192,128]{2,1,0:T(8,128)(2,1)}), bf16[16,192,128]{2,1,0:T(8,128)(2,1)S(1)}, u32[]{:S(2)}, u32[]{:S(2)}) async-start(bf16[16,192,128]{2,1,0:T(8,128)(2,1)} %grads_to_owners.1.after_ref), calls=%async_computation.2 | async-start | bytes 1572864 | tf_op jit(solution)/shard_map/all_to_all | solution.py:485
  87.0 1.4 %convert_reduce_fusion = f32[16,1024]{1,0:T(8,128)S(1)} fusion(bf16[32,16,1024]{2,1,0:T(8,128)(2,1)} %all-to-all-done.3), kind=kLoop, calls=%fused_computation | loop fusion | flops 1032192 | bytes 1114112 | tf_op jit(solution)/shard_map/reduce_sum | solution.py:543
  88.4 6.9 %collective-permute-start.5 = (f32[2,4,1024]{2,1,0:T(4,128)S(1)}, f32[2,4,1024]{2,1,0:T(4,128)S(1)}, u32[]{:S(2)}, u32[]{:S(2)}) collective-permute-start(f32[2,4,1024]{2,1,0:T(4,128)S(1)} %dynamic-slice_bitcast_fusion), channel_id=1, source_target_pairs={{0,128},{64,192},{128,0},{192,64},{1,129},{65,193},{129,1},{193,65... | collective-permute-start | bytes 98312 | tf_op jit(solution)/shard_map/ppermute | solution.py:550
  95.3 1.9 %collective-permute-done.5 = f32[2,4,1024]{2,1,0:T(4,128)S(1)} collective-permute-done((f32[2,4,1024]{2,1,0:T(4,128)S(1)}, f32[2,4,1024]{2,1,0:T(4,128)S(1)}, u32[]{:S(2)}, u32[]{:S(2)}) %collective-permute-start.5) | collective-permute-done | bytes 32800 | tf_op jit(solution)/shard_map/ppermute | solution.py:550
  97.3 2.8 %collective-permute-start.6 = (f32[1,4,1024]{2,1,0:T(4,128)S(1)}, f32[1,4,1024]{2,1,0:T(4,128)S(1)}, u32[]{:S(2)}, u32[]{:S(2)}) collective-permute-start(f32[1,4,1024]{2,1,0:T(4,128)S(1)} %constant_dynamic-slice_fusion), channel_id=1, source_target_pairs={{0,64},{64,0},{128,192},{192,128},{1,65},{65,1},{129,193},{193,129... | collective-permute-start | bytes 49160 | tf_op jit(solution)/shard_map/ppermute | solution.py:550
  100.1 0.0 copy-done.2
  100.1 1.1 %d_gate.1 = bf16[128,1024]{1,0:T(8,128)(2,1)} custom-call(bf16[16,144,128]{2,1,0:T(8,128)(2,1)S(1)} %all-to-all-done.1.got_ref, f32[1024,128]{1,0:T(8,128)S(1)} %copy-done.2, bf16[16,192,128]{2,1,0:T(8,128)(2,1)} %grads_to_owners.1.after_ref), custom_call_target="tpu_custom_call" | custom-call | flops 1048576 | bytes 2097152 | tf_op jit(solution)/shard_map/d_gate/pallas_call | solution.py:379
  101.2 0.0 all-to-all-done.2.got_ref
  101.2 1.0 finish.1
  102.2 0.0 collective-permute-done.6
  102.2 0.6 multiply_bitcast_fusion
  (4 shorter events, 0.1 us)
Async XLA Ops:
  0.6 11.7 %copy-start.3 = (s32[1,4]{1,0:T(1,128)S(1)}, s32[1,4]{1,0:T(1,128)}, u32[]{:S(2)}) copy-start(s32[1,4]{1,0:T(1,128)} %param.13) | copy-start | bytes 52
  4.8 22.5 %all-to-all-start = ((bf16[16,256,128]{2,1,0:T(8,128)(2,1)}), bf16[16,256,128]{2,1,0:T(8,128)(2,1)S(1)}, u32[]{:S(2)}, u32[]{:S(2)}) async-start(bf16[16,256,128]{2,1,0:T(8,128)(2,1)} %get-tuple-element.21), calls=%async_computation | async-start | bytes 2097152 | tf_op jit(solution)/shard_map/all_to_all | solution.py:485
  28.1 16.1 %copy-start.1 = (bf16[128,1024]{1,0:T(8,128)(2,1)S(1)}, bf16[128,1024]{1,0:T(8,128)(2,1)}, u32[]{:S(2)}) copy-start(bf16[128,1024]{1,0:T(8,128)(2,1)} %refs_2_.1) | copy-start | bytes 786436
  28.1 2.0 %collective-permute-start = (bf16[8,256,128]{2,1,0:T(8,128)(2,1)S(1)}, bf16[8,256,128]{2,1,0:T(8,128)(2,1)S(1)}, u32[]{:S(2)}, u32[]{:S(2)}) collective-permute-start(bf16[8,256,128]{2,1,0:T(8,128)(2,1)S(1)} %other_half.1), channel_id=1, source_target_pairs={{0,1},{1,0},{2,3},{3,2},{4,5},{5,4},{6,7},{7,6},{8,9},{9,8},{10,11... | collective-permute-start | bytes 1572872 | tf_op jit(solution)/shard_map/ppermute | solution.py:482
  35.0 1.4 %collective-permute-start.1 = (bf16[8,64,128]{2,1,0:T(8,128)(2,1)S(1)}, bf16[8,64,128]{2,1,0:T(8,128)(2,1)S(1)}, u32[]{:S(2)}, u32[]{:S(2)}) collective-permute-start(bf16[8,64,128]{2,1,0:T(8,128)(2,1)S(1)} %get-tuple-element.24), channel_id=1, source_target_pairs={{0,1},{1,0},{2,3},{3,2},{4,5},{5,4},{6,7},{7,6},{8,9},{9,8},{10,11... | collective-permute-start | bytes 393224 | tf_op jit(solution)/shard_map/ppermute | solution.py:482
  38.0 16.7 %all-to-all-start.1 = ((bf16[16,144,128]{2,1,0:T(8,128)(2,1)}), bf16[16,144,128]{2,1,0:T(8,128)(2,1)S(1)}, u32[]{:S(2)}, u32[]{:S(2)}) async-start(bf16[16,144,128]{2,1,0:T(8,128)(2,1)} %attn_to_owners.1), calls=%async_computation.1 | async-start | bytes 1179648 | tf_op jit(solution)/shard_map/all_to_all | solution.py:485
  44.1 11.6 %collective-permute-start.4 = (bf16[128,1024]{1,0:T(8,128)(2,1)S(1)}, bf16[128,1024]{1,0:T(8,128)(2,1)S(1)}, u32[]{:S(2)}, u32[]{:S(2)}) collective-permute-start(bf16[128,1024]{1,0:T(8,128)(2,1)S(1)} %copy-done.1), channel_id=1, source_target_pairs={{0,1},{1,0},{2,3},{3,2},{4,5},{5,4},{6,7},{7,6},{8,9},{9,8},{10,11... | collective-permute-start | bytes 786440 | tf_op jit(solution)/shard_map/ppermute | solution.py:482
  44.4 10.2 %copy-start = (bf16[128,1024]{1,0:T(8,128)(2,1)S(1)}, bf16[128,1024]{1,0:T(8,128)(2,1)}, u32[]{:S(2)}) copy-start(bf16[128,1024]{1,0:T(8,128)(2,1)} %u_ref.1) | copy-start | bytes 786436
  55.6 1.4 %collective-permute-start.3 = (bf16[512,128]{1,0:T(8,128)(2,1)S(1)}, bf16[512,128]{1,0:T(8,128)(2,1)S(1)}, u32[]{:S(2)}, u32[]{:S(2)}) collective-permute-start(bf16[512,128]{1,0:T(8,128)(2,1)S(1)} %get-tuple-element.35), channel_id=1, source_target_pairs={{0,1},{1,0},{2,3},{3,2},{4,5},{5,4},{6,7},{7,6},{8,9},{9,8},{10,11... | collective-permute-start | bytes 393224 | tf_op jit(solution)/shard_map/ppermute | solution.py:482
  58.5 23.5 %all-to-all-start.3 = ((bf16[32,16,1024]{2,1,0:T(8,128)(2,1)}), bf16[32,16,1024]{2,1,0:T(8,128)(2,1)}, u32[]{:S(2)}, u32[]{:S(2)}) async-start(bf16[32,16,1024]{2,1,0:T(8,128)(2,1)} %bitcast.2), calls=%async_computation.3 | async-start | bytes 2097152 | tf_op jit(solution)/shard_map/all_to_all | solution.py:522
  74.1 2.0 %collective-permute-start.2 = (bf16[8,192,128]{2,1,0:T(8,128)(2,1)S(1)}, bf16[8,192,128]{2,1,0:T(8,128)(2,1)S(1)}, u32[]{:S(2)}, u32[]{:S(2)}) collective-permute-start(bf16[8,192,128]{2,1,0:T(8,128)(2,1)S(1)} %get-tuple-element.29), channel_id=1, source_target_pairs={{0,1},{1,0},{2,3},{3,2},{4,5},{5,4},{6,7},{7,6},{8,9},{9,8},{10,11... | collective-permute-start | bytes 1179656 | tf_op jit(solution)/shard_map/ppermute | solution.py:482
  76.1 24.0 %copy-start.2 = (f32[1024,128]{1,0:T(8,128)S(1)}, f32[1024,128]{1,0:T(8,128)}, u32[]{:S(2)}) copy-start(f32[1024,128]{1,0:T(8,128)} %get-tuple-element.33.dg_ref) | copy-start | bytes 1572868
  82.0 19.2 %all-to-all-start.2 = ((bf16[16,192,128]{2,1,0:T(8,128)(2,1)}), bf16[16,192,128]{2,1,0:T(8,128)(2,1)S(1)}, u32[]{:S(2)}, u32[]{:S(2)}) async-start(bf16[16,192,128]{2,1,0:T(8,128)(2,1)} %grads_to_owners.1.after_ref), calls=%async_computation.2 | async-start | bytes 1572864 | tf_op jit(solution)/shard_map/all_to_all | solution.py:485
  88.4 8.8 %collective-permute-start.5 = (f32[2,4,1024]{2,1,0:T(4,128)S(1)}, f32[2,4,1024]{2,1,0:T(4,128)S(1)}, u32[]{:S(2)}, u32[]{:S(2)}) collective-permute-start(f32[2,4,1024]{2,1,0:T(4,128)S(1)} %dynamic-slice_bitcast_fusion), channel_id=1, source_target_pairs={{0,128},{64,192},{128,0},{192,64},{1,129},{65,193},{129,1},{193,65... | collective-permute-start | bytes 98312 | tf_op jit(solution)/shard_map/ppermute | solution.py:550
  97.3 4.9 %collective-permute-start.6 = (f32[1,4,1024]{2,1,0:T(4,128)S(1)}, f32[1,4,1024]{2,1,0:T(4,128)S(1)}, u32[]{:S(2)}, u32[]{:S(2)}) collective-permute-start(f32[1,4,1024]{2,1,0:T(4,128)S(1)} %constant_dynamic-slice_fusion), channel_id=1, source_target_pairs={{0,64},{64,0},{128,192},{192,128},{1,65},{65,1},{129,193},{193,129... | collective-permute-start | bytes 49160 | tf_op jit(solution)/shard_map/ppermute | solution.py:550

commit v8 on v7

--- a/solution.py
+++ b/solution.py
@@ -529,7 +529,6 @@
         [SMEM] + [VMEM] * 2,
         (place, mine, swap(theirs)),
     )
-    got = chips(send)
     d_gate = call(
         d_gate_kernel,
         "d_gate",
@@ -538,6 +537,8 @@
         (got_attn, d_gated_t, send),
         flops=1 << 20,
     )
+    send, d_gate = lax.optimization_barrier((send, d_gate))
+    got = chips(send)
 
     parts, _ = lax.optimization_barrier((parts, send))
     part = jnp.sum(parts.astype(F32), axis=0).reshape(4, 4, WIDTH)

time: 103 us -> 103 us (level)
    all_to_all x1, waiting for transfers between devices: 4.39 us -> 3.26 us  [on_device(): lax.all_to_all(part.reshape(32, 16, WIDTH), ('zl',) + CHIP, 0, 0, tiled=T...]
  transfers between devices with their start and end apart: 11 -> 11, of which waited for: 8 -> 9; matrix products, arithmetic and copies ran while one was open for 1% -> 1% of each run, Pallas kernels for 19% -> 19%
where the time goes in v8:
time: 103 us
  starting transfers between devices  36.7 us (36%)
  Pallas kernels  32.5 us (32%)
  waiting for transfers between devices  30.4 us (30%)
  other arithmetic  2.09 us (2%)
    pallas_call x11, Pallas kernels, call(): pl.pallas_call(kernel, out_shape=out_shape, in_specs=in_specs, out_specs=...  32.5 us
    all_to_all x3, starting transfers between devices, chips(): return lax.all_to_all(x, CHIP, 0, 0, tiled=True)  18.6 us
    all_to_all x3, waiting for transfers between devices, chips(): return lax.all_to_all(x, CHIP, 0, 0, tiled=True)  18.1 us
    ppermute x2, starting transfers between devices, on_device(): part = kept + lax.ppermute(away, 'zh', [(i, i ^ step) for i in range(4)])  9.7 us
    all_to_all x1, starting transfers between devices, on_device(): lax.all_to_all(part.reshape(32, 16, WIDTH), ('zl',) + CHIP, 0, 0, tiled=T...  7.43 us
    ppermute x5, waiting for transfers between devices, swap(): return lax.ppermute(x, 'core', SWAP)  6.14 us
    all_to_all x1, waiting for transfers between devices, on_device(): lax.all_to_all(part.reshape(32, 16, WIDTH), ('zl',) + CHIP, 0, 0, tiled=T...  3.26 us
    ppermute x2, waiting for transfers between devices, on_device(): part = kept + lax.ppermute(away, 'zh', [(i, i ^ step) for i in range(4)])  2.87 us
  transfers between devices with their start and end apart: 11, of which 9 were waited for; matrix products, arithmetic and copies ran while one was open for 1% of the time, Pallas kernels for 19%

profile of v8, /device:TPU:2, one launch (start us, length us, event | category | flops | bytes accessed | tf_op | source)
XLA Modules:
  0.0 102.6 jit_solution(15689099299223496068)
XLA Ops:
  0.6 0.0 copy-start.3
  0.6 4.2 %prepare.1 = (bf16[16,256,128]{2,1,0:T(8,128)(2,1)}, f32[1024,128]{1,0:T(8,128)}) custom-call(bf16[128,1024]{1,0:T(8,128)(2,1)} %q_in.1, bf16[128,1024]{1,0:T(8,128)(2,1)} %k_in.1, bf16[128,1024]{1,0:T(8,128)(2,1)} %v_in.1, bf16[128,1024]{1,0:T(8,128)(2,1)} %u_ref.1, bf16[128,1024]{1,0:T(8,128)(2,1)} %refs_2_.1, bf16[1024,1024]{1,0:T(8,128)(2,1)} %w_in.1), custom_call_target="tpu_custom_call" | custom-call | flops 67108864 | bytes 2097152 | tf_op jit(solution)/shard_map/prepare/pallas_call | solution.py:379
  4.8 7.5 %all-to-all-start = ((bf16[16,256,128]{2,1,0:T(8,128)(2,1)}), bf16[16,256,128]{2,1,0:T(8,128)(2,1)S(1)}, u32[]{:S(2)}, u32[]{:S(2)}) async-start(bf16[16,256,128]{2,1,0:T(8,128)(2,1)} %get-tuple-element.23), calls=%async_computation | async-start | bytes 2097152 | tf_op jit(solution)/shard_map/all_to_all | solution.py:485
  12.3 0.0 copy-done.3
  12.3 0.1 pad_add_fusion.place_ref
  12.4 15.0 %all-to-all-done.got_ref = bf16[16,256,128]{2,1,0:T(8,128)(2,1)S(1)} async-done(((bf16[16,256,128]{2,1,0:T(8,128)(2,1)}), bf16[16,256,128]{2,1,0:T(8,128)(2,1)S(1)}, u32[]{:S(2)}, u32[]{:S(2)}) %all-to-all-start) | async-done | bytes 1048608 | tf_op jit(solution)/shard_map/all_to_all | solution.py:485
  27.4 0.7 other_half.1
  28.1 0.0 copy-start.1
  28.1 0.1 collective-permute-start
  28.2 1.9 %collective-permute-done.other_ref = bf16[8,256,128]{2,1,0:T(8,128)(2,1)S(1)} collective-permute-done((bf16[8,256,128]{2,1,0:T(8,128)(2,1)S(1)}, bf16[8,256,128]{2,1,0:T(8,128)(2,1)S(1)}, u32[]{:S(2)}, u32[]{:S(2)}) %collective-permute-start) | collective-permute-done | bytes 524320 | tf_op jit(solution)/shard_map/ppermute | solution.py:482
  30.1 5.0 %attend_forward.1 = (bf16[320,2048]{1,0:T(8,128)(2,1)S(1)}, bf16[8,64,128]{2,1,0:T(8,128)(2,1)S(1)}, bf16[8,64,128]{2,1,0:T(8,128)(2,1)S(1)}, bf16[80,128]{1,0:T(8,128)(2,1)S(1)}) custom-call(s32[5]{0:T(128)S(1)} %pad_add_fusion.place_ref, bf16[16,256,128]{2,1,0:T(8,128)(2,1)S(1)} %all-to-all-done.got_ref, ...), custom_call_target="tpu_custom_call" | custom-call | flops 1073741824 | bytes 2097152 | tf_op jit(solution)/shard_map/attend_forward/pallas_call | solution.py:379
  35.0 0.2 collective-permute-start.1
  35.2 1.2 %collective-permute-done.1.theirs_ref = bf16[8,64,128]{2,1,0:T(8,128)(2,1)S(1)} collective-permute-done((bf16[8,64,128]{2,1,0:T(8,128)(2,1)S(1)}, bf16[8,64,128]{2,1,0:T(8,128)(2,1)S(1)}, u32[]{:S(2)}, u32[]{:S(2)}) %collective-permute-start.1) | collective-permute-done | bytes 131104 | tf_op jit(solution)/shard_map/ppermute | solution.py:482
  36.5 1.5 %attn_to_owners.1 = bf16[16,144,128]{2,1,0:T(8,128)(2,1)} custom-call(s32[5]{0:T(128)S(1)} %pad_add_fusion.place_ref, bf16[8,64,128]{2,1,0:T(8,128)(2,1)S(1)} %get-tuple-element.25.mine_ref, bf16[8,64,128]{2,1,0:T(8,128)(2,1)S(1)} %collective-permute-done.1.theirs_ref, bf16[80,128]{1,0:T(8,128)(2,1)S(1)} %get-tuple-element.27.stat_ref), custom_call_target="tpu_custom_call" | custom-call | flops 67108864 | bytes 2097152 | tf_op jit(solution)/shard_map/attn_to_owners/pallas_call | solution.py:379
  38.0 6.1 %all-to-all-start.1 = ((bf16[16,144,128]{2,1,0:T(8,128)(2,1)}), bf16[16,144,128]{2,1,0:T(8,128)(2,1)S(1)}, u32[]{:S(2)}, u32[]{:S(2)}) async-start(bf16[16,144,128]{2,1,0:T(8,128)(2,1)} %attn_to_owners.1), calls=%async_computation.1 | async-start | bytes 1179648 | tf_op jit(solution)/shard_map/all_to_all | solution.py:485
  44.1 0.0 copy-done.1
  44.1 0.3 collective-permute-start.4
  44.4 0.0 copy-start
  44.4 7.0 %derive.1.tile_in = bf16[80,256,256]{2,1,0:T(8,128)(2,1)} custom-call(s32[5]{0:T(128)S(1)} %pad_add_fusion.place_ref, bf16[320,2048]{1,0:T(8,128)(2,1)S(1)} %get-tuple-element.24.x_ref), custom_call_target="tpu_custom_call" | custom-call | flops 2147483648 | bytes 2097152 | tf_op jit(solution)/shard_map/derive/pallas_call | solution.py:379
  51.5 3.2 %all-to-all-done.1.got_ref = bf16[16,144,128]{2,1,0:T(8,128)(2,1)S(1)} async-done(((bf16[16,144,128]{2,1,0:T(8,128)(2,1)}), bf16[16,144,128]{2,1,0:T(8,128)(2,1)S(1)}, u32[]{:S(2)}, u32[]{:S(2)}) %all-to-all-start.1) | async-done | bytes 589856 | tf_op jit(solution)/shard_map/all_to_all | solution.py:485
  54.6 0.0 copy-done
  54.7 1.0 gated.1
  55.6 0.1 collective-permute-start.3
  55.7 0.0 collective-permute-done.4.refs_3_
  55.7 1.3 %collective-permute-done.3.refs_1_ = bf16[512,128]{1,0:T(8,128)(2,1)S(1)} collective-permute-done((bf16[512,128]{1,0:T(8,128)(2,1)S(1)}, bf16[512,128]{1,0:T(8,128)(2,1)S(1)}, u32[]{:S(2)}, u32[]{:S(2)}) %collective-permute-start.3) | collective-permute-done | bytes 131104 | tf_op jit(solution)/shard_map/ppermute | solution.py:482
  57.1 1.4 %product.1 = bf16[512,1024]{1,0:T(8,128)(2,1)} custom-call(bf16[512,128]{1,0:T(8,128)(2,1)S(1)} %get-tuple-element.38.refs_0_, bf16[512,128]{1,0:T(8,128)(2,1)S(1)} %collective-permute-done.3.refs_1_, bf16[128,1024]{1,0:T(8,128)(2,1)S(1)} %copy-done.1, bf16[128,1024]{1,0:T(8,128)(2,1)S(1)} %collective-permute-done.4.refs_3_), custom_call_target="tpu_custom_call" | custom-call | flops 67108864 | bytes 2097152 | tf_op jit(solution)/shard_map/product/pallas_call | solution.py:379
  58.5 7.4 %all-to-all-start.3 = ((bf16[32,16,1024]{2,1,0:T(8,128)(2,1)}), bf16[32,16,1024]{2,1,0:T(8,128)(2,1)}, u32[]{:S(2)}, u32[]{:S(2)}) async-start(bf16[32,16,1024]{2,1,0:T(8,128)(2,1)} %bitcast.2), calls=%async_computation.3 | async-start | bytes 2097152 | tf_op jit(solution)/shard_map/all_to_all | solution.py:522
  66.0 0.0 copy-start.2
  66.0 8.1 %attend_backward.1 = (bf16[8,192,128]{2,1,0:T(8,128)(2,1)S(1)}, bf16[8,192,128]{2,1,0:T(8,128)(2,1)S(1)}) custom-call(s32[5]{0:T(128)S(1)} %pad_add_fusion.place_ref, bf16[320,2048]{1,0:T(8,128)(2,1)S(1)} %get-tuple-element.24.x_ref, bf16[16,144,128]{2,1,0:T(8,128)(2,1)S(1)} %all-to-all-done.1.got_ref, bf16[80,256,256]{2,1,0:T(8,128)(2,1)} %derive.1.tile_in), custom_call_target="tpu_custom_call" | custom-call | flops 8589934592 | bytes 2097152 | tf_op jit(solution)/shard_map/attend_backward/pallas_call | solution.py:379
  74.1 0.3 collective-permute-start.2
  74.4 1.7 %collective-permute-done.2.theirs_ref = bf16[8,192,128]{2,1,0:T(8,128)(2,1)S(1)} collective-permute-done((bf16[8,192,128]{2,1,0:T(8,128)(2,1)S(1)}, bf16[8,192,128]{2,1,0:T(8,128)(2,1)S(1)}, u32[]{:S(2)}, u32[]{:S(2)}) %collective-permute-start.2) | collective-permute-done | bytes 393248 | tf_op jit(solution)/shard_map/ppermute | solution.py:482
  76.1 1.6 %grads_to_owners.1.after_ref = bf16[16,192,128]{2,1,0:T(8,128)(2,1)} custom-call(s32[5]{0:T(128)S(1)} %pad_add_fusion.place_ref, bf16[8,192,128]{2,1,0:T(8,128)(2,1)S(1)} %get-tuple-element.30.mine_ref, bf16[8,192,128]{2,1,0:T(8,128)(2,1)S(1)} %collective-permute-done.2.theirs_ref), custom_call_target="tpu_custom_call" | custom-call | flops 67108864 | bytes 2097152 | tf_op jit(solution)/shard_map/grads_to_owners/pallas_call | solution.py:379
  77.7 0.0 copy-done.2
  77.7 1.1 %d_gate.1 = bf16[128,1024]{1,0:T(8,128)(2,1)} custom-call(bf16[16,144,128]{2,1,0:T(8,128)(2,1)S(1)} %all-to-all-done.1.got_ref, f32[1024,128]{1,0:T(8,128)S(1)} %copy-done.2, bf16[16,192,128]{2,1,0:T(8,128)(2,1)} %grads_to_owners.1.after_ref), custom_call_target="tpu_custom_call" | custom-call | flops 1048576 | bytes 2097152 | tf_op jit(solution)/shard_map/d_gate/pallas_call | solution.py:379
  78.8 3.3 %all-to-all-done.3 = bf16[32,16,1024]{2,1,0:T(8,128)(2,1)} async-done(((bf16[32,16,1024]{2,1,0:T(8,128)(2,1)}), bf16[32,16,1024]{2,1,0:T(8,128)(2,1)}, u32[]{:S(2)}, u32[]{:S(2)}) %all-to-all-start.3) | async-done | bytes 1048608 | tf_op jit(solution)/shard_map/all_to_all | solution.py:522
  82.0 4.9 %all-to-all-start.2 = ((bf16[16,192,128]{2,1,0:T(8,128)(2,1)}), bf16[16,192,128]{2,1,0:T(8,128)(2,1)S(1)}, u32[]{:S(2)}, u32[]{:S(2)}) async-start(bf16[16,192,128]{2,1,0:T(8,128)(2,1)} %grads_to_owners.1.after_ref), calls=%async_computation.2 | async-start | bytes 1572864 | tf_op jit(solution)/shard_map/all_to_all | solution.py:485
  87.0 1.4 %convert_reduce_fusion = f32[16,1024]{1,0:T(8,128)S(1)} fusion(bf16[32,16,1024]{2,1,0:T(8,128)(2,1)} %all-to-all-done.3), kind=kLoop, calls=%fused_computation | loop fusion | flops 1032192 | bytes 1114112 | tf_op jit(solution)/shard_map/reduce_sum | solution.py:544
  88.4 6.9 %collective-permute-start.5 = (f32[2,4,1024]{2,1,0:T(4,128)S(1)}, f32[2,4,1024]{2,1,0:T(4,128)S(1)}, u32[]{:S(2)}, u32[]{:S(2)}) collective-permute-start(f32[2,4,1024]{2,1,0:T(4,128)S(1)} %dynamic-slice_bitcast_fusion), channel_id=1, source_target_pairs={{0,128},{64,192},{128,0},{192,64},{1,129},{65,193},{129,1},{193,65... | collective-permute-start | bytes 98312 | tf_op jit(solution)/shard_map/ppermute | solution.py:551
  95.3 1.9 %collective-permute-done.5 = f32[2,4,1024]{2,1,0:T(4,128)S(1)} collective-permute-done((f32[2,4,1024]{2,1,0:T(4,128)S(1)}, f32[2,4,1024]{2,1,0:T(4,128)S(1)}, u32[]{:S(2)}, u32[]{:S(2)}) %collective-permute-start.5) | collective-permute-done | bytes 32800 | tf_op jit(solution)/shard_map/ppermute | solution.py:551
  97.3 2.8 %collective-permute-start.6 = (f32[1,4,1024]{2,1,0:T(4,128)S(1)}, f32[1,4,1024]{2,1,0:T(4,128)S(1)}, u32[]{:S(2)}, u32[]{:S(2)}) collective-permute-start(f32[1,4,1024]{2,1,0:T(4,128)S(1)} %constant_dynamic-slice_fusion), channel_id=1, source_target_pairs={{0,64},{64,0},{128,192},{192,128},{1,65},{65,1},{129,193},{193,129... | collective-permute-start | bytes 49160 | tf_op jit(solution)/shard_map/ppermute | solution.py:551
  100.1 0.0 all-to-all-done.2.got_ref
  100.1 1.0 finish.1
  101.1 0.9 collective-permute-done.6
  102.0 0.6 multiply_bitcast_fusion
  (4 shorter events, 0.1 us)
Async XLA Ops:
  0.6 11.7 %copy-start.3 = (s32[1,4]{1,0:T(1,128)S(1)}, s32[1,4]{1,0:T(1,128)}, u32[]{:S(2)}) copy-start(s32[1,4]{1,0:T(1,128)} %param.13) | copy-start | bytes 52
  4.8 22.5 %all-to-all-start = ((bf16[16,256,128]{2,1,0:T(8,128)(2,1)}), bf16[16,256,128]{2,1,0:T(8,128)(2,1)S(1)}, u32[]{:S(2)}, u32[]{:S(2)}) async-start(bf16[16,256,128]{2,1,0:T(8,128)(2,1)} %get-tuple-element.23), calls=%async_computation | async-start | bytes 2097152 | tf_op jit(solution)/shard_map/all_to_all | solution.py:485
  28.1 16.1 %copy-start.1 = (bf16[128,1024]{1,0:T(8,128)(2,1)S(1)}, bf16[128,1024]{1,0:T(8,128)(2,1)}, u32[]{:S(2)}) copy-start(bf16[128,1024]{1,0:T(8,128)(2,1)} %refs_2_.1) | copy-start | bytes 786436
  28.1 2.0 %collective-permute-start = (bf16[8,256,128]{2,1,0:T(8,128)(2,1)S(1)}, bf16[8,256,128]{2,1,0:T(8,128)(2,1)S(1)}, u32[]{:S(2)}, u32[]{:S(2)}) collective-permute-start(bf16[8,256,128]{2,1,0:T(8,128)(2,1)S(1)} %other_half.1), channel_id=1, source_target_pairs={{0,1},{1,0},{2,3},{3,2},{4,5},{5,4},{6,7},{7,6},{8,9},{9,8},{10,11... | collective-permute-start | bytes 1572872 | tf_op jit(solution)/shard_map/ppermute | solution.py:482
  35.0 1.4 %collective-permute-start.1 = (bf16[8,64,128]{2,1,0:T(8,128)(2,1)S(1)}, bf16[8,64,128]{2,1,0:T(8,128)(2,1)S(1)}, u32[]{:S(2)}, u32[]{:S(2)}) collective-permute-start(bf16[8,64,128]{2,1,0:T(8,128)(2,1)S(1)} %get-tuple-element.26), channel_id=1, source_target_pairs={{0,1},{1,0},{2,3},{3,2},{4,5},{5,4},{6,7},{7,6},{8,9},{9,8},{10,11... | collective-permute-start | bytes 393224 | tf_op jit(solution)/shard_map/ppermute | solution.py:482
  38.0 16.7 %all-to-all-start.1 = ((bf16[16,144,128]{2,1,0:T(8,128)(2,1)}), bf16[16,144,128]{2,1,0:T(8,128)(2,1)S(1)}, u32[]{:S(2)}, u32[]{:S(2)}) async-start(bf16[16,144,128]{2,1,0:T(8,128)(2,1)} %attn_to_owners.1), calls=%async_computation.1 | async-start | bytes 1179648 | tf_op jit(solution)/shard_map/all_to_all | solution.py:485
  44.1 11.6 %collective-permute-start.4 = (bf16[128,1024]{1,0:T(8,128)(2,1)S(1)}, bf16[128,1024]{1,0:T(8,128)(2,1)S(1)}, u32[]{:S(2)}, u32[]{:S(2)}) collective-permute-start(bf16[128,1024]{1,0:T(8,128)(2,1)S(1)} %copy-done.1), channel_id=1, source_target_pairs={{0,1},{1,0},{2,3},{3,2},{4,5},{5,4},{6,7},{7,6},{8,9},{9,8},{10,11... | collective-permute-start | bytes 786440 | tf_op jit(solution)/shard_map/ppermute | solution.py:482
  44.4 10.2 %copy-start = (bf16[128,1024]{1,0:T(8,128)(2,1)S(1)}, bf16[128,1024]{1,0:T(8,128)(2,1)}, u32[]{:S(2)}) copy-start(bf16[128,1024]{1,0:T(8,128)(2,1)} %u_ref.1) | copy-start | bytes 786436
  55.6 1.4 %collective-permute-start.3 = (bf16[512,128]{1,0:T(8,128)(2,1)S(1)}, bf16[512,128]{1,0:T(8,128)(2,1)S(1)}, u32[]{:S(2)}, u32[]{:S(2)}) collective-permute-start(bf16[512,128]{1,0:T(8,128)(2,1)S(1)} %get-tuple-element.39), channel_id=1, source_target_pairs={{0,1},{1,0},{2,3},{3,2},{4,5},{5,4},{6,7},{7,6},{8,9},{9,8},{10,11... | collective-permute-start | bytes 393224 | tf_op jit(solution)/shard_map/ppermute | solution.py:482
  58.5 23.5 %all-to-all-start.3 = ((bf16[32,16,1024]{2,1,0:T(8,128)(2,1)}), bf16[32,16,1024]{2,1,0:T(8,128)(2,1)}, u32[]{:S(2)}, u32[]{:S(2)}) async-start(bf16[32,16,1024]{2,1,0:T(8,128)(2,1)} %bitcast.2), calls=%async_computation.3 | async-start | bytes 2097152 | tf_op jit(solution)/shard_map/all_to_all | solution.py:522
  66.0 11.7 %copy-start.2 = (f32[1024,128]{1,0:T(8,128)S(1)}, f32[1024,128]{1,0:T(8,128)}, u32[]{:S(2)}) copy-start(f32[1024,128]{1,0:T(8,128)} %get-tuple-element.32.dg_ref) | copy-start | bytes 1572868
  74.1 2.0 %collective-permute-start.2 = (bf16[8,192,128]{2,1,0:T(8,128)(2,1)S(1)}, bf16[8,192,128]{2,1,0:T(8,128)(2,1)S(1)}, u32[]{:S(2)}, u32[]{:S(2)}) collective-permute-start(bf16[8,192,128]{2,1,0:T(8,128)(2,1)S(1)} %get-tuple-element.31), channel_id=1, source_target_pairs={{0,1},{1,0},{2,3},{3,2},{4,5},{5,4},{6,7},{7,6},{8,9},{9,8},{10,11... | collective-permute-start | bytes 1179656 | tf_op jit(solution)/shard_map/ppermute | solution.py:482
  82.0 18.0 %all-to-all-start.2 = ((bf16[16,192,128]{2,1,0:T(8,128)(2,1)}), bf16[16,192,128]{2,1,0:T(8,128)(2,1)S(1)}, u32[]{:S(2)}, u32[]{:S(2)}) async-start(bf16[16,192,128]{2,1,0:T(8,128)(2,1)} %grads_to_owners.1.after_ref), calls=%async_computation.2 | async-start | bytes 1572864 | tf_op jit(solution)/shard_map/all_to_all | solution.py:485
  88.4 8.9 %collective-permute-start.5 = (f32[2,4,1024]{2,1,0:T(4,128)S(1)}, f32[2,4,1024]{2,1,0:T(4,128)S(1)}, u32[]{:S(2)}, u32[]{:S(2)}) collective-permute-start(f32[2,4,1024]{2,1,0:T(4,128)S(1)} %dynamic-slice_bitcast_fusion), channel_id=1, source_target_pairs={{0,128},{64,192},{128,0},{192,64},{1,129},{65,193},{129,1},{193,65... | collective-permute-start | bytes 98312 | tf_op jit(solution)/shard_map/ppermute | solution.py:551
  97.3 4.7 %collective-permute-start.6 = (f32[1,4,1024]{2,1,0:T(4,128)S(1)}, f32[1,4,1024]{2,1,0:T(4,128)S(1)}, u32[]{:S(2)}, u32[]{:S(2)}) collective-permute-start(f32[1,4,1024]{2,1,0:T(4,128)S(1)} %constant_dynamic-slice_fusion), channel_id=1, source_target_pairs={{0,64},{64,0},{128,192},{192,128},{1,65},{65,1},{129,193},{193,129... | collective-permute-start | bytes 49160 | tf_op jit(solution)/shard_map/ppermute | solution.py:551
